TPU v7x, 32 devices: a whole 2x2x4 slice. The times are simulated.
32 devices in a mesh: lat: 8 (over z, x), batch: 4 (over y, core).
Axes of the slice: x: 2, y: 2, z: 4, core: 2. Of those that a mesh axis runs over, the one named last changes fastest.
Arguments:
- analysis: bfloat16 [8, 12, 96, 2, 12, 128], P('batch', None, 'lat'), may hold values from -6 to 6
- target: float32 [8, 12, 96, 2, 12, 128], P('batch', None, 'lat'), may hold values from -6 to 6
- lead_step: int32 [8], P('batch'), may hold values from 1 to 20
- loss_mask: int32 [8, 12, 96, 2, 12], P('batch', None, 'lat'), may hold values from 0 to 1, as said below
- embed_w: float32 [128, 192], replicated, may hold values from -0.5 to 0.5
- lead_table: float32 [20, 192], replicated, may hold values from -3 to 3
- qkv_w: float32 [2, 192, 576], replicated, may hold values from -0.4375 to 0.4375
- proj_w: float32 [2, 192, 192], replicated, may hold values from -1.5 to 1.5
- up_w: float32 [2, 192, 768], replicated, may hold values from -0.4375 to 0.4375
- down_w: float32 [2, 768, 192], replicated, may hold values from -0.4375 to 0.4375
- decode_w: float32 [192, 128], replicated, may hold values from -0.4375 to 0.4375
- norm_params: float32 [2, 5, 192], replicated
- loss_scale: float32 [128], replicated, may hold values from -1 to -0.3
- embed_mom: float32 [128, 192], replicated, may hold values from -5.9604645e-07 to 5.9604645e-07
- lead_mom: float32 [20, 192], replicated, may hold values from -5.9604645e-07 to 5.9604645e-07
- qkv_mom: float32 [2, 192, 576], replicated, may hold values from -5.9604645e-07 to 5.9604645e-07
- proj_mom: float32 [2, 192, 192], replicated, may hold values from -5.9604645e-07 to 5.9604645e-07
- up_mom: float32 [2, 192, 768], replicated, may hold values from -5.9604645e-07 to 5.9604645e-07
- down_mom: float32 [2, 768, 192], replicated, may hold values from -5.9604645e-07 to 5.9604645e-07
- decode_mom: float32 [192, 128], replicated, may hold values from -5.9604645e-07 to 5.9604645e-07
- norm_mom: float32 [2, 5, 192], replicated, may hold values from -5.9604645e-07 to 5.9604645e-07
- scale_mom: float32 [128], replicated, may hold values from -0.00030517578 to 0.00030517578
- embed_sec: float32 [128, 192], replicated, may hold values from 8.830318e-16 to 3.5321272e-15
- lead_sec: float32 [20, 192], replicated, may hold values from 8.830318e-16 to 3.5321272e-15
- qkv_sec: float32 [2, 192, 576], replicated, may hold values from 8.830318e-16 to 3.5321272e-15
- proj_sec: float32 [2, 192, 192], replicated, may hold values from 8.830318e-16 to 3.5321272e-15
- up_sec: float32 [2, 192, 768], replicated, may hold values from 8.830318e-16 to 3.5321272e-15
- down_sec: float32 [2, 768, 192], replicated, may hold values from 8.830318e-16 to 3.5321272e-15
- decode_sec: float32 [192, 128], replicated, may hold values from 8.830318e-16 to 3.5321272e-15
- norm_sec: float32 [2, 5, 192], replicated, may hold values from 8.830318e-16 to 3.5321272e-15
- scale_sec: float32 [128], replicated, may hold values from 1.953125e-10 to 7.8125e-10
Outputs:
- embed_new: float32 [128, 192], replicated
- lead_new: float32 [20, 192], replicated
- qkv_new: float32 [2, 192, 576], replicated
- proj_new: float32 [2, 192, 192], replicated
- up_new: float32 [2, 192, 768], replicated
- down_new: float32 [2, 768, 192], replicated
- decode_new: float32 [192, 128], replicated
- norm_new: float32 [2, 5, 192], replicated
- scale_new: float32 [128], replicated
- embed_mom_new: float32 [128, 192], replicated
- lead_mom_new: float32 [20, 192], replicated
- qkv_mom_new: float32 [2, 192, 576], replicated
- proj_mom_new: float32 [2, 192, 192], replicated
- up_mom_new: float32 [2, 192, 768], replicated
- down_mom_new: float32 [2, 768, 192], replicated
- decode_mom_new: float32 [192, 128], replicated
- norm_mom_new: float32 [2, 5, 192], replicated
- scale_mom_new: float32 [128], replicated
- embed_sec_new: float32 [128, 192], replicated
- lead_sec_new: float32 [20, 192], replicated
- qkv_sec_new: float32 [2, 192, 576], replicated
- proj_sec_new: float32 [2, 192, 192], replicated
- up_sec_new: float32 [2, 192, 768], replicated
- down_sec_new: float32 [2, 768, 192], replicated
- decode_sec_new: float32 [192, 128], replicated
- norm_sec_new: float32 [2, 5, 192], replicated
- scale_sec_new: float32 [128], replicated
- loss_sum: float32 [], replicated
- loss_count: float32 [], replicated
- grad_norm: float32 [], replicated
Inputs may be any that keep to these rules, and one draw needn't show every extreme that they name: `loss_mask`: 1 where a cell counts; the first longitude column always counts.
All inputs are finite; a program needn't handle non-finite values.
Results may differ from a plain program's by a relative error of at most 0.0017.
The roundings to bfloat16 on the way count: a program that leaves them out, or rounds other values in their place, can miss the bound.
Values may be sent and summed in bfloat16 or wider, within the bound.
A program may use at most 640 MiB of HBM per device.

v0:
```python
from functools import partial

import jax
import jax.numpy as jnp
from jax import lax
from jax.sharding import PartitionSpec as P

HEADS = 6
LEADS = 20
STEP = 10


beta_one = 0.9
beta_two = 0.999
adam_eps = 1e-08
clip_max = 0.005
rate_table = (0.2, 1.0, 0.2, 0.2, 0.2, 0.2, 0.2, 1.0, 1.0)
decay_table = (0.1, 0.1, 0.1, 0.1, 0.1, 0.1, 0.1, 0.0, 0.0)


def extended_2(block, sides, width):
    for axis, dim in sides:
        count = lax.axis_size(axis)
        forward = [(i, i + 1) for i in range(count - 1)]
        backward = [(target, source) for source, target in forward]
        low = lax.ppermute(
            lax.slice_in_dim(block, block.shape[dim] - width, None, axis=dim), axis, forward
        )
        high = lax.ppermute(lax.slice_in_dim(block, 0, width, axis=dim), axis, backward)
        block = jnp.concatenate([low, block, high], axis=dim)
    return block


def layer_norm(field, gain, bias):
    center = field - jnp.mean(field, axis=-1, keepdims=True)
    spread = jnp.mean(center * center, axis=-1, keepdims=True)
    return center * lax.rsqrt(spread + 1e-05) * gain + bias


def to_windows(field):
    samples, blocks, row_count = (field.shape[0], field.shape[1], field.shape[2])
    return field.reshape(samples * blocks * (row_count // 6), -1, field.shape[-1])


def key_valid(shape_ext, start, total_rows):
    samples, blocks, ext_rows, levels, twelve = shape_ext
    global_row = start + jnp.arange(ext_rows, dtype=jnp.int32)
    row_ok = ((global_row >= 0) & (global_row < total_rows)).astype(jnp.float32)
    row_grid = jnp.broadcast_to(
        row_ok[None, None, :, None, None, None], (samples, blocks, ext_rows, levels, twelve, 1)
    )
    return to_windows(row_grid)[..., 0] > 0.5


def scores_of(packed, validity):
    count_w, width, _ = packed.shape
    parts = packed.reshape(count_w, width, 3, HEADS, -1)
    query_rows, key_rows, value_rows = (parts[:, :, 0], parts[:, :, 1], parts[:, :, 2])
    score_scale = query_rows.shape[-1] ** (-0.5)
    scores = (
        jnp.einsum("wqhd,wkhd->whqk", query_rows, key_rows, preferred_element_type=jnp.float32)
        * score_scale
    )
    scores = jnp.where(validity[:, None, None, :], scores, -1e30)
    return (scores, query_rows, key_rows, value_rows, score_scale)


def forward_block(hidden, w_qkv, w_proj, w_up, w_down, gains, shifted):
    samples, blocks, row_count, levels, twelve, channels = hidden.shape
    normed = layer_norm(hidden, gains[0, 0], gains[1, 0]).astype(jnp.bfloat16)
    if shifted:
        extended = extended_2(normed, (("lat", 2),), 3)
        start = lax.axis_index("lat") * row_count - 3
    else:
        extended = normed
        start = 0
    ext_rows = extended.shape[2]
    validity = key_valid(
        (samples, blocks, ext_rows, levels, twelve), start, row_count * lax.axis_size("lat")
    )
    windows = to_windows(extended)
    count_w, width = (windows.shape[0], windows.shape[1])
    packed = jnp.dot(windows.reshape(-1, channels), w_qkv, preferred_element_type=jnp.float32)
    packed = packed.astype(jnp.bfloat16).reshape(count_w, width, -1)
    scores, query_rows, key_rows, value_rows, score_scale = scores_of(packed, validity)
    highest = jnp.max(scores, axis=-1, keepdims=True)
    expo = jnp.exp(scores - highest)
    totals = jnp.sum(expo, axis=-1, keepdims=True)
    log_total = highest + jnp.log(totals)
    probability = (expo / totals).astype(jnp.bfloat16)
    mixture = jnp.einsum(
        "whqk,wkhd->wqhd", probability, value_rows, preferred_element_type=jnp.float32
    )
    mixture = mixture.astype(jnp.bfloat16).reshape(-1, channels)
    output = jnp.dot(mixture, w_proj, preferred_element_type=jnp.float32)
    output = output.reshape(samples, blocks, ext_rows, levels, twelve, channels)
    if shifted:
        output = output[:, :, 3 : 3 + row_count]
    hidden_two = hidden + output
    normed_two = (
        layer_norm(hidden_two, gains[0, 1], gains[1, 1]).astype(jnp.bfloat16).reshape(-1, channels)
    )
    inner_pre = jnp.dot(normed_two, w_up, preferred_element_type=jnp.float32)
    active = jax.nn.gelu(inner_pre).astype(jnp.bfloat16)
    down_out = jnp.dot(active, w_down, preferred_element_type=jnp.float32).reshape(hidden.shape)
    stored = (
        hidden,
        windows,
        packed,
        log_total,
        mixture,
        hidden_two,
        normed_two,
        inner_pre,
        validity,
    )
    return (hidden_two + down_out, stored)


def backward_block(gradient, stored, w_qkv, w_proj, w_up, w_down, gains, shifted):
    hidden, windows, packed, log_total, mixture, hidden_two, normed_two, inner_pre, validity = (
        stored
    )
    samples, blocks, row_count, levels, twelve, channels = hidden.shape
    grad_low = gradient.reshape(-1, channels).astype(jnp.bfloat16)
    active, gelu_pull = jax.vjp(jax.nn.gelu, inner_pre)
    g_down = jnp.dot(active.astype(jnp.bfloat16).T, grad_low, preferred_element_type=jnp.float32)
    d_active = jnp.dot(grad_low, w_down.T, preferred_element_type=jnp.float32)
    d_inner = gelu_pull(d_active)[0].astype(jnp.bfloat16)
    g_up = jnp.dot(normed_two.T, d_inner, preferred_element_type=jnp.float32)
    d_normed_two = jnp.dot(d_inner, w_up.T, preferred_element_type=jnp.float32).reshape(
        hidden.shape
    )
    _, norm_pull = jax.vjp(layer_norm, hidden_two, gains[0, 1], gains[1, 1])
    d_hidden_two, g_gain_two, g_bias_two = norm_pull(d_normed_two)
    d_hidden_two = d_hidden_two + gradient
    d_output = d_hidden_two
    if shifted:
        d_output = jnp.pad(d_hidden_two, ((0, 0), (0, 0), (3, 3), (0, 0), (0, 0), (0, 0)))
    ext_rows = d_output.shape[2]
    d_windows = to_windows(d_output).astype(jnp.bfloat16)
    count_w, width = (d_windows.shape[0], d_windows.shape[1])
    d_windows = d_windows.reshape(-1, channels)
    g_proj = jnp.dot(mixture.T, d_windows, preferred_element_type=jnp.float32)
    d_mixture = jnp.dot(d_windows, w_proj.T, preferred_element_type=jnp.float32).astype(
        jnp.bfloat16
    )
    d_mixture = d_mixture.reshape(count_w, width, HEADS, -1)
    scores, query_rows, key_rows, value_rows, score_scale = scores_of(packed, validity)
    probability = jnp.exp(scores - log_total)
    d_values = jnp.einsum(
        "whqk,wqhd->wkhd",
        probability.astype(jnp.bfloat16),
        d_mixture,
        preferred_element_type=jnp.float32,
    )
    d_probability = jnp.einsum(
        "wqhd,wkhd->whqk", d_mixture, value_rows, preferred_element_type=jnp.float32
    )
    row_terms = jnp.sum(d_probability * probability, axis=-1, keepdims=True)
    d_scores = (probability * (d_probability - row_terms)).astype(jnp.bfloat16)
    d_query = (
        jnp.einsum("whqk,wkhd->wqhd", d_scores, key_rows, preferred_element_type=jnp.float32)
        * score_scale
    )
    d_keys = (
        jnp.einsum("whqk,wqhd->wkhd", d_scores, query_rows, preferred_element_type=jnp.float32)
        * score_scale
    )
    d_packed = (
        jnp.stack([d_query, d_keys, d_values], axis=2)
        .reshape(count_w * width, -1)
        .astype(jnp.bfloat16)
    )
    g_qkv = jnp.dot(windows.reshape(-1, channels).T, d_packed, preferred_element_type=jnp.float32)
    d_normed = jnp.dot(d_packed, w_qkv.T, preferred_element_type=jnp.float32)
    d_normed = d_normed.reshape(samples, blocks, ext_rows, levels, twelve, channels)
    if shifted:
        edge_rows = jnp.concatenate([d_normed[:, :, :3], d_normed[:, :, -3:]], axis=2)
        returned = extended_2(edge_rows.astype(jnp.bfloat16), (("lat", 2),), 3).astype(
            edge_rows.dtype
        )
        d_normed = d_normed[:, :, 3 : 3 + row_count]
        d_normed = (
            d_normed.at[:, :, :3].add(returned[:, :, :3]).at[:, :, -3:].add(returned[:, :, -3:])
        )
    _, norm_pull = jax.vjp(layer_norm, hidden, gains[0, 0], gains[1, 0])
    d_hidden, g_gain_one, g_bias_one = norm_pull(d_normed)
    g_norm = jnp.stack([jnp.stack([g_gain_one, g_gain_two]), jnp.stack([g_bias_one, g_bias_two])])
    return (d_hidden + d_hidden_two, (g_qkv, g_proj, g_up, g_down, g_norm))


def cell_loss(predicted, scale_log, target, weight_mask):
    error = predicted - target
    terms = jnp.sqrt(error * error + 1.0) * jnp.exp(-scale_log) + scale_log
    return jnp.sum(terms * weight_mask[..., None])


def apply_update(weights, gradients, firsts, seconds, cell_count):
    scaled = [member / cell_count for member in gradients]
    grad_norm = jnp.sqrt(sum((jnp.sum(member * member) for member in scaled)))
    factor = jnp.minimum(1.0, clip_max / grad_norm)
    news, moments, squares = ([], [], [])
    for weight, member, first, second, rate, shrink in zip(
        weights, scaled, firsts, seconds, rate_table, decay_table
    ):
        clipped = member * factor
        first = beta_one * first + (1.0 - beta_one) * clipped
        second = beta_two * second + (1.0 - beta_two) * clipped * clipped
        first_hat = first / (1.0 - beta_one**STEP)
        second_hat = second / (1.0 - beta_two**STEP)
        news.append(
            weight - rate * (first_hat / (jnp.sqrt(second_hat) + adam_eps) + shrink * weight)
        )
        moments.append(first)
        squares.append(second)
    return (news, moments, squares, grad_norm)


def on_device(
    analysis,
    target,
    lead_step,
    loss_mask,
    embed_w,
    lead_table,
    qkv_w,
    proj_w,
    up_w,
    down_w,
    decode_w,
    norm_params,
    loss_scale,
    embed_mom,
    lead_mom,
    qkv_mom,
    proj_mom,
    up_mom,
    down_mom,
    decode_mom,
    norm_mom,
    scale_mom,
    embed_sec,
    lead_sec,
    qkv_sec,
    proj_sec,
    up_sec,
    down_sec,
    decode_sec,
    norm_sec,
    scale_sec,
):
    inputs = analysis.shape[-1]
    samples = analysis.shape[0]
    channels = embed_w.shape[1]
    embed_low = embed_w.astype(jnp.bfloat16)
    decode_low = decode_w.astype(jnp.bfloat16)
    qkv_low = qkv_w.astype(jnp.bfloat16)
    proj_low = proj_w.astype(jnp.bfloat16)
    up_low = up_w.astype(jnp.bfloat16)
    down_low = down_w.astype(jnp.bfloat16)
    token_rows = analysis.reshape(-1, inputs)
    hidden = jnp.dot(token_rows, embed_low, preferred_element_type=jnp.float32)
    hidden = hidden.reshape(analysis.shape[:-1] + (channels,))
    lead_hot = (jnp.arange(LEADS, dtype=jnp.int32)[None, :] == lead_step[:, None] - 1).astype(
        jnp.float32
    )
    lead_rows = jnp.dot(lead_hot, lead_table, precision=lax.Precision.HIGHEST)
    hidden = hidden + lead_rows[:, None, None, None, None, :]
    saved = []
    for depth_index in range(2):
        hidden, stored = forward_block(
            hidden,
            qkv_low[depth_index],
            proj_low[depth_index],
            up_low[depth_index],
            down_low[depth_index],
            norm_params[:, 2 * depth_index : 2 * depth_index + 2],
            depth_index == 1,
        )
        saved.append(stored)
    normed, final_pull = jax.vjp(layer_norm, hidden, norm_params[0, 4], norm_params[1, 4])
    normed_low = normed.astype(jnp.bfloat16).reshape(-1, channels)
    predicted = jnp.dot(normed_low, decode_low, preferred_element_type=jnp.float32).reshape(
        target.shape
    )
    weight_mask = loss_mask.astype(jnp.float32)
    loss_part, loss_pull = jax.vjp(
        partial(cell_loss, target=target, weight_mask=weight_mask), predicted, loss_scale
    )
    count_part = jnp.sum(weight_mask) * inputs
    d_predicted, g_scale = loss_pull(jnp.ones((), jnp.float32))
    d_predicted = d_predicted.reshape(-1, inputs).astype(jnp.bfloat16)
    g_decode = jnp.dot(normed_low.T, d_predicted, preferred_element_type=jnp.float32)
    d_normed = jnp.dot(d_predicted, decode_low.T, preferred_element_type=jnp.float32).reshape(
        hidden.shape
    )
    d_hidden, g_gain_last, g_bias_last = final_pull(d_normed)
    g_final = jnp.stack([g_gain_last, g_bias_last])[:, None, :]
    layer_grads = [None, None]
    for depth_index in (1, 0):
        d_hidden, gradients = backward_block(
            d_hidden,
            saved[depth_index],
            qkv_low[depth_index],
            proj_low[depth_index],
            up_low[depth_index],
            down_low[depth_index],
            norm_params[:, 2 * depth_index : 2 * depth_index + 2],
            depth_index == 1,
        )
        layer_grads[depth_index] = gradients
    g_embed = jnp.dot(
        token_rows.T,
        d_hidden.reshape(-1, channels).astype(jnp.bfloat16),
        preferred_element_type=jnp.float32,
    )
    per_sample = jnp.sum(d_hidden.reshape(samples, -1, channels), axis=1)
    g_lead = jnp.dot(lead_hot.T, per_sample, precision=lax.Precision.HIGHEST)
    stacked = [
        jnp.stack([layer_grads[0][position], layer_grads[1][position]]) for position in range(5)
    ]
    g_norm_all = jnp.concatenate(
        [stacked[4].transpose(1, 0, 2, 3).reshape(2, 4, channels), g_final], axis=1
    )
    g_qkv_all, g_proj_all, g_up_all, g_down_all = (stacked[0], stacked[1], stacked[2], stacked[3])
    (
        g_embed,
        g_lead,
        g_qkv_all,
        g_proj_all,
        g_up_all,
        g_down_all,
        g_decode,
        g_norm_all,
        g_scale,
        loss_sum,
        cell_count,
    ) = lax.psum(
        (
            g_embed,
            g_lead,
            g_qkv_all,
            g_proj_all,
            g_up_all,
            g_down_all,
            g_decode,
            g_norm_all,
            g_scale,
            loss_part,
            count_part,
        ),
        ("lat", "batch"),
    )
    weights = (embed_w, lead_table, qkv_w, proj_w, up_w, down_w, decode_w, norm_params, loss_scale)
    firsts = (
        embed_mom,
        lead_mom,
        qkv_mom,
        proj_mom,
        up_mom,
        down_mom,
        decode_mom,
        norm_mom,
        scale_mom,
    )
    seconds = (
        embed_sec,
        lead_sec,
        qkv_sec,
        proj_sec,
        up_sec,
        down_sec,
        decode_sec,
        norm_sec,
        scale_sec,
    )
    gradients = (
        g_embed,
        g_lead,
        g_qkv_all,
        g_proj_all,
        g_up_all,
        g_down_all,
        g_decode,
        g_norm_all,
        g_scale,
    )
    news, moments, squares, grad_norm = apply_update(
        weights, gradients, firsts, seconds, cell_count
    )
    return (
        news[0],
        news[1],
        news[2],
        news[3],
        news[4],
        news[5],
        news[6],
        news[7],
        news[8],
        moments[0],
        moments[1],
        moments[2],
        moments[3],
        moments[4],
        moments[5],
        moments[6],
        moments[7],
        moments[8],
        squares[0],
        squares[1],
        squares[2],
        squares[3],
        squares[4],
        squares[5],
        squares[6],
        squares[7],
        squares[8],
        loss_sum,
        cell_count,
        grad_norm,
    )


def solution(mesh):
    placed = (
        P("batch", None, "lat", None, None, None),
        P("batch", None, "lat", None, None, None),
        P("batch"),
        P("batch", None, "lat", None, None),
        P(),
        P(),
        P(),
        P(),
        P(),
        P(),
        P(),
        P(),
        P(),
        P(),
        P(),
        P(),
        P(),
        P(),
        P(),
        P(),
        P(),
        P(),
        P(),
        P(),
        P(),
        P(),
        P(),
        P(),
        P(),
        P(),
        P(),
    )
    return jax.shard_map(
        on_device,
        mesh=mesh,
        in_specs=placed,
        out_specs=(
            P(),
            P(),
            P(),
            P(),
            P(),
            P(),
            P(),
            P(),
            P(),
            P(),
            P(),
            P(),
            P(),
            P(),
            P(),
            P(),
            P(),
            P(),
            P(),
            P(),
            P(),
            P(),
            P(),
            P(),
            P(),
            P(),
            P(),
            P(),
            P(),
            P(),
        ),
        check_vma=False,
    )
```

profile of v0, /device:TPU:0, one launch (start us, length us, event | category | flops | bytes accessed | tf_op | source)
XLA Modules:
  0.0 1825.9 jit_solution(2646327471414229739)
XLA Ops:
  43.3 25.5 %reshape_reshape.17 = bf16[48,144,3,6,32]{1,0,4,3,2:T(8,128)(2,1)} reshape(bf16[6912,576]{0,1:T(8,128)(2,1)} %convolution_convert_fusion.2) | data formatting | bytes 15925248 | tf_op jit(solution)/shard_map/reshape;reshape | solution.py:57
  77.2 20.4 %fusion.26 = (f32[48,6,144]{2,1,0:T(8,128)S(1)}, f32[48,6,144,144]{2,3,1,0:T(8,128)}) fusion(pred[48,144]{1,0:T(8,128)(4,1)S(1)} %gt.30, bf16[48,144,1,6,32]{1,0,4,3,2:T(8,128)(2,1)S(1)} %get-tuple-element.128, bf16[48,144,1,6,32]{1,0,4,3,2:T(8,128)(2,1)S(1)} %get-tuple-element.127), kind=kOutput, calls=%fused_computation.43 | convolution fusion | flops 400080384 | bytes 29369088 | tf_op jit(solution)/shard_map/wqhd,wkhd->whqk/dot_general | solution.py:61
  97.6 20.8 %fusion.2 = f32[48,6,144]{2,1,0:T(8,128)S(1)} fusion(f32[48,6,144]{2,1,0:T(8,128)S(1)} %get-tuple-element.145, f32[48,6,144,144]{2,3,1,0:T(8,128)} %get-tuple-element.146, pred[48,144]{1,0:T(8,128)(4,1)S(1)} %gt.30), kind=kLoop, calls=%fused_computation.14 | loop fusion | flops 23846400 | bytes 24226560 | tf_op jit(solution)/shard_map/reduce_sum | solution.py:88
  118.4 20.5 %convert_bitcast_fusion.3 = bf16[48,144,6,32]{1,3,2,0:T(8,128)(2,1)} fusion(f32[48,6,144]{2,1,0:T(8,128)S(1)} %fusion.2, f32[48,6,144]{2,1,0:T(8,128)S(1)} %get-tuple-element.145, f32[48,6,144,144]{2,3,1,0:T(8,128)} %get-tuple-element.146, pred[48,144]{1,0:T(8,128)(4,1)S(1)} %gt.30, bf16[48,144,1,6,32]{1,0,4,3,2:T(8,128)(2,1)S(1)} %copy-done.15), kind=kOutput, calls=%fused_computation.110 | convolution fusion | flops 413392896 | bytes 29534976 | tf_op jit(solution)/shard_map/whqk,wkhd->wqhd/dot_general | solution.py:91
  315.5 32.2 %reshape_reshape.19 = bf16[72,144,3,6,32]{1,0,4,3,2:T(8,128)(2,1)} reshape(bf16[10368,576]{0,1:T(8,128)(2,1)} %convolution_convert_fusion) | data formatting | bytes 23887872 | tf_op jit(solution)/shard_map/reshape;reshape | solution.py:57
  361.3 45.8 %fusion.154 = (f32[72,6,144]{2,1,0:T(8,128)S(1)}, f32[72,6,144,144]{2,3,1,0:T(8,128)}) fusion(bf16[72,144,1,6,32]{1,0,4,3,2:T(8,128)(2,1)} %get-tuple-element.125, bf16[72,144,1,6,32]{1,0,4,3,2:T(8,128)(2,1)} %get-tuple-element.124, pred[72,144]{1,0:T(8,128)(4,1)S(1)} %gt.33), kind=kOutput, calls=%fused_computation.314 | convolution fusion | flops 600120576 | bytes 44053632 | tf_op jit(solution)/shard_map/wqhd,wkhd->whqk/dot_general | solution.py:61
  407.1 20.3 %fusion = f32[72,6,144]{2,1,0:T(8,128)S(1)} fusion(f32[72,6,144,144]{2,3,1,0:T(8,128)} %get-tuple-element.154, f32[72,6,144]{2,1,0:T(8,128)S(1)} %get-tuple-element.153), kind=kLoop, calls=%fused_computation.6 | loop fusion | flops 17853696 | bytes 36329472 | tf_op jit(solution)/shard_map/reduce_sum | solution.py:88
  428.4 28.1 %convert_bitcast_fusion.1 = bf16[72,144,6,32]{1,3,2,0:T(8,128)(2,1)} fusion(f32[72,6,144,144]{2,3,1,0:T(8,128)} %get-tuple-element.154, f32[72,6,144]{2,1,0:T(8,128)S(1)} %fusion, f32[72,6,144]{2,1,0:T(8,128)S(1)} %get-tuple-element.153, bf16[72,144,1,6,32]{1,0,4,3,2:T(8,128)(2,1)} %get-tuple-element.123), kind=kOutput, calls=%fused_computation.91 | convolution fusion | flops 602173440 | bytes 44292096 | tf_op jit(solution)/shard_map/whqk,wkhd->wqhd/dot_general | solution.py:91
  485.2 25.5 %dot_general.158 = bf16[2,12,18,2,12,192]{5,4,3,2,1,0:T(8,128)(2,1)} reshape(bf16[72,144,6,32]{3,2,1,0:T(8,128)(2,1)} %copy.125) | data formatting | bytes 7962624 | tf_op jit(solution)/shard_map/dot_general | solution.py:95
  738.5 31.1 %convert_bitcast_fusion = bf16[72,144,1,6,32]{1,4,3,0,2:T(8,128)(2,1)} fusion(f32[72,6,144,144]{2,3,1,0:T(8,128)} %get-tuple-element.154, f32[72,6,144]{2,1,0:T(8,128)S(1)} %copy-done.26, bf16[72,144,6,32]{1,0,3,2:T(8,128)(2,1)} %reshape.492), kind=kOutput, calls=%fused_computation.90 | convolution fusion | flops 593215488 | bytes 44043264 | tf_op jit(solution)/shard_map/whqk,wqhd->wkhd/dot_general | solution.py:151
  769.6 48.8 %multiply_reduce_fusion = (f32[72,6,144]{2,1,0:T(8,128)S(1)}, f32[72,6,144,144]{2,3,1,0:T(8,128)}) fusion(f32[72,6,144,144]{2,3,1,0:T(8,128)} %get-tuple-element.154, f32[72,6,144]{2,1,0:T(8,128)S(1)} %copy-done.26, bf16[72,144,1,6,32]{1,0,4,3,2:T(8,128)(2,1)} %get-tuple-element.123, bf16[72,144,6,32]{1,0,3,2:T(8,128)(2,1)} %reshape.492), kind=kOutput, calls=%fused_computation.1 | convolution fusion | flops 600120576 | bytes 80123904 | tf_op jit(solution)/shard_map/wqhd,wkhd->whqk/dot_general | solution.py:157
  818.3 50.8 %multiply_convert_fusion = bf16[72,6,144,144]{2,3,1,0:T(8,128)(2,1)} fusion(f32[72,6,144,144]{2,3,1,0:T(8,128)} %get-tuple-element.165, f32[72,6,144,144]{2,3,1,0:T(8,128)} %get-tuple-element.154, f32[72,6,144]{2,1,0:T(8,128)S(1)} %get-tuple-element.164, f32[72,6,144]{2,1,0:T(8,128)S(1)} %copy-done.26), kind=kLoop, calls=%fused_computation | loop fusion | flops 35831808 | bytes 90077184 | tf_op jit(solution)/shard_map/convert_element_type | solution.py:161
  925.0 26.2 %copy.145 = bf16[72,144,3,6,32]{1,0,4,3,2:T(8,128)(2,1)} copy(bf16[72,144,3,6,32]{1,4,3,0,2:T(8,128)(2,1)S(1)} %pad_maximum_fusion) | data formatting | bytes 23887872 | tf_op jit(solution)/shard_map/stack | solution.py:171
  951.2 53.5 %copy.132 = bf16[72,144,3,6,32]{4,3,2,1,0:T(8,128)(2,1)} copy(bf16[72,144,3,6,32]{1,4,3,0,2:T(8,128)(2,1)} %copy-done.4) | data formatting | bytes 23887872 | tf_op jit(solution)/shard_map/stack | solution.py:171
  1016.6 29.1 %convert_element_type.235 = bf16[10368,576]{0,1:T(8,128)(2,1)} reshape(bf16[72,144,3,6,32]{1,0,4,3,2:T(8,128)(2,1)} %copy.145) | data formatting | bytes 23887872 | tf_op jit(solution)/shard_map/convert_element_type | solution.py:173
  1057.2 70.0 %convert_element_type.222 = bf16[2,12,18,2,12,576]{5,4,3,2,1,0:T(8,128)(2,1)} reshape(bf16[72,144,3,6,32]{4,3,2,1,0:T(8,128)(2,1)} %copy.132) | data formatting | bytes 23887872 | tf_op jit(solution)/shard_map/convert_element_type | solution.py:173
  1326.9 20.8 %convert_bitcast_fusion.2 = bf16[48,144,1,6,32]{1,4,3,0,2:T(8,128)(2,1)} fusion(f32[48,6,144]{2,1,0:T(8,128)} %log_add_fusion.1, f32[48,6,144,144]{2,3,1,0:T(8,128)} %get-tuple-element.146, pred[48,144]{1,0:T(8,128)(4,1)S(1)} %copy-done.90, bf16[48,144,6,32]{1,0,3,2:T(8,128)(2,1)} %reshape.493), kind=kOutput, calls=%fused_computation.108 | convolution fusion | flops 407420928 | bytes 29369088 | tf_op jit(solution)/shard_map/whqk,wqhd->wkhd/dot_general | solution.py:151
  1347.7 41.3 %multiply_reduce_fusion.1 = (f32[48,6,144]{2,1,0:T(8,128)}, f32[48,6,144,144]{2,3,1,0:T(8,128)}) fusion(f32[48,6,144]{2,1,0:T(8,128)} %log_add_fusion.1, f32[48,6,144,144]{2,3,1,0:T(8,128)} %get-tuple-element.146, pred[48,144]{1,0:T(8,128)(4,1)S(1)} %copy-done.90, bf16[48,144,1,6,32]{1,0,4,3,2:T(8,128)(2,1)} %get-tuple-element.126, ...), kind=kOutput, calls=%fused_computation.9 | convolution fusion | flops 412024320 | bytes 53422848 | tf_op jit(solution)/shard_map/wqhd,wkhd->whqk/dot_general | solution.py:157
  1389.0 34.4 %multiply_convert_fusion.1 = bf16[48,6,144,144]{2,3,1,0:T(8,128)(2,1)} fusion(f32[48,6,144,144]{2,3,1,0:T(8,128)} %get-tuple-element.171, f32[48,6,144]{2,1,0:T(8,128)} %get-tuple-element.170, f32[48,6,144]{2,1,0:T(8,128)} %log_add_fusion.1, f32[48,6,144,144]{2,3,1,0:T(8,128)} %get-tuple-element.146, pred[48,144]{1,0:T(8,128)(4,1)S(1)} %copy-done.90), kind=kLoop, calls=%fused_computation.8 | loop fusion | flops 35831808 | bytes 60058368 | tf_op jit(solution)/shard_map/convert_element_type | solution.py:161
  1474.7 36.3 %copy.142 = bf16[48,144,3,6,32]{4,3,2,1,0:T(8,128)(2,1)} copy(bf16[48,144,3,6,32]{1,4,3,0,2:T(8,128)(2,1)} %copy-done.5) | data formatting | bytes 15925248 | tf_op jit(solution)/shard_map/stack | solution.py:171
  1514.3 24.5 %convert_element_type.234 = bf16[6912,576]{0,1:T(8,128)(2,1)} reshape(bf16[48,144,3,6,32]{1,0,4,3,2:T(8,128)(2,1)} %copy.144) | data formatting | bytes 15925248 | tf_op jit(solution)/shard_map/convert_element_type | solution.py:173
  1546.1 47.3 %convert_element_type.232 = bf16[2,12,12,2,12,576]{5,4,3,2,1,0:T(8,128)(2,1)} reshape(bf16[48,144,3,6,32]{4,3,2,1,0:T(8,128)(2,1)} %copy.142) | data formatting | bytes 15925248 | tf_op jit(solution)/shard_map/convert_element_type | solution.py:173
  1637.5 42.9 %all-reduce.1 = (f32[]{:T(128)}, f32[20,192]{1,0:T(8,128)S(1)}, f32[2,5,192]{2,0,1:T(2,128)S(1)}, f32[128]{0:T(128)S(1)}, f32[]{:T(128)}) all-reduce(f32[]{:T(128)S(6)} %mul.956, f32[20,192]{1,0:T(8,128)S(1)} %fusion.122, f32[2,5,192]{2,0,1:T(2,128)S(1)} %pad_maximum_fusion.10, ...), channel_id=1, replica_groups=mesh['lat'=8,'batch'=4] {'lat','batch'}, use_global_device_ids=true, to_apply=%region_28.29 | all-reduce | flops 5890 | bytes 47120 | tf_op jit(solution)/shard_map/psum | solution.py:339
  1684.2 90.1 %all-reduce.5.cloned.1.call-done = (f32[128,192]{0,1:T(8,128)}, f32[2,192,576]{2,1,0:T(8,128)}, f32[2,192,192]{2,1,0:T(8,128)}, f32[2,192,768]{2,1,0:T(8,128)}, ...) async-done(((f32[128,192]{0,1:T(8,128)}, f32[2,192,576]{2,1,0:T(8,128)}, f32[2,192,192]{2,1,0:T(8,128)}, f32[2,192,768]{2,1,0:T(8,128)}, f32[2,768,192]{1,2,0:T(8,128)}, ...) | async-done | bytes 3735568 | tf_op jit(solution)/shard_map/psum | solution.py:339
  (508 shorter events, 915.2 us)
Async XLA Ops:
  7.2 1767.1 %all-reduce.5.cloned.1.call-start = ((), (), s32[]{:S(2)}) async-start(), calls=%async_computation | async-start | bytes 7864320 | tf_op jit(solution)/shard_map/psum | solution.py:339
  9.7 108.7 %copy-start.89 = (pred[48,144]{1,0:T(8,128)(4,1)}, pred[48,144]{1,0:T(8,128)(4,1)S(1)}, u32[]{:S(2)}) copy-start(pred[48,144]{1,0:T(8,128)(4,1)S(1)} %gt.30) | copy-start | bytes 20740
  18.6 150.3 %copy-start.95 = (f32[2,192]{1,0:T(2,128)}, f32[2,192]{1,0:T(2,128)S(1)}, u32[]{:S(2)}) copy-start(f32[2,192]{1,0:T(2,128)S(1)} %fusion.123) | copy-start | bytes 4612
  243.5 30.4 %collective-permute-start.1 = (bf16[2,12,3,2,12,192]{5,3,4,2,1,0:T(2,128)(2,1)S(1)}, bf16[2,12,3,2,12,192]{5,3,4,2,1,0:T(2,128)(2,1)S(1)}, u32[]{:S(2)}, u32[]{:S(2)}) collective-permute-start(bf16[2,12,3,2,12,192]{5,3,4,2,1,0:T(2,128)(2,1)S(1)} %copy.118), channel_id=1, source_target_pairs={{4,0},{8,4},{12,8},{16,12},{20,16},{24,20},{28,24},{5,1},{9,5},{13... | collective-permute-start | bytes 1990664 | tf_op jit(solution)/shard_map/ppermute | solution.py:29
  246.4 40.8 %collective-permute-start = (bf16[2,12,3,2,12,192]{5,3,4,2,1,0:T(2,128)(2,1)}, bf16[2,12,3,2,12,192]{5,3,4,2,1,0:T(2,128)(2,1)}, u32[]{:S(2)}, u32[]{:S(2)}) collective-permute-start(bf16[2,12,3,2,12,192]{5,3,4,2,1,0:T(2,128)(2,1)} %copy.117), channel_id=1, source_target_pairs={{0,4},{4,8},{8,12},{12,16},{16,20},{20,24},{24,28},{1,5},{5,9},{9,... | collective-permute-start | bytes 1990664 | tf_op jit(solution)/shard_map/ppermute | solution.py:26
  1057.2 70.0 %copy-start.51 = (bf16[2,192,576]{2,1,0:T(8,128)(2,1)S(1)}, bf16[2,192,576]{2,1,0:T(8,128)(2,1)}, u32[]{:S(2)}) copy-start(bf16[2,192,576]{2,1,0:T(8,128)(2,1)} %convert_element_type.192) | copy-start | bytes 1327108
  1146.2 24.5 %collective-permute-start.3 = (bf16[2,12,3,2,12,192]{5,3,4,2,1,0:T(2,128)(2,1)}, bf16[2,12,3,2,12,192]{5,3,4,2,1,0:T(2,128)(2,1)}, u32[]{:S(2)}, u32[]{:S(2)}) collective-permute-start(bf16[2,12,3,2,12,192]{5,3,4,2,1,0:T(2,128)(2,1)} %copy.134), channel_id=1, source_target_pairs={{4,0},{8,4},{12,8},{16,12},{20,16},{24,20},{28,24},{5,1},{9,5},{13... | collective-permute-start | bytes 1990664 | tf_op jit(solution)/shard_map/ppermute | solution.py:29
  1147.5 42.3 %collective-permute-start.2 = (bf16[2,12,3,2,12,192]{5,3,4,2,1,0:T(2,128)(2,1)}, bf16[2,12,3,2,12,192]{5,3,4,2,1,0:T(2,128)(2,1)}, u32[]{:S(2)}, u32[]{:S(2)}) collective-permute-start(bf16[2,12,3,2,12,192]{5,3,4,2,1,0:T(2,128)(2,1)} %copy.133), channel_id=1, source_target_pairs={{0,4},{4,8},{8,12},{12,16},{16,20},{20,24},{24,28},{1,5},{5,9},{9,... | collective-permute-start | bytes 1990664 | tf_op jit(solution)/shard_map/ppermute | solution.py:26
  1474.7 36.3 %copy-start.118 = (f32[192]{0:T(256)S(1)}, f32[192]{0:T(256)}, u32[]{:S(2)}) copy-start(f32[192]{0:T(256)} %get-tuple-element.56) | copy-start | bytes 2308
  1474.7 36.3 %copy-start.122 = (f32[192]{0:T(256)S(1)}, f32[192]{0:T(256)}, u32[]{:S(2)}) copy-start(f32[192]{0:T(256)} %get-tuple-element.60) | copy-start | bytes 2308
  1474.7 36.3 %copy-start.117 = (f32[192]{0:T(256)S(1)}, f32[192]{0:T(256)}, u32[]{:S(2)}) copy-start(f32[192]{0:T(256)} %get-tuple-element.67) | copy-start | bytes 2308
  1474.7 36.3 %copy-start.121 = (f32[192]{0:T(256)S(1)}, f32[192]{0:T(256)}, u32[]{:S(2)}) copy-start(f32[192]{0:T(256)} %get-tuple-element.66) | copy-start | bytes 2308
  1546.1 47.3 %copy-start.34 = (f32[2,12,12,2,12]{4,3,2,1,0:T(2,128)S(1)}, f32[2,12,12,2,12]{4,3,2,1,0:T(2,128)}, u32[]{:S(2)}) copy-start(f32[2,12,12,2,12]{4,3,2,1,0:T(2,128)} %copy-done.33) | copy-start | bytes 82948
  1546.1 47.3 %copy-start.52 = (bf16[2,192,576]{2,1,0:T(8,128)(2,1)S(1)}, bf16[2,192,576]{2,1,0:T(8,128)(2,1)}, u32[]{:S(2)}) copy-start(bf16[2,192,576]{2,1,0:T(8,128)(2,1)} %convert_element_type.192) | copy-start | bytes 1327108
  1546.1 47.3 %copy-start.54 = (f32[2,12,12,2,12]{4,3,2,1,0:T(2,128)S(1)}, f32[2,12,12,2,12]{4,3,2,1,0:T(2,128)}, u32[]{:S(2)}) copy-start(f32[2,12,12,2,12]{4,3,2,1,0:T(2,128)} %copy-done.53) | copy-start | bytes 82948
  1546.1 47.3 %copy-start.96 = (f32[2,192]{1,0:T(2,128)S(1)}, f32[2,192]{1,0:T(2,128)}, u32[]{:S(2)}) copy-start(f32[2,192]{1,0:T(2,128)} %copy-done.95) | copy-start | bytes 4612
  1546.1 47.4 %copy-start.111 = (f32[1,1,192]{2,0,1:T(1,128)S(1)}, f32[1,1,192]{2,0,1:T(1,128)}, u32[]{:S(2)}) copy-start(f32[1,1,192]{2,0,1:T(1,128)} %copy-done.110) | copy-start | bytes 2308
  1629.6 165.8 %copy-start.99 = (f32[20,192]{1,0:T(8,128)S(1)}, f32[20,192]{1,0:T(8,128)}, u32[]{:S(2)}) copy-start(f32[20,192]{1,0:T(8,128)} %param.40) | copy-start | bytes 46084
  1629.6 165.8 %copy-start.100 = (f32[20,192]{1,0:T(8,128)S(1)}, f32[20,192]{1,0:T(8,128)}, u32[]{:S(2)}) copy-start(f32[20,192]{1,0:T(8,128)} %param.49) | copy-start | bytes 46084
  1629.7 165.7 %copy-start.101 = (f32[20,192]{1,0:T(8,128)S(1)}, f32[20,192]{1,0:T(8,128)}, u32[]{:S(2)}) copy-start(f32[20,192]{1,0:T(8,128)} %param.58) | copy-start | bytes 46084
  1629.7 169.6 %copy-start.93 = (f32[128,192]{0,1:T(8,128)S(1)}, f32[128,192]{0,1:T(8,128)}, u32[]{:S(2)}) copy-start(f32[128,192]{0,1:T(8,128)} %param.39) | copy-start | bytes 294916
  1629.7 175.8 %copy-start.46 = (f32[2,192,576]{2,1,0:T(8,128)S(1)}, f32[2,192,576]{2,1,0:T(8,128)}, u32[]{:S(2)}) copy-start(f32[2,192,576]{2,1,0:T(8,128)} %param.41) | copy-start | bytes 2654212
  1637.2 172.8 %copy-start.35 = (f32[2,768,192]{1,2,0:T(8,128)S(1)}, f32[2,768,192]{1,2,0:T(8,128)}, u32[]{:S(2)}) copy-start(f32[2,768,192]{1,2,0:T(8,128)} %param.44) | copy-start | bytes 3538948
  1774.3 35.7 %copy-start.38 = (f32[2,768,192]{1,2,0:T(8,128)S(1)}, f32[2,768,192]{1,2,0:T(8,128)}, u32[]{:S(2)}) copy-start(f32[2,768,192]{1,2,0:T(8,128)} %get-tuple-element.80) | copy-start | bytes 3538948
  (142 other events, 1610.4 us)
Sparse Core Ops, SparseCore 0:
  1629.7 144.5 all-reduce.4
where the time goes:
time: 1840 us; the launch traced here: 1830 us
  local copies, waits for them, and re-layouts  694 us (38%)
  matrix products  581 us (32%)
  other arithmetic  338 us (18%)
  waiting for transfers between devices  131 us (7%)
  blocking collectives  42.9 us (2%)
  between operations  24.5 us (1%)
    convert_element_type x4, local copies, waits for them, and re-layouts, backward_block(): d_packed = jnp.stack([d_query, d_keys, d_values], axis=2).reshape(count_w...  171 us
    another operation x4, local copies, waits for them, and re-layouts, backward_block(): jnp.stack([d_query, d_keys, d_values], axis=2).reshape(count_w * width, -1)  126 us
    psum x1, waiting for transfers between devices, on_device(): lax.psum((g_embed, g_lead, g_qkv_all, g_proj_all, g_up_all, g_down_all, g...  90.1 us
    dot_general x2, matrix products, backward_block(): jnp.einsum('wqhd,wkhd->whqk', d_mixture, value_rows, preferred_element_ty...  90.1 us
    convert_element_type x2, other arithmetic, backward_block(): d_scores = (probability * (d_probability - row_terms)).astype(jnp.bfloat16)  85.2 us
    dot_general x2, matrix products, scores_of(): jnp.einsum('wqhd,wkhd->whqk', query_rows, key_rows, preferred_element_typ...  66.2 us
    another operation x2, local copies, waits for them, and re-layouts, scores_of(): parts = packed.reshape(count_w, width, 3, HEADS, -1)  57.7 us
    dot_general x2, matrix products, backward_block(): jnp.einsum('whqk,wqhd->wkhd', probability.astype(jnp.bfloat16), d_mixture...  51.9 us
  transfers between devices with their start and end apart: 5, of which 4 were waited for; matrix products, arithmetic and copies ran while one was open for 2% of the time, Pallas kernels for 0%

commit v1 on v0

v1 whole, which is shorter than its diff:
```python
from functools import partial
import math

import jax
import jax.numpy as jnp
from jax import lax
from jax.experimental import pallas as pl
from jax.experimental.pallas import tpu as pltpu
from jax.sharding import PartitionSpec as P

HEADS = 6
LEADS = 20
STEP = 10
C = 192
FF = 768
CIN = 128
HDIM = 32
COL = 288
WIN = 144
HALF = 72
LANES = 896
SCALE = HDIM ** (-0.5)
SCALE2 = SCALE * math.log2(math.e)
BF = jnp.bfloat16
F32 = jnp.float32

beta_one = 0.9
beta_two = 0.999
adam_eps = 1e-08
clip_max = 0.005
rate_table = (0.2, 1.0, 0.2, 0.2, 0.2, 0.2, 0.2, 1.0, 1.0)
decay_table = (0.1, 0.1, 0.1, 0.1, 0.1, 0.1, 0.1, 0.0, 0.0)

VMEM_BYTES = 56 * 1024 * 1024


def dot(a, b):
    return lax.dot_general(a, b, (((1,), (0,)), ((), ())), preferred_element_type=F32)


def dot_nt(a, b):
    return lax.dot_general(a, b, (((1,), (1,)), ((), ())), preferred_element_type=F32)


def dot_tn(a, b):
    return lax.dot_general(a, b, (((0,), (0,)), ((), ())), preferred_element_type=F32)


def norm_stats(x):
    center = x - jnp.mean(x, axis=-1, keepdims=True)
    rstd = lax.rsqrt(jnp.mean(center * center, axis=-1, keepdims=True) + 1e-05)
    return center * rstd, rstd


def norm_back(dy, xhat, rstd, gain):
    dxhat = dy * gain
    first = jnp.mean(dxhat, axis=-1, keepdims=True)
    second = jnp.mean(dxhat * xhat, axis=-1, keepdims=True)
    return rstd * (dxhat - first - xhat * second)


def add_norm_grads(acc_ref, index, dy, xhat):
    acc_ref[2 * index : 2 * index + 1] += jnp.sum(dy * xhat, axis=0, keepdims=True)
    acc_ref[2 * index + 1 : 2 * index + 2] += jnp.sum(dy, axis=0, keepdims=True)


def gelu_both(x):
    c0 = math.sqrt(2.0 / math.pi)
    c1 = c0 * 0.044715
    square = x * x
    slope = jnp.tanh(x * (c0 + c1 * square))
    half = 0.5 + 0.5 * slope
    active = x * half
    return active, half + active * ((1.0 - slope) * (c0 + (3.0 * c1) * square))


def head_masks():
    lane = lax.broadcasted_iota(jnp.int32, (1, C), 1) // HDIM
    return [(lane == h).astype(F32).astype(BF) for h in range(HEADS)]


def expand(x, masks, edge):
    rem = [x[128:144] * masks[h] for h in range(HEADS)] + [jnp.zeros((32, C), BF)]
    if edge:
        low = [x[0:64] * masks[h] for h in range(HEADS)]
        high = [x[64:128] * masks[h] for h in range(HEADS)]
        return jnp.concatenate(low + rem + high, axis=0)
    return jnp.concatenate([x[0:128] * masks[h] for h in range(HEADS)] + rem, axis=0)


def low_lanes():
    return lax.broadcasted_iota(jnp.int32, (1, 128), 1) % 16 < 8


def score_like(keys, expanded, edge):
    if not edge:
        return dot_nt(keys, expanded)
    low = dot_nt(keys[0], expanded[0:512])
    high = dot_nt(keys[1], expanded[384:896])
    rem = jnp.where(low_lanes(), low[:, 384:512], high[:, 0:128])
    return jnp.concatenate([low[:, 0:384], rem, high[:, 128:512]], axis=1)


def pick_rem(rem, masks32):
    back = rem.T
    total = back[0:16] * masks32[0]
    for h in range(1, HEADS):
        total = total + back[16 * h : 16 * h + 16] * masks32[h]
    return total


def query_side(vals_t, weights, masks32, edge):
    if not edge:
        blocks = []
        for pair in range(3):
            both = dot(vals_t[64 * pair : 64 * pair + 64], weights[:, 256 * pair : 256 * pair + 256])
            blocks += [both[0:32, 0:128], both[32:64, 128:256]]
        rem = dot(vals_t, weights[:, 768:896])
    else:
        low_a = dot(vals_t[0][0:128], weights[:, 0:256])
        low_b = dot(vals_t[0][128:192], weights[:, 256:384])
        high_a = dot(vals_t[1][0:128], weights[:, 512:768])
        high_b = dot(vals_t[1][128:192], weights[:, 768:896])
        rem_low = dot(vals_t[0], weights[:, 384:512])
        rem_high = dot(vals_t[1], weights[:, 384:512])
        rem = jnp.where(low_lanes(), rem_low, rem_high)
        left = lax.broadcasted_iota(jnp.int32, (1, 128), 1) < 64
        blocks = []
        for h in range(HEADS):
            src_low, src_high, local = (low_a, high_a, h) if h < 4 else (low_b, high_b, h - 4)
            group = slice(128 * (local // 2), 128 * (local // 2) + 128)
            low = src_low[32 * local : 32 * local + 32, group]
            high = src_high[32 * local : 32 * local + 32, group]
            if h % 2:
                low = pltpu.roll(low, 64, 1)
            else:
                high = pltpu.roll(high, 64, 1)
            blocks.append(jnp.where(left, low, high))
    main = jnp.concatenate(blocks, axis=0).T
    return jnp.concatenate([main, pick_rem(rem, masks32)], axis=0)


def key_side(weights, expanded, edge):
    if not edge:
        return dot(weights, expanded)
    mask = low_lanes()
    rem = weights[:, 384:512]
    zero = jnp.zeros((), weights.dtype)
    low = jnp.concatenate([weights[:, 0:384], jnp.where(mask, rem, zero)], axis=1)
    high = jnp.concatenate([jnp.where(mask, zero, rem), weights[:, 512:896]], axis=1)
    return dot(low, expanded[0:512]), dot(high, expanded[384:896])


def edge_bias(scores, bias):
    low, high = bias
    low_rem = jnp.where(low_lanes(), low, high)
    top = scores[0:HALF]
    top = jnp.concatenate([top[:, 0:384] + low, top[:, 384:512] + low_rem, top[:, 512:896] + high], axis=1)
    return jnp.concatenate([top, scores[HALF:]], axis=0)


def attention_forward(q, k, vals, masks, masks32, edge, bias=None):
    queries = expand(q, masks, edge)
    scores = score_like(k, queries, edge)
    if edge:
        scores = edge_bias(scores, bias)
    scores = scores * SCALE2
    highest = jnp.max(scores, axis=0, keepdims=True)
    expo = jnp.exp2(scores - highest)
    total = jnp.sum(expo, axis=0, keepdims=True)
    probs = (expo * (1.0 / total)).astype(BF)
    vals_t = (vals[0].T, vals[1].T) if edge else vals.T
    mixture = query_side(vals_t, probs, masks32, edge)
    return mixture, highest + jnp.log2(total)


def attention_backward(q, k, vals, log_total, dmix, masks, masks32, edge, bias=None):
    queries = expand(q, masks, edge)
    scores = score_like(k, queries, edge)
    if edge:
        scores = edge_bias(scores, bias)
    probs = jnp.exp2(scores * SCALE2 - log_total)
    douts = expand(dmix, masks, edge)
    dprobs = score_like(vals, douts, edge)
    row_terms = jnp.sum(dprobs * probs, axis=0, keepdims=True)
    dscores = (probs * (dprobs - row_terms)).astype(BF)
    dvals = key_side(probs.astype(BF), douts, edge)
    dkeys = key_side(dscores, queries, edge)
    k_t = (k[0].T, k[1].T) if edge else k.T
    dq = query_side(k_t, dscores, masks32, edge) * SCALE
    if edge:
        dkeys = (dkeys[0] * SCALE, dkeys[1] * SCALE)
    else:
        dkeys = dkeys * SCALE
    return dq, dkeys, dvals


def forward_zero(
    columns,
    step_ref,
    an_ref,
    lead_ref,
    embed_ref,
    qkv_ref,
    proj_ref,
    up_ref,
    down_ref,
    norm_ref,
    h0_ref,
    pack_ref,
    lse_ref,
    mix_ref,
    h2_ref,
    act_ref,
    slope_ref,
    h1_ref,
    top_ref,
    bot_ref,
    wembed,
    wqkv,
    wproj,
    wup,
    wdown,
    sample,
):
    @pl.when(pl.program_id(0) == 0)
    def _():
        wembed[...] = embed_ref[...].astype(BF)
        wqkv[...] = qkv_ref[0].astype(BF)
        wproj[...] = proj_ref[0].astype(BF)
        wup[...] = up_ref[0].astype(BF)
        wdown[...] = down_ref[0].astype(BF)

    masks = head_masks()
    masks32 = [m.astype(F32) for m in masks]
    lead_row = lead_ref[pl.ds(step_ref[sample] - 1, 1), :]
    for col in range(columns):
        hidden = dot_nt(an_ref[col], wembed[...]) + lead_row
        h0_ref[col] = hidden
        xhat, _ = norm_stats(hidden)
        normed = (xhat * norm_ref[0, 0:1] + norm_ref[0, 1:2]).astype(BF)
        packed = dot(normed, wqkv[...]).astype(BF)
        pack_ref[col] = packed
        mixtures = []
        for w in range(2):
            part = packed[WIN * w : WIN * w + WIN]
            mixture, log_total = attention_forward(
                part[:, 0:C], part[:, C : 2 * C], part[:, 2 * C :], masks, masks32, False
            )
            lse_ref[col, w : w + 1] = log_total
            mixtures.append(mixture)
        mixture = jnp.concatenate(mixtures, axis=0).astype(BF)
        mix_ref[col] = mixture
        hidden_two = hidden + dot(mixture, wproj[...])
        h2_ref[col] = hidden_two
        xhat, _ = norm_stats(hidden_two)
        normed_two = (xhat * norm_ref[1, 0:1] + norm_ref[1, 1:2]).astype(BF)
        active, slope = gelu_both(dot(normed_two, wup[...]))
        active = active.astype(BF)
        act_ref[col] = active
        slope_ref[col] = slope
        hidden_one = hidden_two + dot_nt(active, wdown[...])
        h1_ref[col] = hidden_one
        xhat, _ = norm_stats(jnp.concatenate([hidden_one[0:HALF], hidden_one[COL - HALF :]], axis=0))
        normed = xhat * norm_ref[2, 0:1] + norm_ref[2, 1:2]
        top_ref[col] = normed[0:HALF].astype(BF)
        bot_ref[col] = normed[HALF:].astype(BF)


def spread(top, middle_and_ends):
    return jnp.concatenate([top[0:64], middle_and_ends[0:64], top[64:72], middle_and_ends[64:72]], axis=0)


def middle(
    columns,
    flag_ref,
    h1_ref,
    up_in_ref,
    down_in_ref,
    target_ref,
    mask_ref,
    qkv_ref,
    proj_ref,
    up_ref,
    down_ref,
    decode_ref,
    norm_ref,
    scale_ref,
    *rest,
    first,
):
    if first:
        prev = None
    else:
        prev, rest = rest[:8], rest[8:]
    (
        dh2_ref,
        dn_ref,
        dtop_ref,
        dbot_ref,
        gqkv_ref,
        gproj_ref,
        gup_ref,
        gdown_ref,
        gdec_ref,
        gnorm_ref,
        gscale_ref,
        count_ref,
        wqkv,
        wproj,
        wup,
        wdown,
        wdec,
    ) = rest
    sums = (gqkv_ref, gproj_ref, gup_ref, gdown_ref, gdec_ref, gnorm_ref, gscale_ref, count_ref)

    @pl.when(pl.program_id(0) == 0)
    def _():
        wqkv[...] = qkv_ref[0].astype(BF)
        wproj[...] = proj_ref[0].astype(BF)
        wup[...] = up_ref[0].astype(BF)
        wdown[...] = down_ref[0].astype(BF)
        wdec[...] = decode_ref[...].astype(BF)
        for at, ref in enumerate(sums):
            ref[...] = jnp.zeros_like(ref) if prev is None else prev[at][...]

    masks = head_masks()
    masks32 = [m.astype(F32) for m in masks]
    bias = (flag_ref[0], flag_ref[1])
    inverse = jnp.exp(-scale_ref[...])
    for col in range(columns):
        h1 = jnp.concatenate(
            [
                h1_ref[col, 0:64],
                h1_ref[col, 216:280],
                h1_ref[col, 64:72],
                h1_ref[col, 280:288],
                h1_ref[col, 72:216],
            ],
            axis=0,
        )
        xhat_one, rstd_one = norm_stats(h1)
        normed = xhat_one * norm_ref[2, 0:1] + norm_ref[2, 1:2]
        normed_low = normed.astype(BF)
        n_top = jnp.concatenate([up_in_ref[col].astype(F32), normed[0:64], normed[128:136]], axis=0).astype(BF)
        n_bot = jnp.concatenate([down_in_ref[col].astype(F32), normed[64:128], normed[136:144]], axis=0).astype(BF)
        n_kv = jnp.concatenate([n_top, n_bot, normed_low[WIN:]], axis=0)
        queries = dot(normed_low, wqkv[:, 0:C]).astype(BF)
        keys_vals = dot(n_kv, wqkv[:, C:]).astype(BF)
        keys, vals = keys_vals[:, 0:C], keys_vals[:, C:]
        k_edge, v_edge = (keys[0:WIN], keys[WIN : 2 * WIN]), (vals[0:WIN], vals[WIN : 2 * WIN])
        mix_e, lse_e = attention_forward(queries[0:WIN], k_edge, v_edge, masks, masks32, True, bias)
        mix_m, lse_m = attention_forward(queries[WIN:], keys[2 * WIN :], vals[2 * WIN :], masks, masks32, False)
        mixture = jnp.concatenate([mix_e, mix_m], axis=0).astype(BF)
        hidden_two = h1 + dot(mixture, wproj[...])
        xhat_two, rstd_two = norm_stats(hidden_two)
        normed_two = (xhat_two * norm_ref[3, 0:1] + norm_ref[3, 1:2]).astype(BF)
        active, slope = gelu_both(dot(normed_two, wup[...]))
        active = active.astype(BF)
        hidden = hidden_two + dot_nt(active, wdown[...])
        xhat, rstd = norm_stats(hidden)
        normed_last = (xhat * norm_ref[4, 0:1] + norm_ref[4, 1:2]).astype(BF)
        predicted = dot(normed_last, wdec[...])
        target = jnp.concatenate(
            [
                target_ref[col, 0:64],
                target_ref[col, 216:280],
                target_ref[col, 64:72],
                target_ref[col, 280:288],
                target_ref[col, 72:216],
            ],
            axis=0,
        )
        cells = dot_tn(mask_ref[col], jnp.ones((8, CIN), BF))
        cells = jnp.concatenate([cells[0:64], cells[216:280], cells[64:72], cells[280:288], cells[72:216]], axis=0)
        error = predicted - target
        square = error * error + 1.0
        back = lax.rsqrt(square)
        gscale_ref[0:1] += jnp.sum(cells * (1.0 - square * back * inverse), axis=0, keepdims=True)
        count_ref[0:1] += jnp.sum(cells, axis=0, keepdims=True)
        dpred = (cells * inverse * error * back).astype(BF)
        gdec_ref[...] += dot_tn(normed_last, dpred)
        dnorm = dot_nt(dpred, wdec[...])
        add_norm_grads(gnorm_ref, 2, dnorm, xhat)
        grad = norm_back(dnorm, xhat, rstd, norm_ref[4, 0:1])
        grad_low = grad.astype(BF)
        gdown_ref[...] += dot_tn(grad_low, active)
        dinner = (dot(grad_low, wdown[...]) * slope).astype(BF)
        gup_ref[...] += dot_tn(normed_two, dinner)
        dnorm = dot_nt(dinner, wup[...])
        add_norm_grads(gnorm_ref, 1, dnorm, xhat_two)
        grad = grad + norm_back(dnorm, xhat_two, rstd_two, norm_ref[3, 0:1])
        grad_low = grad.astype(BF)
        gproj_ref[...] += dot_tn(mixture, grad_low)
        dmix = dot_nt(grad_low, wproj[...]).astype(BF)
        dq_e, dk_e, dv_e = attention_backward(
            queries[0:WIN], k_edge, v_edge, lse_e, dmix[0:WIN], masks, masks32, True, bias
        )
        dq_m, dk_m, dv_m = attention_backward(
            queries[WIN:], keys[2 * WIN :], vals[2 * WIN :], lse_m, dmix[WIN:], masks, masks32, False
        )
        dq = jnp.concatenate([dq_e, dq_m], axis=0).astype(BF)
        dk = jnp.concatenate([dk_e[0], dk_e[1], dk_m], axis=0).astype(BF)
        dv = jnp.concatenate([dv_e[0], dv_e[1], dv_m], axis=0).astype(BF)
        dkv = jnp.concatenate([dk, dv], axis=1)
        gqkv_ref[:, 0:C] += dot_tn(normed_low, dq)
        gqkv_ref[:, C:] += dot_tn(n_kv, dkv)
        dn_q = dot_nt(dq, wqkv[:, 0:C])
        dn_kv = dot_nt(dkv, wqkv[:, C:])
        dtop_ref[col] = dn_kv[0:HALF].astype(BF)
        dbot_ref[col] = dn_kv[WIN : WIN + HALF].astype(BF)
        dn_ref[col, 0:64] = dn_q[0:64] + dn_kv[72:136]
        dn_ref[col, 64:72] = dn_q[128:136] + dn_kv[136:144]
        dn_ref[col, 72:216] = dn_q[144:288] + dn_kv[288:432]
        dn_ref[col, 216:280] = dn_q[64:128] + dn_kv[216:280]
        dn_ref[col, 280:288] = dn_q[136:144] + dn_kv[280:288]
        dh2_ref[col, 0:64] = grad[0:64]
        dh2_ref[col, 64:72] = grad[128:136]
        dh2_ref[col, 72:216] = grad[144:288]
        dh2_ref[col, 216:280] = grad[64:128]
        dh2_ref[col, 280:288] = grad[136:144]


def backward_zero(
    columns,
    step_ref,
    an_ref,
    h0_ref,
    pack_ref,
    lse_ref,
    mix_ref,
    h2_ref,
    act_ref,
    slope_ref,
    h1_ref,
    dh2_ref,
    dn_ref,
    ret_top_ref,
    ret_bot_ref,
    qkv_ref,
    proj_ref,
    up_ref,
    down_ref,
    norm_ref,
    *rest,
    first,
    sample,
):
    if first:
        prev = None
    else:
        prev, rest = rest[:7], rest[7:]
    (
        gembed_ref,
        glead_ref,
        gqkv_ref,
        gproj_ref,
        gup_ref,
        gdown_ref,
        gnorm_ref,
        wqkv,
        wproj,
        wup,
        wdown,
    ) = rest
    sums = (gembed_ref, glead_ref, gqkv_ref, gproj_ref, gup_ref, gdown_ref, gnorm_ref)

    @pl.when(pl.program_id(0) == 0)
    def _():
        wqkv[...] = qkv_ref[0].astype(BF)
        wproj[...] = proj_ref[0].astype(BF)
        wup[...] = up_ref[0].astype(BF)
        wdown[...] = down_ref[0].astype(BF)
        for at, ref in enumerate(sums):
            ref[...] = jnp.zeros_like(ref) if prev is None else prev[at][...]

    masks = head_masks()
    masks32 = [m.astype(F32) for m in masks]
    lead_at = pl.ds(step_ref[sample] - 1, 1)
    for col in range(columns):
        dn = jnp.concatenate(
            [
                dn_ref[col, 0:HALF] + ret_top_ref[col].astype(F32),
                dn_ref[col, HALF : COL - HALF],
                dn_ref[col, COL - HALF :] + ret_bot_ref[col].astype(F32),
            ],
            axis=0,
        )
        xhat, rstd = norm_stats(h1_ref[col])
        add_norm_grads(gnorm_ref, 2, dn, xhat)
        grad = dh2_ref[col] + norm_back(dn, xhat, rstd, norm_ref[2, 0:1])
        grad_low = grad.astype(BF)
        gdown_ref[...] += dot_tn(grad_low, act_ref[col])
        dinner = (dot(grad_low, wdown[...]) * slope_ref[col]).astype(BF)
        xhat, rstd = norm_stats(h2_ref[col])
        normed_two = (xhat * norm_ref[1, 0:1] + norm_ref[1, 1:2]).astype(BF)
        gup_ref[...] += dot_tn(normed_two, dinner)
        dnorm = dot_nt(dinner, wup[...])
        add_norm_grads(gnorm_ref, 1, dnorm, xhat)
        grad = grad + norm_back(dnorm, xhat, rstd, norm_ref[1, 0:1])
        grad_low = grad.astype(BF)
        gproj_ref[...] += dot_tn(mix_ref[col], grad_low)
        dmix = dot_nt(grad_low, wproj[...]).astype(BF)
        parts = []
        for w in range(2):
            part = pack_ref[col, WIN * w : WIN * w + WIN]
            dq, dk, dv = attention_backward(
                part[:, 0:C],
                part[:, C : 2 * C],
                part[:, 2 * C :],
                lse_ref[col, w : w + 1],
                dmix[WIN * w : WIN * w + WIN],
                masks,
                masks32,
                False,
            )
            parts.append(jnp.concatenate([dq.astype(BF), dk.astype(BF), dv.astype(BF)], axis=1))
        dpacked = jnp.concatenate(parts, axis=0)
        xhat, rstd = norm_stats(h0_ref[col])
        normed = (xhat * norm_ref[0, 0:1] + norm_ref[0, 1:2]).astype(BF)
        gqkv_ref[...] += dot_tn(normed, dpacked)
        dn = dot_nt(dpacked, wqkv[...])
        add_norm_grads(gnorm_ref, 0, dn, xhat)
        grad = grad + norm_back(dn, xhat, rstd, norm_ref[0, 0:1])
        gembed_ref[...] += dot_tn(an_ref[col], grad.astype(BF))
        glead_ref[lead_at, :] += jnp.sum(grad, axis=0, keepdims=True)


def whole(shape):
    zeros = (0,) * len(shape)
    return pl.BlockSpec(shape, lambda i: zeros)


def layer(shape, index):
    at = (index,) + (0,) * len(shape)
    return pl.BlockSpec((1,) + shape, lambda i: at)


def rows(columns, *shape):
    tail = (0,) * len(shape)
    return pl.BlockSpec((columns,) + shape, lambda i: (i,) + tail)


def rows_of(columns, offset, *shape):
    tail = (0,) * len(shape)
    return pl.BlockSpec((columns,) + shape, lambda i: (i + offset,) + tail)


SMEM = pl.BlockSpec(memory_space=pltpu.SMEM)


def struct(shape, dtype):
    return jax.ShapeDtypeStruct(shape, dtype)


def run_forward(lead_step, tokens, lead_table, embed_t, qkv_w, proj_w, up_w, down_t, norm_t, sample, count, columns):
    steps = count // columns
    outs = [
        ((count, COL, C), F32),
        ((count, COL, 3 * C), BF),
        ((count, 2, LANES), F32),
        ((count, COL, C), BF),
        ((count, COL, C), F32),
        ((count, COL, FF), BF),
        ((count, COL, FF), F32),
        ((count, COL, C), F32),
        ((count, HALF, C), BF),
        ((count, HALF, C), BF),
    ]

    def body(*refs):
        forward_zero(columns, *refs, sample=sample)

    return pl.pallas_call(
        body,
        grid=(steps,),
        in_specs=[
            SMEM,
            rows_of(columns, sample * steps, COL, CIN),
            whole((LEADS, C)),
            whole((C, CIN)),
            layer((C, 3 * C), 0),
            layer((C, C), 0),
            layer((C, FF), 0),
            layer((C, FF), 0),
            whole((5, 2, C)),
        ],
        out_specs=[rows(columns, *shape[1:]) for shape, _ in outs],
        out_shape=[struct(*o) for o in outs],
        scratch_shapes=[
            pltpu.VMEM((C, CIN), BF),
            pltpu.VMEM((C, 3 * C), BF),
            pltpu.VMEM((C, C), BF),
            pltpu.VMEM((C, FF), BF),
            pltpu.VMEM((C, FF), BF),
        ],
        compiler_params=pltpu.CompilerParams(vmem_limit_bytes=VMEM_BYTES),
        name="forward_zero",
    )(lead_step, tokens, lead_table, embed_t, qkv_w, proj_w, up_w, down_t, norm_t)


MIDDLE_SUMS = [
    ((C, 3 * C), F32),
    ((C, C), F32),
    ((C, FF), F32),
    ((C, FF), F32),
    ((C, CIN), F32),
    ((8, C), F32),
    ((8, CIN), F32),
    ((8, CIN), F32),
]


def run_middle(flags, h1, up_in, down_in, target, cells, qkv_w, proj_w, up_w, down_t, decode_w, norm_t, scale, prev, sample, count, columns):
    steps = count // columns
    outs = [
        ((count, COL, C), F32),
        ((count, COL, C), F32),
        ((count, HALF, C), BF),
        ((count, HALF, C), BF),
    ]
    first = prev is None
    return pl.pallas_call(
        partial(middle, columns, first=first),
        grid=(steps,),
        in_specs=[
            SMEM,
            rows(columns, COL, C),
            rows(columns, HALF, C),
            rows(columns, HALF, C),
            rows_of(columns, sample * steps, COL, CIN),
            rows_of(columns, sample * steps, 8, COL),
            layer((C, 3 * C), 1),
            layer((C, C), 1),
            layer((C, FF), 1),
            layer((C, FF), 1),
            whole((C, CIN)),
            whole((5, 2, C)),
            whole((1, CIN)),
        ]
        + ([] if first else [whole(shape) for shape, _ in MIDDLE_SUMS]),
        out_specs=[rows(columns, *shape[1:]) for shape, _ in outs] + [whole(shape) for shape, _ in MIDDLE_SUMS],
        out_shape=[struct(*o) for o in outs + MIDDLE_SUMS],
        scratch_shapes=[
            pltpu.VMEM((C, 3 * C), BF),
            pltpu.VMEM((C, C), BF),
            pltpu.VMEM((C, FF), BF),
            pltpu.VMEM((C, FF), BF),
            pltpu.VMEM((C, CIN), BF),
        ],
        compiler_params=pltpu.CompilerParams(vmem_limit_bytes=VMEM_BYTES),
        name="middle",
    )(flags, h1, up_in, down_in, target, cells, qkv_w, proj_w, up_w, down_t, decode_w, norm_t, scale, *(prev or ()))


BACK_SUMS = [
    ((CIN, C), F32),
    ((LEADS, C), F32),
    ((C, 3 * C), F32),
    ((C, C), F32),
    ((C, FF), F32),
    ((C, FF), F32),
    ((8, C), F32),
]


def run_backward(lead_step, tokens, saved, dh2, dn, ret_top, ret_bot, qkv_w, proj_w, up_w, down_t, norm_t, prev, sample, count, columns):
    steps = count // columns
    first = prev is None
    return pl.pallas_call(
        partial(backward_zero, columns, first=first, sample=sample),
        grid=(steps,),
        in_specs=[
            SMEM,
            rows_of(columns, sample * steps, COL, CIN),
            rows(columns, COL, C),
            rows(columns, COL, 3 * C),
            rows(columns, 2, LANES),
            rows(columns, COL, C),
            rows(columns, COL, C),
            rows(columns, COL, FF),
            rows(columns, COL, FF),
            rows(columns, COL, C),
            rows(columns, COL, C),
            rows(columns, COL, C),
            rows(columns, HALF, C),
            rows(columns, HALF, C),
            layer((C, 3 * C), 0),
            layer((C, C), 0),
            layer((C, FF), 0),
            layer((C, FF), 0),
            whole((5, 2, C)),
        ]
        + ([] if first else [whole(shape) for shape, _ in BACK_SUMS]),
        out_specs=[whole(shape) for shape, _ in BACK_SUMS],
        out_shape=[struct(*o) for o in BACK_SUMS],
        scratch_shapes=[
            pltpu.VMEM((C, 3 * C), BF),
            pltpu.VMEM((C, C), BF),
            pltpu.VMEM((C, FF), BF),
            pltpu.VMEM((C, FF), BF),
        ],
        compiler_params=pltpu.CompilerParams(vmem_limit_bytes=VMEM_BYTES),
        name="backward_zero",
    )(lead_step, tokens, *saved, dh2, dn, ret_top, ret_bot, qkv_w, proj_w, up_w, down_t, norm_t, *(prev or ()))


def apply_update(weights, gradients, firsts, seconds, cell_count):
    scaled = [member / cell_count for member in gradients]
    grad_norm = jnp.sqrt(sum((jnp.sum(member * member) for member in scaled)))
    factor = jnp.minimum(1.0, clip_max / grad_norm)
    news, moments, squares = ([], [], [])
    for weight, member, first, second, rate, shrink in zip(
        weights, scaled, firsts, seconds, rate_table, decay_table
    ):
        clipped = member * factor
        first = beta_one * first + (1.0 - beta_one) * clipped
        second = beta_two * second + (1.0 - beta_two) * clipped * clipped
        first_hat = first / (1.0 - beta_one**STEP)
        second_hat = second / (1.0 - beta_two**STEP)
        news.append(
            weight - rate * (first_hat / (jnp.sqrt(second_hat) + adam_eps) + shrink * weight)
        )
        moments.append(first)
        squares.append(second)
    return (news, moments, squares, grad_norm)


def neighbours(low, high):
    count = lax.axis_size("lat")
    forward = [(i, i + 1) for i in range(count - 1)]
    backward = [(b, a) for a, b in forward]
    return lax.ppermute(high, "lat", forward), lax.ppermute(low, "lat", backward)


def on_device(analysis, target, lead_step, loss_mask, *state):
    weights, firsts, seconds = state[0:9], state[9:18], state[18:27]
    embed_w, lead_table, qkv_w, proj_w, up_w, down_w, decode_w, norm_params, loss_scale = weights
    samples, blocks = analysis.shape[0], analysis.shape[1]
    tokens = analysis.transpose(0, 1, 2, 4, 3, 5).reshape(samples * blocks, COL, CIN)
    truth = target.transpose(0, 1, 2, 4, 3, 5).reshape(samples * blocks, COL, CIN)
    cells = loss_mask.transpose(0, 1, 2, 4, 3).reshape(samples * blocks, 1, COL).astype(BF)
    cells = jnp.pad(cells, ((0, 0), (0, 7), (0, 0)))
    embed_t = embed_w.T
    down_t = down_w.transpose(0, 2, 1)
    norm_t = norm_params.transpose(1, 0, 2)
    scale = loss_scale[None, :]
    at = lax.axis_index("lat")
    flags = jnp.stack(
        [jnp.where(at > 0, 0.0, -1e30), jnp.where(at < lax.axis_size("lat") - 1, 0.0, -1e30)]
    ).astype(F32)

    forward = [
        run_forward(lead_step, tokens, lead_table, embed_t, qkv_w, proj_w, up_w, down_t, norm_t, s, blocks, 1)
        for s in range(samples)
    ]
    edges = [neighbours(f[8], f[9]) for f in forward]
    sums = None
    mids = []
    for s in range(samples):
        up_in, down_in = edges[s]
        out = run_middle(
            flags, forward[s][7], up_in, down_in, truth, cells, qkv_w, proj_w, up_w, down_t, decode_w, norm_t, scale,
            sums, s, blocks, 1,
        )
        sums = out[4:]
        mids.append(out[:4])
    returned = [neighbours(m[2], m[3]) for m in mids]
    back = None
    for s in range(samples):
        ret_top, ret_bot = returned[s]
        back = run_backward(
            lead_step, tokens, forward[s][:8], mids[s][0], mids[s][1], ret_top, ret_bot,
            qkv_w, proj_w, up_w, down_t, norm_t, back, s, blocks, 1,
        )
    sums, back = lax.psum((sums, back), ("lat", "batch"))
    g_qkv1, g_proj1, g_up1, g_down1, g_dec, g_norm1, g_scale, count = sums
    g_embed, g_lead, g_qkv0, g_proj0, g_up0, g_down0, g_norm0 = back
    g_scale = g_scale[0]
    cell_total = count[0, 0]
    cell_count = cell_total * CIN
    loss_sum = jnp.sum((cell_total - g_scale) + loss_scale * cell_total)
    g_norm = jnp.stack(
        [g_norm0[0:2], g_norm0[2:4], g_norm0[4:6], g_norm1[2:4], g_norm1[4:6]], axis=1
    )
    gradients = (
        g_embed,
        g_lead,
        jnp.stack([g_qkv0, g_qkv1]),
        jnp.stack([g_proj0, g_proj1]),
        jnp.stack([g_up0, g_up1]),
        jnp.stack([g_down0, g_down1]).transpose(0, 2, 1),
        g_dec,
        g_norm,
        g_scale,
    )
    news, moments, squares, grad_norm = apply_update(weights, gradients, firsts, seconds, cell_count)
    return (*news, *moments, *squares, loss_sum, cell_count, grad_norm)


def solution(mesh):
    split = P("batch", None, "lat", None, None, None)
    placed = (split, split, P("batch"), P("batch", None, "lat", None, None)) + (P(),) * 27
    return jax.shard_map(
        on_device, mesh=mesh, in_specs=placed, out_specs=(P(),) * 30, check_vma=False
    )
```

time: 1840 us -> 561 us (0.30)
  local copies, waits for them, and re-layouts: 694 us -> 14.4 us
  matrix products: 581 us -> 0 us
  Pallas kernels: 0 us -> 322 us
  other arithmetic: 338 us -> 29 us
  waiting for transfers between devices: 131 us -> 101 us
    dot_general x42 -> x0, matrix products: 574 us -> none  [the longest x2 90.1 us: backward_block(): jnp.einsum('wqhd,wkhd->whqk', d_mixture, value_rows, preferred_element_ty...]
    pallas_call x0 -> x6, Pallas kernels: none -> 322 us  [the longest x2 154 us: run_middle(): pl.pallas_call(partial(middle, columns, first=first), grid=(steps,), in_s...]
    convert_element_type x12 -> x3, local copies, waits for them, and re-layouts: 247 us -> 0.66 us  [on_device(): loss_mask.transpose(0, 1, 2, 4, 3).reshape(samples * blocks, 1, COL)]
    another operation x12 -> x1, local copies, waits for them, and re-layouts: 199 us -> 0.01 us  [on_device(): jnp.stack([g_norm0[0:2], g_norm0[2:4], g_norm0[4:6], g_norm1[2:4], g_norm...]
    convert_element_type x14 -> x1, other arithmetic: 131 us -> 0.1 us  [on_device(): loss_mask.transpose(0, 1, 2, 4, 3).reshape(samples * blocks, 1, COL)]
    reduce_sum x15 -> x0, other arithmetic: 113 us -> none  [the longest x2 41.1 us: forward_block(): totals = jnp.sum(expo, axis=-1, keepdims=True)]
    dot_general x6 -> x0, local copies, waits for them, and re-layouts: 112 us -> none  [the longest x2 42.8 us: forward_block(): output = jnp.dot(mixture, w_proj, preferred_element_type=jnp.float32)]
    reshape x6 -> x0, local copies, waits for them, and re-layouts: 52.9 us -> none  [the longest x2 21.7 us: backward_block(): d_mixture = d_mixture.reshape(count_w, width, HEADS, -1)]
  transfers between devices with their start and end apart: 5 -> 9, of which waited for: 4 -> 1; matrix products, arithmetic and copies ran while one was open for 2% -> 1% of each run, Pallas kernels for 0% -> 42%
where the time goes in v1:
time: 561 us; the launch traced here: 560 us
  Pallas kernels  322 us (57%)
  waiting for transfers between devices  101 us (18%)
  blocking collectives  44.1 us (8%)
  other arithmetic  29 us (5%)
  starting transfers between devices  25.4 us (5%)
  between operations  23.6 us (4%)
  local copies, waits for them, and re-layouts  14.4 us (3%)
    pallas_call x2, Pallas kernels, run_middle(): pl.pallas_call(partial(middle, columns, first=first), grid=(steps,), in_s...  154 us
    psum x1, waiting for transfers between devices, on_device(): sums, back = lax.psum((sums, back), ('lat', 'batch'))  101 us
    pallas_call x2, Pallas kernels, run_backward(): pl.pallas_call(partial(backward_zero, columns, first=first, sample=sample...  93.5 us
    pallas_call x2, Pallas kernels, run_forward(): pl.pallas_call(body, grid=(steps,), in_specs=[SMEM, rows_of(columns, samp...  74.6 us
    psum x1, blocking collectives, on_device(): sums, back = lax.psum((sums, back), ('lat', 'batch'))  44.1 us
    ppermute x4, starting transfers between devices, neighbours(): lax.ppermute(high, 'lat', forward)  19.9 us
    sub x9, other arithmetic, apply_update(): weight - rate * (first_hat / (jnp.sqrt(second_hat) + adam_eps) + shrink *...  17.3 us
    unnamed x104, local copies, waits for them, and re-layouts  12.6 us
  transfers between devices with their start and end apart: 9, of which 1 were waited for; matrix products, arithmetic and copies ran while one was open for 1% of the time, Pallas kernels for 42%

profile of v1, /device:TPU:0, one launch (start us, length us, event | category | flops | bytes accessed | tf_op | source)
XLA Modules:
  0.0 560.3 jit_solution(13699397508341362195)
XLA Ops:
  7.2 37.3 %forward_zero.3 = (f32[12,288,192]{2,1,0:T(8,128)}, bf16[12,288,576]{2,1,0:T(8,128)(2,1)}, f32[12,2,896]{2,1,0:T(2,128)}, bf16[12,288,192]{2,1,0:T(8,128)(2,1)},...) custom-call(s32[2]{0:T(128)} %step_ref.3, ...), custom_call_target="tpu_custom_call" | custom-call | tf_op jit(solution)/shard_map/forward_zero/pallas_call | solution.py:574
  44.5 4.9 collective-permute-start.2
  50.8 37.3 %forward_zero.2 = (f32[12,288,192]{2,1,0:T(8,128)}, bf16[12,288,576]{2,1,0:T(8,128)(2,1)}, f32[12,2,896]{2,1,0:T(2,128)}, bf16[12,288,192]{2,1,0:T(8,128)(2,1)},...) custom-call(s32[2]{0:T(128)} %step_ref.3, ...), custom_call_target="tpu_custom_call" | custom-call | tf_op jit(solution)/shard_map/forward_zero/pallas_call | solution.py:574
  88.1 4.6 collective-permute-start
  97.0 76.7 %middle.2 = (f32[12,288,192]{2,1,0:T(8,128)}, f32[12,288,192]{2,1,0:T(8,128)}, bf16[12,72,192]{2,1,0:T(8,128)(2,1)}, bf16[12,72,192]{2,1,0:T(8,128)(2,1)}, f32[1...) custom-call(f32[2]{0:T(128)} %pad_maximum_fusion.flag_ref, ...), custom_call_target="tpu_custom_call" | custom-call | tf_op jit(solution)/shard_map/middle/pallas_call | solution.py:623
  173.7 5.0 collective-permute-start.6
  181.1 77.7 %middle.3 = (f32[12,288,192]{2,1,0:T(8,128)}, f32[12,288,192]{2,1,0:T(8,128)}, bf16[12,72,192]{2,1,0:T(8,128)(2,1)}, bf16[12,72,192]{2,1,0:T(8,128)(2,1)}, f32[1...) custom-call(f32[2]{0:T(128)} %pad_maximum_fusion.flag_ref, ...), custom_call_target="tpu_custom_call" | custom-call | tf_op jit(solution)/shard_map/middle/pallas_call | solution.py:623
  258.8 5.5 collective-permute-start.4
  266.5 46.3 %backward_zero.2 = (f32[128,192]{1,0:T(8,128)}, f32[20,192]{1,0:T(8,128)}, f32[192,576]{1,0:T(8,128)}, f32[192,192]{1,0:T(8,128)}, f32[192,768]{1,0:T(8,128)}, /*index=5*/f32[192,768]{1,0:T(8,128)}, f32[8,192]{1,0:T(8,128)}) custom-call(s32[2]{0:T(128)} %step_ref.3, bf16[24,288,128]{2,1,0:T(8,128)(2,1)} %bitcast.71, ...), custom_call_target="tpu_custom_call" | custom-call | tf_op jit(solution)/shard_map/backward_zero/pallas_call | solution.py:670
  313.8 47.2 %backward_zero.3 = (f32[128,192]{1,0:T(8,128)}, f32[20,192]{1,0:T(8,128)}, f32[192,576]{1,0:T(8,128)}, f32[192,192]{1,0:T(8,128)}, f32[192,768]{1,0:T(8,128)}, /*index=5*/f32[192,768]{1,0:T(8,128)}, f32[8,192]{1,0:T(8,128)}) custom-call(s32[2]{0:T(128)} %step_ref.3, bf16[24,288,128]{2,1,0:T(8,128)(2,1)} %bitcast.72, ...), custom_call_target="tpu_custom_call" | custom-call | tf_op jit(solution)/shard_map/backward_zero/pallas_call | solution.py:670
  364.2 44.1 %all-reduce.1 = (f32[8,128]{1,0:T(8,128)S(1)}, f32[20,192]{1,0:T(8,128)S(1)}, f32[8,192]{1,0:T(8,128)S(1)}, f32[8,192]{1,0:T(8,128)S(1)}, f32[8,128]{1,0:T(8,128)S(1)}) all-reduce(f32[8,128]{1,0:T(8,128)S(1)} %copy-done.43, f32[20,192]{1,0:T(8,128)S(1)} %copy-done.34, ...), channel_id=1, replica_groups=mesh['lat'=8,'batch'=4] {'lat','batch'}, use_global_device_ids=true, to_apply=%region_1.2 | all-reduce | flops 8960 | bytes 71680 | tf_op jit(solution)/shard_map/psum | solution.py:776
  411.5 101.1 %all-reduce.5.cloned.1.call-done = (f32[128,192]{1,0:T(8,128)}, f32[1,192,576]{2,1,0:T(8,128)}, f32[1,192,576]{2,1,0:T(8,128)}, f32[1,192,192]{2,1,0:T(8,128)}, ...) async-done(((f32[128,192]{1,0:T(8,128)}, ...) | async-done | bytes 3735568 | tf_op jit(solution)/shard_map/psum | solution.py:776
  515.8 1.7 multiply_reduce_fusion.3
  517.5 2.0 multiply_reduce_fusion.2
  522.2 2.2 multiply_reduce_fusion
  527.9 1.9 multiply_subtract_fusion.4
  529.8 1.6 copy.75
  531.4 1.6 copy.76
  533.0 1.6 copy.77
  534.7 1.8 multiply_subtract_fusion.5
  536.5 4.2 multiply_subtract_fusion
  540.8 2.4 multiply_subtract_fusion.1
  545.2 2.1 multiply_subtract_fusion.2
  548.0 2.5 add_subtract_fusion.2
  (131 shorter events, 23.3 us)
Async XLA Ops:
  7.2 505.4 %all-reduce.5.cloned.1.call-start = ((), (), s32[]{:S(2)}) async-start(), calls=%async_computation | async-start | bytes 7929856 | tf_op jit(solution)/shard_map/psum | solution.py:776
  44.5 51.6 %collective-permute-start.2 = (bf16[12,72,192]{2,1,0:T(8,128)(2,1)}, bf16[12,72,192]{2,1,0:T(8,128)(2,1)S(1)}, u32[]{:S(2)}, u32[]{:S(2)}) collective-permute-start(bf16[12,72,192]{2,1,0:T(8,128)(2,1)} %get-tuple-element.99), channel_id=1, source_target_pairs={{0,4},{4,8},{8,12},{12,16},{16,20},{20,24},{24,28},{1,5},{5,9},{9,... | collective-permute-start | bytes 995336 | tf_op jit(solution)/shard_map/ppermute | solution.py:733
  49.4 44.7 %copy-start.28 = (s32[2,12,12,2,12]{4,3,2,1,0:T(2,128)S(1)}, s32[2,12,12,2,12]{4,3,2,1,0:T(2,128)}, u32[]{:S(2)}) copy-start(s32[2,12,12,2,12]{4,3,2,1,0:T(2,128)} %param.34) | copy-start | bytes 82948
  49.4 46.7 %collective-permute-start.3 = (bf16[12,72,192]{2,1,0:T(8,128)(2,1)}, bf16[12,72,192]{2,1,0:T(8,128)(2,1)S(1)}, u32[]{:S(2)}, u32[]{:S(2)}) collective-permute-start(bf16[12,72,192]{2,1,0:T(8,128)(2,1)} %get-tuple-element.100), channel_id=1, source_target_pairs={{4,0},{8,4},{12,8},{16,12},{20,16},{24,20},{28,24},{5,1},{9,5},{13... | collective-permute-start | bytes 995336 | tf_op jit(solution)/shard_map/ppermute | solution.py:733
  88.1 92.1 %collective-permute-start = (bf16[12,72,192]{2,1,0:T(8,128)(2,1)}, bf16[12,72,192]{2,1,0:T(8,128)(2,1)S(1)}, u32[]{:S(2)}, u32[]{:S(2)}) collective-permute-start(bf16[12,72,192]{2,1,0:T(8,128)(2,1)} %get-tuple-element.96), channel_id=1, source_target_pairs={{0,4},{4,8},{8,12},{12,16},{16,20},{20,24},{24,28},{1,5},{5,9},{9,... | collective-permute-start | bytes 995336 | tf_op jit(solution)/shard_map/ppermute | solution.py:733
  92.7 87.5 %collective-permute-start.1 = (bf16[12,72,192]{2,1,0:T(8,128)(2,1)}, bf16[12,72,192]{2,1,0:T(8,128)(2,1)S(1)}, u32[]{:S(2)}, u32[]{:S(2)}) collective-permute-start(bf16[12,72,192]{2,1,0:T(8,128)(2,1)} %get-tuple-element.97), channel_id=1, source_target_pairs={{4,0},{8,4},{12,8},{16,12},{20,16},{24,20},{28,24},{5,1},{9,5},{13... | collective-permute-start | bytes 995336 | tf_op jit(solution)/shard_map/ppermute | solution.py:733
  173.7 91.9 %collective-permute-start.6 = (bf16[12,72,192]{2,1,0:T(8,128)(2,1)}, bf16[12,72,192]{2,1,0:T(8,128)(2,1)S(1)}, u32[]{:S(2)}, u32[]{:S(2)}) collective-permute-start(bf16[12,72,192]{2,1,0:T(8,128)(2,1)} %get-tuple-element.122), channel_id=1, source_target_pairs={{0,4},{4,8},{8,12},{12,16},{16,20},{20,24},{24,28},{1,5},{5,9},{9,... | collective-permute-start | bytes 995336 | tf_op jit(solution)/shard_map/ppermute | solution.py:733
  178.7 86.9 %collective-permute-start.7 = (bf16[12,72,192]{2,1,0:T(8,128)(2,1)}, bf16[12,72,192]{2,1,0:T(8,128)(2,1)S(1)}, u32[]{:S(2)}, u32[]{:S(2)}) collective-permute-start(bf16[12,72,192]{2,1,0:T(8,128)(2,1)} %get-tuple-element.123), channel_id=1, source_target_pairs={{4,0},{8,4},{12,8},{16,12},{20,16},{24,20},{28,24},{5,1},{9,5},{13... | collective-permute-start | bytes 995336 | tf_op jit(solution)/shard_map/ppermute | solution.py:733
  258.8 54.0 %collective-permute-start.4 = (bf16[12,72,192]{2,1,0:T(8,128)(2,1)}, bf16[12,72,192]{2,1,0:T(8,128)(2,1)S(1)}, u32[]{:S(2)}, u32[]{:S(2)}) collective-permute-start(bf16[12,72,192]{2,1,0:T(8,128)(2,1)} %get-tuple-element.111), channel_id=1, source_target_pairs={{0,4},{4,8},{8,12},{12,16},{16,20},{20,24},{24,28},{1,5},{5,9},{9,... | collective-permute-start | bytes 995336 | tf_op jit(solution)/shard_map/ppermute | solution.py:733
  264.3 48.6 %collective-permute-start.5 = (bf16[12,72,192]{2,1,0:T(8,128)(2,1)}, bf16[12,72,192]{2,1,0:T(8,128)(2,1)S(1)}, u32[]{:S(2)}, u32[]{:S(2)}) collective-permute-start(bf16[12,72,192]{2,1,0:T(8,128)(2,1)} %get-tuple-element.112), channel_id=1, source_target_pairs={{4,0},{8,4},{12,8},{16,12},{20,16},{24,20},{28,24},{5,1},{9,5},{13... | collective-permute-start | bytes 995336 | tf_op jit(solution)/shard_map/ppermute | solution.py:733
  361.1 3.1 copy-start.34
  512.6 9.5 %copy-start.4 = (f32[1,192,768]{2,1,0:T(8,128)S(1)}, f32[1,192,768]{2,1,0:T(8,128)}, u32[]{:S(2)}) copy-start(f32[1,192,768]{2,1,0:T(8,128)} %get-tuple-element.216) | copy-start | bytes 1769476
  512.6 9.6 %copy-start.5 = (f32[1,192,768]{2,1,0:T(8,128)S(1)}, f32[1,192,768]{2,1,0:T(8,128)}, u32[]{:S(2)}) copy-start(f32[1,192,768]{2,1,0:T(8,128)} %get-tuple-element.217) | copy-start | bytes 1769476
  522.2 14.3 %copy-start.7 = (f32[1,192,768]{2,1,0:T(8,128)S(1)}, f32[1,192,768]{2,1,0:T(8,128)}, u32[]{:S(2)}) copy-start(f32[1,192,768]{2,1,0:T(8,128)} %get-tuple-element.219) | copy-start | bytes 1769476
  524.4 12.1 %copy-start = (f32[2,768,192]{1,2,0:T(8,128)S(1)}, f32[2,768,192]{1,2,0:T(8,128)}, u32[]{:S(2)}) copy-start(f32[2,768,192]{1,2,0:T(8,128)} %param.40) | copy-start | bytes 3538948
  524.4 12.1 %copy-start.6 = (f32[1,192,768]{2,1,0:T(8,128)S(1)}, f32[1,192,768]{2,1,0:T(8,128)}, u32[]{:S(2)}) copy-start(f32[1,192,768]{2,1,0:T(8,128)} %get-tuple-element.218) | copy-start | bytes 1769476
  536.5 4.2 copy-start.1
  536.5 4.2 copy-start.10
  536.5 4.2 copy-start.11
  540.7 3.7 copy-start.12
  540.8 3.7 copy-start.13
  545.2 5.3 copy-start.17
  545.2 5.3 copy-start.37
  545.2 5.3 copy-start.38
  (32 other events, 64.4 us)
Sparse Core Ops, SparseCore 0:
  361.3 151.2 all-reduce.4

commit v2 on v1

v2 whole, which is shorter than its diff:
```python
from functools import partial
import math

import jax
import jax.numpy as jnp
from jax import lax
from jax.experimental import pallas as pl
from jax.experimental.pallas import tpu as pltpu
from jax.sharding import PartitionSpec as P

HEADS = 6
LEADS = 20
STEP = 10
C = 192
FF = 768
CIN = 128
HDIM = 32
COL = 288
WIN = 144
HALF = 72
LANES = 896
TAIL = COL - 256
KV = 3 * WIN
SCALE = HDIM ** (-0.5)
SCALE2 = SCALE * math.log2(math.e)
BF = jnp.bfloat16
F32 = jnp.float32

beta_one = 0.9
beta_two = 0.999
adam_eps = 1e-08
clip_max = 0.005
rate_table = (0.2, 1.0, 0.2, 0.2, 0.2, 0.2, 0.2, 1.0, 1.0)
decay_table = (0.1, 0.1, 0.1, 0.1, 0.1, 0.1, 0.1, 0.0, 0.0)

VMEM_BYTES = 56 * 1024 * 1024
OFFSET = 1


def dot(a, b):
    return lax.dot_general(a, b, (((1,), (0,)), ((), ())), preferred_element_type=F32)


def dot_nt(a, b):
    return lax.dot_general(a, b, (((1,), (1,)), ((), ())), preferred_element_type=F32)


def dot_tn(a, b):
    return lax.dot_general(a, b, (((0,), (0,)), ((), ())), preferred_element_type=F32)


def drive(parts, offset):
    live = [(at * offset, part) for at, part in enumerate(parts)]
    tick = 0
    while live:
        left = []
        for start, part in live:
            if tick >= start and next(part, 0) == 0:
                continue
            left.append((start, part))
        live = left
        tick += 1


def norm_stats(x):
    center = x - jnp.mean(x, axis=-1, keepdims=True)
    rstd = lax.rsqrt(jnp.mean(center * center, axis=-1, keepdims=True) + 1e-05)
    return center * rstd, rstd


def norm_back(dy, xhat, rstd, gain):
    dxhat = dy * gain
    first = jnp.mean(dxhat, axis=-1, keepdims=True)
    second = jnp.mean(dxhat * xhat, axis=-1, keepdims=True)
    return rstd * (dxhat - first - xhat * second)


def add_norm_grads(acc_ref, index, dy, xhat):
    acc_ref[2 * index : 2 * index + 1] += jnp.sum(dy * xhat, axis=0, keepdims=True)
    acc_ref[2 * index + 1 : 2 * index + 2] += jnp.sum(dy, axis=0, keepdims=True)


def gelu_both(x):
    c0 = math.sqrt(2.0 / math.pi)
    c1 = c0 * 0.044715
    square = x * x
    slope = jnp.tanh(x * (c0 + c1 * square))
    half = 0.5 + 0.5 * slope
    active = x * half
    return active, half + active * ((1.0 - slope) * (c0 + (3.0 * c1) * square))


def head_masks():
    lane = lax.broadcasted_iota(jnp.int32, (1, C), 1) // HDIM
    return [(lane == h).astype(F32).astype(BF) for h in range(HEADS)]


def expand(x, masks, edge):
    rem = [x[128:144] * masks[h] for h in range(HEADS)] + [jnp.zeros((32, C), BF)]
    if edge:
        low = [x[0:64] * masks[h] for h in range(HEADS)]
        high = [x[64:128] * masks[h] for h in (4, 5, 0, 1, 2, 3)]
        return jnp.concatenate(low + rem + high, axis=0)
    return jnp.concatenate([x[0:128] * masks[h] for h in range(HEADS)] + rem, axis=0)


def low_lanes():
    return lax.broadcasted_iota(jnp.int32, (1, 128), 1) % 16 < 8


CHUNKS = ((0, 256), (256, 512), (512, 768), (768, 896))
EDGE_CHUNKS = ((0, 256), (256, 640), (640, 896))


def chunks_of(edge):
    return EDGE_CHUNKS if edge else CHUNKS


def add_bias(scores, bias):
    return jnp.concatenate([scores[0:HALF] + bias, scores[HALF:]], axis=0)


def score_chunk(keys, expanded, edge, at, bias=None):
    a, b = chunks_of(edge)[at]
    if not edge:
        return dot_nt(keys, expanded[a:b])
    if at != 1:
        out = dot_nt(keys[at // 2], expanded[a:b])
        return out if bias is None else add_bias(out, bias[at // 2])
    low = dot_nt(keys[0], expanded[256:512])
    high = dot_nt(keys[1], expanded[384:640])
    rem = jnp.where(low_lanes(), low[:, 128:256], high[:, 0:128])
    low, high = low[:, 0:128], high[:, 128:256]
    if bias is not None:
        low, high = add_bias(low, bias[0]), add_bias(high, bias[1])
        rem = add_bias(rem, jnp.where(low_lanes(), bias[0], bias[1]))
    return jnp.concatenate([low, rem, high], axis=1)


def query_chunk(vals_t, weights, edge, at):
    if not edge:
        return dot(vals_t[64 * at : 64 * at + 64] if at < 3 else vals_t, weights)
    if at != 1:
        return dot(vals_t[at // 2][0:128], weights)
    return dot(vals_t[0], weights[:, 0:256]), dot(vals_t[1], weights[:, 128:384])


def query_gather(parts, masks32, edge):
    if not edge:
        blocks = []
        for both in parts[:3]:
            blocks += [both[0:32, 0:128], both[32:64, 128:256]]
        rem = parts[3]
    else:
        low_a, (low_b, high_b), high_a = parts
        rem = jnp.where(low_lanes(), low_b[:, 128:256], high_b[:, 0:128])
        low_b, high_b = low_b[128:192, 0:128], high_b[128:192, 128:256]
        left = lax.broadcasted_iota(jnp.int32, (1, 128), 1) < 64
        blocks = []
        for h in range(HEADS):
            src_low, src_high, local = (low_a, high_a, h) if h < 4 else (low_b, high_b, h - 4)
            group = slice(128 * (local // 2), 128 * (local // 2) + 128)
            low = src_low[32 * local : 32 * local + 32, group]
            high = src_high[32 * local : 32 * local + 32, group]
            if h % 2:
                low = pltpu.roll(low, 64, 1)
            else:
                high = pltpu.roll(high, 64, 1)
            blocks.append(jnp.where(left, low, high))
    main = jnp.concatenate(blocks, axis=0).T
    back = rem.T
    total = back[0:16] * masks32[0]
    for h in range(1, HEADS):
        total = total + back[16 * h : 16 * h + 16] * masks32[h]
    return jnp.concatenate([main, total], axis=0)


def key_side(weights, expanded, edge):
    if not edge:
        return dot(jnp.concatenate(weights, axis=1), expanded)
    mask = low_lanes()
    rem = weights[1][:, 128:256]
    zero = jnp.zeros((), rem.dtype)
    low = jnp.concatenate([weights[0], weights[1][:, 0:128], jnp.where(mask, rem, zero)], axis=1)
    high = jnp.concatenate([jnp.where(mask, zero, rem), weights[1][:, 256:384], weights[2]], axis=1)
    return dot(low, expanded[0:512]), dot(high, expanded[384:896])


def attention_forward(q, k, vals, masks, masks32, edge, probs_ref, result, bias=None):
    queries = expand(q, masks, edge)
    vals_t = (vals[0].T, vals[1].T) if edge else vals.T
    spans = chunks_of(edge)
    ahead = score_chunk(k, queries, edge, 0, bias)
    yield 1
    parts = []
    for at, (a, b) in enumerate(spans):
        scores = ahead * SCALE2
        if at + 1 < len(spans):
            ahead = score_chunk(k, queries, edge, at + 1, bias)
        expo = jnp.exp2(scores - jnp.max(scores, axis=0, keepdims=True))
        probs = expo * (1.0 / jnp.sum(expo, axis=0, keepdims=True))
        probs_ref[:, a:b] = probs
        yield 1
        parts.append(query_chunk(vals_t, probs.astype(BF), edge, at))
        yield 1
    result.append(query_gather(parts, masks32, edge))


def attention_backward(q, k, vals, probs_ref, dmix, masks, masks32, edge, result):
    queries = expand(q, masks, edge)
    douts = expand(dmix, masks, edge)
    k_t = (k[0].T, k[1].T) if edge else k.T
    spans = chunks_of(edge)
    ahead = score_chunk(vals, douts, edge, 0)
    yield 1
    parts, lows, dlows = [], [], []
    for at, (a, b) in enumerate(spans):
        dprobs = ahead
        if at + 1 < len(spans):
            ahead = score_chunk(vals, douts, edge, at + 1)
        probs = probs_ref[:, a:b]
        row_terms = jnp.sum(dprobs * probs, axis=0, keepdims=True)
        dscores = (probs * (dprobs - row_terms)).astype(BF)
        lows.append(probs.astype(BF))
        dlows.append(dscores)
        yield 1
        parts.append(query_chunk(k_t, dscores, edge, at))
        yield 1
    dvals = key_side(lows, douts, edge)
    yield 1
    dkeys = key_side(dlows, queries, edge)
    yield 1
    dq = query_gather(parts, masks32, edge) * SCALE
    dkeys = (dkeys[0] * SCALE, dkeys[1] * SCALE) if edge else dkeys * SCALE
    result.extend([dq, dkeys, dvals])


def store_wide(out_ref, row, acc_ref, width):
    for j in range(width // 128):
        out_ref[row + C * j : row + C * j + C] = acc_ref[:, 128 * j : 128 * j + 128]


def store_qkv_proj(out_ref, row, qkv_ref, proj_ref):
    store_wide(out_ref, row, qkv_ref, 512)
    out_ref[row + 4 * C : row + 5 * C] = jnp.concatenate([qkv_ref[:, 512:576], proj_ref[:, 128:192]], axis=1)
    out_ref[row + 5 * C : row + 6 * C] = proj_ref[:, 0:128]


def clear_from(out_ref, row):
    if out_ref.shape[0] > row:
        out_ref[row:] = jnp.zeros((out_ref.shape[0] - row, 128), F32)


def store_narrow(out_ref, row, acc_ref, rows):
    out_ref[row : row + rows] = acc_ref[:, 0:128]
    out_ref[row + rows : row + 2 * rows] = jnp.concatenate(
        [acc_ref[:, 128:192], jnp.zeros((rows, 64), F32)], axis=1
    )


FLAT_MIDDLE = 19 * C + 24
FLAT_ZERO = 19 * C + 64


def forward_zero(
    columns,
    sample,
    step_ref,
    an_ref,
    lead_ref,
    embed_ref,
    qkv_ref,
    proj_ref,
    up_ref,
    down_ref,
    norm_ref,
    x0_ref,
    r0_ref,
    pack_ref,
    probs_ref,
    mix_ref,
    x1_ref,
    r1_ref,
    act_ref,
    slope_ref,
    h1_ref,
    top_ref,
    bot_ref,
    wembed,
    wqkv,
    wproj,
    wup,
    wdown,
):
    @pl.when(pl.program_id(0) == 0)
    def _():
        wembed[...] = embed_ref[...].astype(BF)
        wqkv[...] = qkv_ref[0].astype(BF)
        wproj[...] = proj_ref[0].astype(BF)
        wup[...] = up_ref[0].astype(BF)
        wdown[...] = down_ref[0].astype(BF)

    masks = head_masks()
    masks32 = [m.astype(F32) for m in masks]
    lead_row = lead_ref[pl.ds(step_ref[sample] - 1, 1), :]

    def one(col):
        hidden = dot_nt(an_ref[col], wembed[...]) + lead_row
        yield 1
        xhat, rstd = norm_stats(hidden)
        x0_ref[col] = xhat
        r0_ref[col] = rstd
        normed = (xhat * norm_ref[0, 0:1] + norm_ref[0, 1:2]).astype(BF)
        yield 1
        packed = dot(normed, wqkv[...]).astype(BF)
        pack_ref[col] = packed
        yield 1
        mixtures = []
        for w in range(2):
            part = packed[WIN * w : WIN * w + WIN]
            yield from attention_forward(
                part[:, 0:C], part[:, C : 2 * C], part[:, 2 * C :], masks, masks32, False, probs_ref.at[col, w], mixtures
            )
        mixture = jnp.concatenate(mixtures, axis=0).astype(BF)
        mix_ref[col] = mixture
        yield 1
        hidden_two = hidden + dot(mixture, wproj[...])
        yield 1
        xhat, rstd = norm_stats(hidden_two)
        x1_ref[col] = xhat
        r1_ref[col] = rstd
        normed_two = (xhat * norm_ref[1, 0:1] + norm_ref[1, 1:2]).astype(BF)
        yield 1
        yield from feed_forward(normed_two, wup, act_ref.at[col], slope_ref.at[col])
        hidden_one = hidden_two + dot_nt(act_ref[col], wdown[...])
        h1_ref[col] = hidden_one
        yield 1
        xhat, _ = norm_stats(jnp.concatenate([hidden_one[0:HALF], hidden_one[COL - HALF :]], axis=0))
        normed = xhat * norm_ref[2, 0:1] + norm_ref[2, 1:2]
        top_ref[col] = normed[0:HALF].astype(BF)
        bot_ref[col] = normed[HALF:].astype(BF)

    drive([one(col) for col in range(columns)], OFFSET)


def feed_forward(normed_two, wup, act_ref, slope_ref):
    ahead = dot(normed_two, wup[:, 0:256])
    yield 1
    for c in range(3):
        span = slice(256 * c, 256 * c + 256)
        inner = ahead
        if c < 2:
            ahead = dot(normed_two, wup[:, 256 * c + 256 : 256 * c + 512])
        active, slope = gelu_both(inner)
        act_ref[:, span] = active.astype(BF)
        slope_ref[:, span] = slope
        yield 1


def feed_backward(grad_low, wdown, act_ref, slope_ref, normed_two, gup_ref, gdown_ref, du_ref, keep):
    ahead = dot(grad_low, wdown[:, 0:256])
    yield 1
    for c in range(3):
        span = slice(256 * c, 256 * c + 256)
        dactive = ahead
        if c < 2:
            ahead = dot(grad_low, wdown[:, 256 * c + 256 : 256 * c + 512])
        dinner = (dactive * slope_ref[:, span]).astype(BF)
        du_ref[:, span] = dinner
        yield 1
        gdown_ref[:, span] += dot_tn(grad_low[0:256], act_ref[0:256, span])
        yield 1
        gup_ref[:, span] += dot_tn(normed_two[0:256], dinner[0:256])
        yield 1
    keep("act", act_ref[256:COL, :])
    keep("du", du_ref[256:COL, :])
    keep("dm", grad_low[256:COL])
    keep("n2", normed_two[256:COL])


MIDDLE_KEEP = (
    ("act", TAIL, FF),
    ("du", TAIL, FF),
    ("dm", TAIL, C),
    ("n2", TAIL, C),
    ("mix", TAIL, C),
    ("da", TAIL, C),
    ("n", TAIL, C),
    ("dq", TAIL, C),
    ("nkv", KV - 256, C),
    ("dkv", KV - 256, 2 * C),
    ("last", TAIL, C),
    ("dp", TAIL, CIN),
)


def edge_first(ref):
    return jnp.concatenate([ref[0:64], ref[216:280], ref[64:72], ref[280:288], ref[72:216]], axis=0)


def middle(columns, count, first, *refs):
    (
        flag_ref,
        h1_ref,
        up_in_ref,
        down_in_ref,
        target_ref,
        mask_ref,
        qkv_ref,
        proj_ref,
        up_ref,
        down_ref,
        decode_ref,
        norm_ref,
        scale_ref,
    ) = refs[:13]
    refs = refs[13:]
    if not first:
        prev_ref, refs = refs[0], refs[1:]
    (
        dh2_ref,
        dn_ref,
        x2_ref,
        r2_ref,
        dtop_ref,
        dbot_ref,
        flat_ref,
        wqkv,
        wproj,
        wup,
        wdown,
        wdec,
        probs_ref,
        act_ref,
        slope_ref,
        du_ref,
        gqkv_ref,
        gproj_ref,
        gup_ref,
        gdown_ref,
        gdec_ref,
        gnorm_ref,
        gscale_ref,
    ) = refs[:23]
    kept = {name: ref for (name, _, _), ref in zip(MIDDLE_KEEP, refs[23:])}
    sums = (gqkv_ref, gproj_ref, gup_ref, gdown_ref, gdec_ref, gnorm_ref, gscale_ref)
    step = pl.program_id(0)

    @pl.when(step == 0)
    def _():
        wqkv[...] = qkv_ref[0].astype(BF)
        wproj[...] = proj_ref[0].astype(BF)
        wup[...] = up_ref[0].astype(BF)
        wdown[...] = down_ref[0].astype(BF)
        wdec[...] = decode_ref[...].astype(BF)
        for ref in sums:
            ref[...] = jnp.zeros_like(ref)

    masks = head_masks()
    masks32 = [m.astype(F32) for m in masks]
    bias = (flag_ref[0], flag_ref[1])
    inverse = jnp.exp(-scale_ref[...])

    def one(col):
        def keep(name, value):
            rows = value.shape[0]
            at = pl.multiple_of((step * columns + col) * rows, 16)
            kept[name][pl.ds(at, rows), :] = value

        act, slope, du = act_ref.at[col], slope_ref.at[col], du_ref.at[col]
        h1 = edge_first(h1_ref[col])
        xhat_one, rstd_one = norm_stats(h1)
        normed = xhat_one * norm_ref[2, 0:1] + norm_ref[2, 1:2]
        normed_low = normed.astype(BF)
        n_top = jnp.concatenate([up_in_ref[col].astype(F32), normed[0:64], normed[128:136]], axis=0).astype(BF)
        n_bot = jnp.concatenate([down_in_ref[col].astype(F32), normed[64:128], normed[136:144]], axis=0).astype(BF)
        n_kv = jnp.concatenate([n_top, n_bot, normed_low[WIN:]], axis=0)
        yield 1
        keys_vals = dot(n_kv, wqkv[:, C:]).astype(BF)
        yield 1
        queries = dot(normed_low, wqkv[:, 0:C]).astype(BF)
        yield 1
        keys, vals = keys_vals[:, 0:C], keys_vals[:, C:]
        k_edge, v_edge = (keys[0:WIN], keys[WIN : 2 * WIN]), (vals[0:WIN], vals[WIN : 2 * WIN])
        k_mid, v_mid = keys[2 * WIN :], vals[2 * WIN :]
        mixtures = []
        yield from attention_forward(
            queries[0:WIN], k_edge, v_edge, masks, masks32, True, probs_ref.at[col, 0], mixtures, bias
        )
        yield from attention_forward(queries[WIN:], k_mid, v_mid, masks, masks32, False, probs_ref.at[col, 1], mixtures)
        mixture = jnp.concatenate(mixtures, axis=0).astype(BF)
        yield 1
        hidden_two = h1 + dot(mixture, wproj[...])
        yield 1
        xhat_two, rstd_two = norm_stats(hidden_two)
        normed_two = (xhat_two * norm_ref[3, 0:1] + norm_ref[3, 1:2]).astype(BF)
        yield 1
        yield from feed_forward(normed_two, wup, act, slope)
        hidden = hidden_two + dot_nt(act[...], wdown[...])
        yield 1
        xhat, rstd = norm_stats(hidden)
        normed_last = (xhat * norm_ref[4, 0:1] + norm_ref[4, 1:2]).astype(BF)
        yield 1
        predicted = dot(normed_last, wdec[...])
        cells = dot_tn(mask_ref[col], jnp.ones((8, CIN), BF))
        yield 1
        error = predicted - edge_first(target_ref[col])
        cells = edge_first(cells)
        square = error * error + 1.0
        back = lax.rsqrt(square)
        gscale_ref[0:1] += jnp.sum(cells * (1.0 - square * back * inverse), axis=0, keepdims=True)
        gscale_ref[1:2] += jnp.sum(cells, axis=0, keepdims=True)
        dpred = (cells * inverse * error * back).astype(BF)
        yield 1
        dnorm = dot_nt(dpred, wdec[...])
        yield 1
        gdec_ref[...] += dot_tn(normed_last[0:256], dpred[0:256])
        keep("last", normed_last[256:])
        keep("dp", dpred[256:])
        yield 1
        add_norm_grads(gnorm_ref, 2, dnorm, xhat)
        grad = norm_back(dnorm, xhat, rstd, norm_ref[4, 0:1])
        grad_low = grad.astype(BF)
        yield 1
        yield from feed_backward(grad_low, wdown, act, slope, normed_two, gup_ref, gdown_ref, du, keep)
        dnorm = dot_nt(du[...], wup[...])
        yield 1
        add_norm_grads(gnorm_ref, 1, dnorm, xhat_two)
        grad = grad + norm_back(dnorm, xhat_two, rstd_two, norm_ref[3, 0:1])
        grad_low = grad.astype(BF)
        dh2_ref[col, 0:64] = grad[0:64]
        dh2_ref[col, 64:72] = grad[128:136]
        dh2_ref[col, 72:216] = grad[144:288]
        dh2_ref[col, 216:280] = grad[64:128]
        dh2_ref[col, 280:288] = grad[136:144]
        x2_ref[col, 0:64] = xhat_one[0:64]
        x2_ref[col, 64:72] = xhat_one[128:136]
        x2_ref[col, 72:216] = xhat_one[144:288]
        x2_ref[col, 216:280] = xhat_one[64:128]
        x2_ref[col, 280:288] = xhat_one[136:144]
        r2_ref[col, 0:64] = rstd_one[0:64]
        r2_ref[col, 64:72] = rstd_one[128:136]
        r2_ref[col, 72:216] = rstd_one[144:288]
        r2_ref[col, 216:280] = rstd_one[64:128]
        r2_ref[col, 280:288] = rstd_one[136:144]
        yield 1
        dmix = dot_nt(grad_low, wproj[...]).astype(BF)
        yield 1
        gproj_ref[...] += dot_tn(mixture[0:256], grad_low[0:256])
        keep("mix", mixture[256:])
        keep("da", grad_low[256:])
        yield 1
        found = []
        yield from attention_backward(
            queries[0:WIN], k_edge, v_edge, probs_ref.at[col, 0], dmix[0:WIN], masks, masks32, True, found
        )
        yield 1
        yield from attention_backward(
            queries[WIN:], k_mid, v_mid, probs_ref.at[col, 1], dmix[WIN:], masks, masks32, False, found
        )
        dq_e, dk_e, dv_e, dq_m, dk_m, dv_m = found
        dq = jnp.concatenate([dq_e, dq_m], axis=0).astype(BF)
        dk = jnp.concatenate([dk_e[0], dk_e[1], dk_m], axis=0).astype(BF)
        dv = jnp.concatenate([dv_e[0], dv_e[1], dv_m], axis=0).astype(BF)
        dkv = jnp.concatenate([dk, dv], axis=1)
        yield 1
        dn_kv = dot_nt(dkv, wqkv[:, C:])
        dtop_ref[col] = dn_kv[0:HALF].astype(BF)
        dbot_ref[col] = dn_kv[WIN : WIN + HALF].astype(BF)
        yield 1
        dn_q = dot_nt(dq, wqkv[:, 0:C])
        dn_ref[col, 0:64] = dn_q[0:64] + dn_kv[72:136]
        dn_ref[col, 64:72] = dn_q[128:136] + dn_kv[136:144]
        dn_ref[col, 72:216] = dn_q[144:288] + dn_kv[288:432]
        dn_ref[col, 216:280] = dn_q[64:128] + dn_kv[216:280]
        dn_ref[col, 280:288] = dn_q[136:144] + dn_kv[280:288]
        yield 1
        gqkv_ref[:, 0:C] += dot_tn(normed_low[0:256], dq[0:256])
        yield 1
        gqkv_ref[:, C:] += dot_tn(n_kv[0:256], dkv[0:256])
        keep("n", normed_low[256:])
        keep("dq", dq[256:])
        keep("nkv", n_kv[256:])
        keep("dkv", dkv[256:])

    drive([one(col) for col in range(columns)], OFFSET)

    @pl.when(step == pl.num_programs(0) - 1)
    def _():
        gup_ref[...] += dot_tn(kept["n2"][...], kept["du"][...])
        gdown_ref[...] += dot_tn(kept["dm"][...], kept["act"][...])
        gproj_ref[...] += dot_tn(kept["mix"][...], kept["da"][...])
        gqkv_ref[:, 0:C] += dot_tn(kept["n"][...], kept["dq"][...])
        gqkv_ref[:, C:] += dot_tn(kept["nkv"][...], kept["dkv"][...])
        gdec_ref[...] += dot_tn(kept["last"][...], kept["dp"][...])
        store_qkv_proj(flat_ref, 0, gqkv_ref, gproj_ref)
        store_wide(flat_ref, 6 * C, gup_ref, FF)
        store_wide(flat_ref, 12 * C, gdown_ref, FF)
        flat_ref[18 * C : 19 * C] = gdec_ref[...]
        store_narrow(flat_ref, 19 * C, gnorm_ref, 8)
        flat_ref[19 * C + 16 : 19 * C + 24] = gscale_ref[...]
        clear_from(flat_ref, FLAT_MIDDLE)
        if not first:
            flat_ref[...] += prev_ref[...]


ZERO_KEEP = (
    ("act", TAIL, FF),
    ("du", TAIL, FF),
    ("dm", TAIL, C),
    ("n2", TAIL, C),
    ("mix", TAIL, C),
    ("da", TAIL, C),
    ("n", TAIL, C),
    ("dp", TAIL, 3 * C),
    ("an", TAIL, CIN),
    ("dh", TAIL, C),
)


def backward_zero(columns, count, first, sample, *refs):
    step_ref, an_ref, x0_ref, r0_ref, pack_ref, probs_ref, mix_ref, x1_ref, r1_ref, act_ref, slope_ref = refs[:11]
    dh2_ref, dn_ref, x2_ref, r2_ref, ret_top_ref, ret_bot_ref = refs[11:17]
    qkv_ref, proj_ref, up_ref, down_ref, norm_ref = refs[17:22]
    refs = refs[22:]
    if not first:
        prev_ref, refs = refs[0], refs[1:]
    flat_ref, wqkv, wproj, wup, wdown, du_ref = refs[:6]
    sums = refs[6:13]
    gembed_ref, glead_ref, gqkv_ref, gproj_ref, gup_ref, gdown_ref, gnorm_ref = sums
    kept = {name: ref for (name, _, _), ref in zip(ZERO_KEEP, refs[13:])}
    step = pl.program_id(0)

    @pl.when(step == 0)
    def _():
        wqkv[...] = qkv_ref[0].astype(BF)
        wproj[...] = proj_ref[0].astype(BF)
        wup[...] = up_ref[0].astype(BF)
        wdown[...] = down_ref[0].astype(BF)
        for ref in sums:
            ref[...] = jnp.zeros_like(ref)

    masks = head_masks()
    masks32 = [m.astype(F32) for m in masks]
    lead_at = pl.ds(step_ref[sample] - 1, 1)

    def one(col):
        def keep(name, value):
            rows = value.shape[0]
            at = pl.multiple_of((step * columns + col) * rows, 16)
            kept[name][pl.ds(at, rows), :] = value

        dn = jnp.concatenate(
            [
                dn_ref[col, 0:HALF] + ret_top_ref[col].astype(F32),
                dn_ref[col, HALF : COL - HALF],
                dn_ref[col, COL - HALF :] + ret_bot_ref[col].astype(F32),
            ],
            axis=0,
        )
        xhat = x2_ref[col]
        add_norm_grads(gnorm_ref, 2, dn, xhat)
        grad = dh2_ref[col] + norm_back(dn, xhat, r2_ref[col], norm_ref[2, 0:1])
        grad_low = grad.astype(BF)
        yield 1
        xhat = x1_ref[col]
        normed_two = (xhat * norm_ref[1, 0:1] + norm_ref[1, 1:2]).astype(BF)
        yield 1
        yield from feed_backward(
            grad_low, wdown, act_ref.at[col], slope_ref.at[col], normed_two, gup_ref, gdown_ref, du_ref.at[col], keep
        )
        dnorm = dot_nt(du_ref[col], wup[...])
        yield 1
        add_norm_grads(gnorm_ref, 1, dnorm, xhat)
        grad = grad + norm_back(dnorm, xhat, r1_ref[col], norm_ref[1, 0:1])
        grad_low = grad.astype(BF)
        yield 1
        dmix = dot_nt(grad_low, wproj[...]).astype(BF)
        yield 1
        gproj_ref[...] += dot_tn(mix_ref[col, 0:256], grad_low[0:256])
        keep("mix", mix_ref[col, 256:COL])
        keep("da", grad_low[256:])
        yield 1
        parts = []
        for w in range(2):
            part = pack_ref[col, WIN * w : WIN * w + WIN]
            found = []
            yield from attention_backward(
                part[:, 0:C],
                part[:, C : 2 * C],
                part[:, 2 * C :],
                probs_ref.at[col, w],
                dmix[WIN * w : WIN * w + WIN],
                masks,
                masks32,
                False,
                found,
            )
            parts.append(jnp.concatenate([g.astype(BF) for g in found], axis=1))
        dpacked = jnp.concatenate(parts, axis=0)
        yield 1
        dn = dot_nt(dpacked, wqkv[...])
        yield 1
        xhat = x0_ref[col]
        normed = (xhat * norm_ref[0, 0:1] + norm_ref[0, 1:2]).astype(BF)
        gqkv_ref[...] += dot_tn(normed[0:256], dpacked[0:256])
        keep("n", normed[256:])
        keep("dp", dpacked[256:])
        yield 1
        add_norm_grads(gnorm_ref, 0, dn, xhat)
        grad = grad + norm_back(dn, xhat, r0_ref[col], norm_ref[0, 0:1])
        glead_ref[lead_at, :] += jnp.sum(grad, axis=0, keepdims=True)
        grad_low = grad.astype(BF)
        yield 1
        gembed_ref[...] += dot_tn(grad_low[0:256], an_ref[col, 0:256])
        keep("an", an_ref[col, 256:COL])
        keep("dh", grad_low[256:])

    drive([one(col) for col in range(columns)], OFFSET)

    @pl.when(step == pl.num_programs(0) - 1)
    def _():
        gup_ref[...] += dot_tn(kept["n2"][...], kept["du"][...])
        gdown_ref[...] += dot_tn(kept["dm"][...], kept["act"][...])
        gproj_ref[...] += dot_tn(kept["mix"][...], kept["da"][...])
        gqkv_ref[...] += dot_tn(kept["n"][...], kept["dp"][...])
        gembed_ref[...] += dot_tn(kept["dh"][...], kept["an"][...])
        store_qkv_proj(flat_ref, 0, gqkv_ref, gproj_ref)
        store_wide(flat_ref, 6 * C, gup_ref, FF)
        store_wide(flat_ref, 12 * C, gdown_ref, FF)
        flat_ref[18 * C : 19 * C] = gembed_ref[...]
        store_narrow(flat_ref, 19 * C, gnorm_ref, 8)
        store_narrow(flat_ref, 19 * C + 16, glead_ref, 24)
        clear_from(flat_ref, FLAT_ZERO)
        if not first:
            flat_ref[...] += prev_ref[...]


def exchanges(sizes):
    out = []
    for axis in ("batch", "lat"):
        size = sizes[axis]
        if size % 2 == 0:
            out.append((axis, 1, 2))
            if size > 2:
                out.append((axis, 2, size // 2))
        elif size > 1:
            out.append((axis, 1, size))
    return out


def streams_of(sizes, arrays, rows):
    base = exchanges(sizes)
    unit = 8 * sizes["lat"] * sizes["batch"]
    orders = [base]
    if len(base) == 4:
        orders = [[base[0], base[i], base[j], base[k]] for i, j, k in ORDERS]
    out = []
    for array in range(arrays):
        units = rows // unit
        at = 0
        for n, order in enumerate(orders):
            left = len(orders) - n
            share = units - at if left == 1 else min(units - at, -(-units * SHARES[n] // sum(SHARES)))
            if share:
                out.append((array, at * unit, share * unit, order))
            at += share
    return out


ORDERS = ((1, 2, 3), (2, 1, 3), (3, 1, 2))
SHARES = (2, 2, 1)


def all_sum(streams, arrays, *refs):
    sources, outs, scratch = refs[:arrays], refs[arrays : 2 * arrays], list(refs[2 * arrays :])

    def take(count):
        head = scratch[:count]
        del scratch[:count]
        return head

    met = []
    for _, _, _, order in streams:
        for stage in order:
            if stage not in met:
                met.append(stage)
    places, peers = {}, {}
    for axis, stride, count in met:
        index = lax.axis_index(axis)
        place = lax.rem(index // stride, count)
        others = []
        for hop in range(1, count):
            other = lax.rem(place + hop, count)
            others.append((other, {axis: index + (other - place) * stride}))
        places[axis, stride, count] = place
        peers[axis, stride, count] = others

    barrier = pltpu.get_barrier_semaphore()
    for others in peers.values():
        for _, device in others:
            pl.semaphore_signal(barrier, inc=1, device_id=device, device_id_type=pl.DeviceIdType.MESH)
    pl.semaphore_wait(barrier, sum(len(others) for others in peers.values()))

    def span(place, rows):
        return pl.ds(pl.multiple_of(place * rows, 8), rows)

    def stream(array, start, length, order):
        levels = len(order)
        held, landed, gathered = take(levels), take(levels), take(levels - 1)
        send, recv, send_back, recv_back = take(levels), take(levels), take(levels), take(levels)
        whole_in = sources[array].at[pl.ds(start, length)]
        whole_out = outs[array].at[pl.ds(start, length)]

        def out_copies(s, outgoing):
            rows = held[s].shape[0]
            source = whole_in if s == 0 else held[s - 1]
            place = places[order[s]]
            return [
                pltpu.make_async_remote_copy(
                    src_ref=source.at[span(other, rows)],
                    dst_ref=landed[s].at[place if outgoing else other],
                    send_sem=send[s].at[other],
                    recv_sem=recv[s].at[place if outgoing else other],
                    device_id=device,
                    device_id_type=pl.DeviceIdType.MESH,
                )
                for other, device in peers[order[s]]
            ]

        def back_copies(s, outgoing):
            rows = held[s].shape[0]
            own = held[s] if s == levels - 1 else gathered[s]
            target = whole_out if s == 0 else gathered[s - 1]
            place = places[order[s]]
            return [
                pltpu.make_async_remote_copy(
                    src_ref=own,
                    dst_ref=target.at[span(place if outgoing else other, rows)],
                    send_sem=send_back[s].at[other],
                    recv_sem=recv_back[s].at[place if outgoing else other],
                    device_id=device,
                    device_id_type=pl.DeviceIdType.MESH,
                )
                for other, device in peers[order[s]]
            ]

        for s in range(levels):
            rows = held[s].shape[0]
            source = whole_in if s == 0 else held[s - 1]
            for copy in out_copies(s, True):
                copy.start()
            yield 1
            for copy in out_copies(s, False):
                copy.wait()
            total = source[span(places[order[s]], rows), :]
            for other, _ in peers[order[s]]:
                total = total + landed[s][other]
            held[s][...] = total
        for s in reversed(range(levels)):
            rows = held[s].shape[0]
            own = held[s] if s == levels - 1 else gathered[s]
            target = whole_out if s == 0 else gathered[s - 1]
            for copy in back_copies(s, True):
                copy.start()
            target[span(places[order[s]], rows), :] = own[...]
            yield 1
            for copy in back_copies(s, False):
                copy.wait()

    drive([stream(*each) for each in streams], 0)


def run_all_sum(flats, sizes):
    rows = flats[0].shape[0]
    streams = streams_of(sizes, len(flats), rows)
    scratch = []
    for _, _, length, order in streams:
        held, landed, sems = [], [], []
        for _, _, count in order:
            length //= count
            held.append(pltpu.VMEM((length, 128), F32))
            landed.append(pltpu.VMEM((count, length, 128), F32))
            sems.append(pltpu.SemaphoreType.DMA((count,)))
        scratch += held + landed + held[:-1] + sems * 4
    return pl.pallas_call(
        partial(all_sum, streams, len(flats)),
        out_shape=[struct(flat.shape, F32) for flat in flats],
        in_specs=[pl.BlockSpec(memory_space=pltpu.VMEM)] * len(flats),
        out_specs=[pl.BlockSpec(memory_space=pltpu.VMEM)] * len(flats),
        scratch_shapes=scratch,
        compiler_params=pltpu.CompilerParams(
            collective_id=0, has_side_effects=True, vmem_limit_bytes=VMEM_BYTES
        ),
        name="all_sum",
    )(*flats)


def update(steps, mid_ref, zero_ref, *refs):
    weights, firsts, seconds = refs[0:9], refs[9:18], refs[18:27]
    news, moms, secs = refs[27:36], refs[36:45], refs[45:54]
    small_ref, factor_ref = refs[54], refs[55]
    step = pl.program_id(0)
    scale_at = 19 * C + 16

    @pl.when(step == 0)
    def _():
        total = mid_ref[scale_at + 1 : scale_at + 2]
        count = total * CIN
        inverse = 1.0 / count

        def squares(ref, a, b):
            part = ref[a:b] * inverse
            return jnp.sum((part * part).reshape((b - a) // 8, 8, 128), axis=0)

        row = lax.broadcasted_iota(jnp.int32, (8, 128), 0)
        scale_grad = mid_ref[scale_at : scale_at + 1]
        mean_grad = scale_grad * inverse
        norms = jnp.sum(
            squares(mid_ref, 0, scale_at)
            + squares(zero_ref, 0, FLAT_ZERO)
            + jnp.where(row == 0, mean_grad * mean_grad, 0.0),
        )
        norm = jnp.sqrt(jnp.broadcast_to(norms, (1, 128)))
        factor_ref[...] = jnp.minimum(1.0, clip_max / norm) * inverse
        loss = jnp.broadcast_to(jnp.sum(total - scale_grad + weights[8][...] * total), (1, 128))
        small_ref[...] = jnp.where(row == 0, loss, jnp.where(row == 1, count, norm))

    factor = factor_ref[...]

    def adam(at, where, grad):
        clipped = grad * factor[:, 0 : grad.shape[-1]]
        first = beta_one * firsts[at][where] + (1.0 - beta_one) * clipped
        second = beta_two * seconds[at][where] + ((1.0 - beta_two) * clipped) * clipped
        weight = weights[at][where]
        root = second * (1.0 / (1.0 - beta_two**STEP))
        root = root * lax.rsqrt(root) + adam_eps
        rate = rate_table[at] / (1.0 - beta_one**STEP)
        new = weight - rate * first * pl.reciprocal(root)
        if decay_table[at]:
            new = new - (rate_table[at] * decay_table[at]) * weight
        news[at][where] = new
        moms[at][where] = first
        secs[at][where] = second

    rows = C // steps
    low = step * rows

    def take(ref, base):
        return ref[pl.ds(pl.multiple_of(base + low, 8), rows), :]

    for layer_at, ref in enumerate((zero_ref, mid_ref)):

        def put(at, a, b, grad):
            adam(at, (layer_at, slice(None), slice(a, b)), grad)

        for j in range(4):
            put(2, 128 * j, 128 * j + 128, take(ref, j * C))
        both = take(ref, 4 * C)
        put(2, 512, 576, both[:, 0:64])
        put(3, 128, 192, both[:, 64:128])
        put(3, 0, 128, take(ref, 5 * C))
        for j in range(6):
            put(4, 128 * j, 128 * j + 128, take(ref, (6 + j) * C))
            put(5, 128 * j, 128 * j + 128, take(ref, (12 + j) * C))
    everything = (slice(None), slice(None))
    adam(0, everything, take(zero_ref, 18 * C))
    adam(6, everything, take(mid_ref, 18 * C))

    @pl.when(step == 0)
    def _():
        lead_at = 19 * C + 16
        adam(1, (slice(None), slice(0, 128)), zero_ref[lead_at : lead_at + LEADS])
        adam(1, (slice(None), slice(128, 192)), zero_ref[lead_at + 24 : lead_at + 24 + LEADS, 0:64])
        adam(8, everything, mid_ref[scale_at : scale_at + 1])
        for at, (ref, index) in enumerate(((zero_ref, 0), (zero_ref, 1), (zero_ref, 2), (mid_ref, 1), (mid_ref, 2))):
            a = 19 * C + 2 * index
            adam(7, (at, slice(None), slice(0, 128)), ref[a : a + 2])
            adam(7, (at, slice(None), slice(128, 192)), ref[a + 8 : a + 10, 0:64])


def run_update(mid, zero, weights, firsts, seconds):
    steps = 6
    rows = C // steps
    kinds = (
        ((C, CIN), True),
        ((LEADS, C), False),
        ((2, C, 3 * C), True),
        ((2, C, C), True),
        ((2, C, FF), True),
        ((2, C, FF), True),
        ((C, CIN), True),
        ((5, 2, C), False),
        ((1, CIN), False),
    )
    specs = []
    for shape, cut in kinds:
        if not cut:
            specs.append(whole(shape))
        elif len(shape) == 2:
            specs.append(pl.BlockSpec((rows, shape[1]), lambda i: (i, 0)))
        else:
            specs.append(pl.BlockSpec((2, rows, shape[2]), lambda i: (0, i, 0)))
    shapes = [struct(shape, F32) for shape, _ in kinds]
    out = pl.pallas_call(
        partial(update, steps),
        grid=(steps,),
        in_specs=[whole(mid.shape), whole(zero.shape)] + specs * 3,
        out_specs=specs * 3 + [whole((8, 128))],
        out_shape=shapes * 3 + [struct((8, 128), F32)],
        scratch_shapes=[pltpu.VMEM((1, 128), F32)],
        compiler_params=pltpu.CompilerParams(vmem_limit_bytes=VMEM_BYTES),
        name="update",
    )(mid, zero, *weights, *firsts, *seconds)
    return out[0:9], out[9:18], out[18:27], out[27]


def whole(shape):
    zeros = (0,) * len(shape)
    return pl.BlockSpec(shape, lambda i: zeros)


def layer(shape, index):
    at = (index,) + (0,) * len(shape)
    return pl.BlockSpec((1,) + shape, lambda i: at)


def rows_of(columns, offset, *shape):
    tail = (0,) * len(shape)
    return pl.BlockSpec((columns,) + shape, lambda i: (i + offset,) + tail)


def rows(columns, *shape):
    return rows_of(columns, 0, *shape)


SMEM = pl.BlockSpec(memory_space=pltpu.SMEM)


def struct(shape, dtype):
    return jax.ShapeDtypeStruct(shape, dtype)


def low(*shape):
    return pltpu.VMEM(shape, BF)


def full(*shape):
    return pltpu.VMEM(shape, F32)


def kept_scratch(kept, count):
    return [low(count * rows, width) for _, rows, width in kept]


def run_forward(lead_step, tokens, lead_table, embed_t, qkv_w, proj_w, up_w, down_t, norm_t, sample, count, columns):
    steps = count // columns
    outs = [
        ((count, COL, C), F32),
        ((count, COL, 1), F32),
        ((count, COL, 3 * C), BF),
        ((count, 2, WIN, LANES), F32),
        ((count, COL, C), BF),
        ((count, COL, C), F32),
        ((count, COL, 1), F32),
        ((count, COL, FF), BF),
        ((count, COL, FF), F32),
        ((count, COL, C), F32),
        ((count, HALF, C), BF),
        ((count, HALF, C), BF),
    ]
    return pl.pallas_call(
        partial(forward_zero, columns, sample),
        grid=(steps,),
        in_specs=[
            SMEM,
            rows_of(columns, sample * steps, COL, CIN),
            whole((LEADS, C)),
            whole((C, CIN)),
            layer((C, 3 * C), 0),
            layer((C, C), 0),
            layer((C, FF), 0),
            layer((C, FF), 0),
            whole((5, 2, C)),
        ],
        out_specs=[rows(columns, *shape[1:]) for shape, _ in outs],
        out_shape=[struct(*o) for o in outs],
        scratch_shapes=[low(C, CIN), low(C, 3 * C), low(C, C), low(C, FF), low(C, FF)],
        compiler_params=pltpu.CompilerParams(vmem_limit_bytes=VMEM_BYTES),
        name="forward_zero",
    )(lead_step, tokens, lead_table, embed_t, qkv_w, proj_w, up_w, down_t, norm_t)


def run_middle(flags, h1, up_in, down_in, target, cells, qkv_w, proj_w, up_w, down_t, decode_w, norm_t, scale, prev, flat_rows, sample, count, columns):
    steps = count // columns
    outs = [
        ((count, COL, C), F32),
        ((count, COL, C), F32),
        ((count, COL, C), F32),
        ((count, COL, 1), F32),
        ((count, HALF, C), BF),
        ((count, HALF, C), BF),
    ]
    first = prev is None
    return pl.pallas_call(
        partial(middle, columns, count, first),
        grid=(steps,),
        in_specs=[
            SMEM,
            rows(columns, COL, C),
            rows(columns, HALF, C),
            rows(columns, HALF, C),
            rows_of(columns, sample * steps, COL, CIN),
            rows_of(columns, sample * steps, 8, COL),
            layer((C, 3 * C), 1),
            layer((C, C), 1),
            layer((C, FF), 1),
            layer((C, FF), 1),
            whole((C, CIN)),
            whole((5, 2, C)),
            whole((1, CIN)),
        ]
        + ([] if first else [whole((flat_rows, 128))]),
        out_specs=[rows(columns, *shape[1:]) for shape, _ in outs] + [whole((flat_rows, 128))],
        out_shape=[struct(*o) for o in outs] + [struct((flat_rows, 128), F32)],
        scratch_shapes=[
            low(C, 3 * C),
            low(C, C),
            low(C, FF),
            low(C, FF),
            low(C, CIN),
            full(columns, 2, WIN, LANES),
            low(columns, COL, FF),
            full(columns, COL, FF),
            low(columns, COL, FF),
            full(C, 3 * C),
            full(C, C),
            full(C, FF),
            full(C, FF),
            full(C, CIN),
            full(8, C),
            full(8, CIN),
        ]
        + kept_scratch(MIDDLE_KEEP, count),
        compiler_params=pltpu.CompilerParams(vmem_limit_bytes=VMEM_BYTES),
        name="middle",
    )(flags, h1, up_in, down_in, target, cells, qkv_w, proj_w, up_w, down_t, decode_w, norm_t, scale, *([] if first else [prev]))


def run_backward(lead_step, tokens, saved, mid_out, returned, qkv_w, proj_w, up_w, down_t, norm_t, prev, flat_rows, sample, count, columns):
    steps = count // columns
    first = prev is None
    return pl.pallas_call(
        partial(backward_zero, columns, count, first, sample),
        grid=(steps,),
        in_specs=[
            SMEM,
            rows_of(columns, sample * steps, COL, CIN),
            rows(columns, COL, C),
            rows(columns, COL, 1),
            rows(columns, COL, 3 * C),
            rows(columns, 2, WIN, LANES),
            rows(columns, COL, C),
            rows(columns, COL, C),
            rows(columns, COL, 1),
            rows(columns, COL, FF),
            rows(columns, COL, FF),
            rows(columns, COL, C),
            rows(columns, COL, C),
            rows(columns, COL, C),
            rows(columns, COL, 1),
            rows(columns, HALF, C),
            rows(columns, HALF, C),
            layer((C, 3 * C), 0),
            layer((C, C), 0),
            layer((C, FF), 0),
            layer((C, FF), 0),
            whole((5, 2, C)),
        ]
        + ([] if first else [whole((flat_rows, 128))]),
        out_specs=whole((flat_rows, 128)),
        out_shape=struct((flat_rows, 128), F32),
        scratch_shapes=[
            low(C, 3 * C),
            low(C, C),
            low(C, FF),
            low(C, FF),
            low(columns, COL, FF),
            full(C, CIN),
            full(24, C),
            full(C, 3 * C),
            full(C, C),
            full(C, FF),
            full(C, FF),
            full(8, C),
        ]
        + kept_scratch(ZERO_KEEP, count),
        compiler_params=pltpu.CompilerParams(vmem_limit_bytes=VMEM_BYTES),
        name="backward_zero",
    )(lead_step, tokens, *saved, *mid_out, *returned, qkv_w, proj_w, up_w, down_t, norm_t, *([] if first else [prev]))


def neighbours(low, high):
    count = lax.axis_size("lat")
    forward = [(i, i + 1) for i in range(count - 1)]
    backward = [(b, a) for a, b in forward]
    return lax.ppermute(high, "lat", forward), lax.ppermute(low, "lat", backward)


def views(group):
    embed, lead, qkv, proj, up, down, decode, norm, scale = group
    return (embed.T, lead, qkv, proj, up, down.transpose(0, 2, 1), decode, norm.transpose(1, 0, 2), scale[None, :])


def unviews(group):
    embed, lead, qkv, proj, up, down, decode, norm, scale = group
    return (embed.T, lead, qkv, proj, up, down.transpose(0, 2, 1), decode, norm.transpose(1, 0, 2), scale[0])


def on_device(analysis, target, lead_step, loss_mask, *state):
    weights, firsts, seconds = (views(state[9 * i : 9 * i + 9]) for i in range(3))
    embed_t, lead_table, qkv_w, proj_w, up_w, down_t, decode_w, norm_t, scale = weights
    samples, blocks = analysis.shape[0], analysis.shape[1]
    sizes = {axis: lax.axis_size(axis) for axis in ("lat", "batch")}
    tokens = analysis.transpose(0, 1, 2, 4, 3, 5).reshape(samples * blocks, COL, CIN)
    truth = target.transpose(0, 1, 2, 4, 3, 5).reshape(samples * blocks, COL, CIN)
    cells = loss_mask.transpose(0, 1, 2, 4, 3).reshape(samples * blocks, 1, COL).astype(BF)
    cells = jnp.pad(cells, ((0, 0), (0, 7), (0, 0)))
    at = lax.axis_index("lat")
    flags = jnp.stack([jnp.where(at > 0, 0.0, -1e30), jnp.where(at < sizes["lat"] - 1, 0.0, -1e30)]).astype(F32)
    columns = 2 if blocks % 2 == 0 else 1
    unit = 8 * sizes["lat"] * sizes["batch"]
    flat_rows = -(-max(FLAT_MIDDLE, FLAT_ZERO) // unit) * unit

    forward = [
        run_forward(lead_step, tokens, lead_table, embed_t, qkv_w, proj_w, up_w, down_t, norm_t, s, blocks, columns)
        for s in range(samples)
    ]
    edges = [neighbours(f[10], f[11]) for f in forward]
    mid = None
    mids = []
    for s in range(samples):
        up_in, down_in = edges[s]
        *out, mid = run_middle(
            flags, forward[s][9], up_in, down_in, truth, cells, qkv_w, proj_w, up_w, down_t, decode_w, norm_t, scale,
            mid, flat_rows, s, blocks, columns,
        )
        mids.append(out)
    returned = [neighbours(m[4], m[5]) for m in mids]
    zero = None
    for s in range(samples):
        zero = run_backward(
            lead_step, tokens, forward[s][:9], mids[s][:4], returned[s], qkv_w, proj_w, up_w, down_t, norm_t,
            zero, flat_rows, s, blocks, columns,
        )
    if unit > 8:
        mid, zero = run_all_sum([mid, zero], sizes)
    news, moments, squares, small = run_update(mid, zero, weights, firsts, seconds)
    return (*unviews(news), *unviews(moments), *unviews(squares), small[0, 0], small[1, 0], small[2, 0])


def solution(mesh):
    split = P("batch", None, "lat", None, None, None)
    placed = (split, split, P("batch"), P("batch", None, "lat", None, None)) + (P(),) * 27
    return jax.shard_map(
        on_device, mesh=mesh, in_specs=placed, out_specs=(P(),) * 30, check_vma=False
    )
```

time: 561 us -> 353 us (0.63)
  waiting for transfers between devices: 101 us -> 0.02 us
  blocking collectives: 44.1 us -> 0 us
  other arithmetic: 29 us -> 0.69 us
  between operations: 23.6 us -> 1.45 us
  Pallas kernels: 322 us -> 313 us
  local copies, waits for them, and re-layouts: 14.4 us -> 6.22 us
    psum x1 -> x0, waiting for transfers between devices: 101 us -> none  [on_device(): sums, back = lax.psum((sums, back), ('lat', 'batch'))]
    psum x1 -> x0, blocking collectives: 44.1 us -> none  [on_device(): sums, back = lax.psum((sums, back), ('lat', 'batch'))]
    sub x9 -> x0, other arithmetic: 17.3 us -> none  [apply_update(): weight - rate * (first_hat / (jnp.sqrt(second_hat) + adam_eps) + shrink *...]
    reduce_sum x8 -> x0, other arithmetic: 11 us -> none  [apply_update(): grad_norm = jnp.sqrt(sum((jnp.sum(member * member) for member in scaled)))]
    pallas_call x6 -> x8, Pallas kernels: 322 us -> 313 us  [the longest x2 112 us: run_middle(): pl.pallas_call(partial(middle, columns, count, first), grid=(steps,), in_...]
    unnamed x104 -> x18, local copies, waits for them, and re-layouts: 12.6 us -> 3.55 us
  transfers between devices with their start and end apart: 9 -> 8, of which waited for: 1 -> 0; matrix products, arithmetic and copies ran while one was open for 1% -> 1% of each run, Pallas kernels for 42% -> 50%
where the time goes in v2:
time: 353 us; the launch traced here: 347 us
  Pallas kernels  313 us (89%)
  starting transfers between devices  25.8 us (7%)
  local copies, waits for them, and re-layouts  6.22 us (2%)
    pallas_call x2, Pallas kernels, run_middle(): pl.pallas_call(partial(middle, columns, count, first), grid=(steps,), in_...  112 us
    pallas_call x2, Pallas kernels, run_backward(): pl.pallas_call(partial(backward_zero, columns, count, first, sample), gri...  69.1 us
    pallas_call x1, Pallas kernels, run_all_sum(): pl.pallas_call(partial(all_sum, streams, len(flats)), out_shape=[struct(f...  60.3 us
    pallas_call x2, Pallas kernels, run_forward(): pl.pallas_call(partial(forward_zero, columns, sample), grid=(steps,), in_...  57.9 us
    ppermute x4, starting transfers between devices, neighbours(): lax.ppermute(high, 'lat', forward)  19.8 us
    pallas_call x1, Pallas kernels, run_update(): pl.pallas_call(partial(update, steps), grid=(steps,), in_specs=[whole(mid...  13.5 us
  transfers between devices with their start and end apart: 8, of which 0 were waited for; matrix products, arithmetic and copies ran while one was open for 1% of the time, Pallas kernels for 50%

profile of v2, /device:TPU:0, one launch (start us, length us, event | category | flops | bytes accessed | tf_op | source)
XLA Modules:
  0.0 346.9 jit_solution(4133510237006971590)
XLA Ops:
  0.7 28.9 %forward_zero.3 = (f32[12,288,192]{2,1,0:T(8,128)}, f32[12,288,1]{2,1,0:T(8,128)}, bf16[12,288,576]{2,1,0:T(8,128)(2,1)}, f32[12,2,144,896]{3,2,1,0:T(8,128)}, b...) custom-call(s32[2]{0:T(128)} %refs_0_.3, ...), custom_call_target="tpu_custom_call" | custom-call | tf_op jit(solution)/shard_map/forward_zero/pallas_call | solution.py:1072
  29.6 4.9 %collective-permute-start.2 = (bf16[12,72,192]{2,1,0:T(8,128)(2,1)}, bf16[12,72,192]{2,1,0:T(8,128)(2,1)S(1)}, u32[]{:S(2)}, u32[]{:S(2)}) collective-permute-start(bf16[12,72,192]{2,1,0:T(8,128)(2,1)} %get-tuple-element.102), channel_id=1, source_target_pairs={{0,4},{4,8},{8,12},{12,16},{16,20},{20,24},{24,28},{1,5},{5,9},{9,... | collective-permute-start | bytes 995336 | tf_op jit(solution)/shard_map/ppermute | solution.py:1207
  34.5 1.4 collective-permute-start.3
  35.9 29.0 %forward_zero.2 = (f32[12,288,192]{2,1,0:T(8,128)}, f32[12,288,1]{2,1,0:T(8,128)}, bf16[12,288,576]{2,1,0:T(8,128)(2,1)}, f32[12,2,144,896]{3,2,1,0:T(8,128)}, b...) custom-call(s32[2]{0:T(128)} %refs_0_.3, ...), custom_call_target="tpu_custom_call" | custom-call | tf_op jit(solution)/shard_map/forward_zero/pallas_call | solution.py:1072
  64.9 4.6 %collective-permute-start = (bf16[12,72,192]{2,1,0:T(8,128)(2,1)}, bf16[12,72,192]{2,1,0:T(8,128)(2,1)S(1)}, u32[]{:S(2)}, u32[]{:S(2)}) collective-permute-start(bf16[12,72,192]{2,1,0:T(8,128)(2,1)} %get-tuple-element.99), channel_id=1, source_target_pairs={{0,4},{4,8},{8,12},{12,16},{16,20},{20,24},{24,28},{1,5},{5,9},{9,... | collective-permute-start | bytes 995336 | tf_op jit(solution)/shard_map/ppermute | solution.py:1207
  69.5 1.5 collective-permute-start.1
  71.1 0.4 copy.62
  71.8 0.7 pad.4.refs_5_
  72.5 0.6 pad_maximum_fusion.refs_0_
  73.1 0.7 copy-done.4
  74.0 55.5 %middle.2 = (f32[12,288,192]{2,1,0:T(8,128)}, f32[12,288,192]{2,1,0:T(8,128)}, f32[12,288,192]{2,1,0:T(8,128)}, f32[12,288,1]{2,1,0:T(8,128)}, bf16[12,72,192]{2...) custom-call(f32[2]{0:T(128)} %pad_maximum_fusion.refs_0_, ...), custom_call_target="tpu_custom_call" | custom-call | tf_op jit(solution)/shard_map/middle/pallas_call | solution.py:1105
  129.5 5.0 %collective-permute-start.6 = (bf16[12,72,192]{2,1,0:T(8,128)(2,1)}, bf16[12,72,192]{2,1,0:T(8,128)(2,1)S(1)}, u32[]{:S(2)}, u32[]{:S(2)}) collective-permute-start(bf16[12,72,192]{2,1,0:T(8,128)(2,1)} %get-tuple-element.134), channel_id=1, source_target_pairs={{0,4},{4,8},{8,12},{12,16},{16,20},{20,24},{24,28},{1,5},{5,9},{9,... | collective-permute-start | bytes 995336 | tf_op jit(solution)/shard_map/ppermute | solution.py:1207
  134.5 1.5 collective-permute-start.7
  136.1 0.7 copy-done.2
  136.9 56.4 %middle.3 = (f32[12,288,192]{2,1,0:T(8,128)}, f32[12,288,192]{2,1,0:T(8,128)}, f32[12,288,192]{2,1,0:T(8,128)}, f32[12,288,1]{2,1,0:T(8,128)}, bf16[12,72,192]{2...) custom-call(f32[2]{0:T(128)} %pad_maximum_fusion.refs_0_, ...), custom_call_target="tpu_custom_call" | custom-call | tf_op jit(solution)/shard_map/middle/pallas_call | solution.py:1105
  193.3 5.5 %collective-permute-start.4 = (bf16[12,72,192]{2,1,0:T(8,128)(2,1)}, bf16[12,72,192]{2,1,0:T(8,128)(2,1)S(1)}, u32[]{:S(2)}, u32[]{:S(2)}) collective-permute-start(bf16[12,72,192]{2,1,0:T(8,128)(2,1)} %get-tuple-element.119), channel_id=1, source_target_pairs={{0,4},{4,8},{8,12},{12,16},{16,20},{20,24},{24,28},{1,5},{5,9},{9,... | collective-permute-start | bytes 995336 | tf_op jit(solution)/shard_map/ppermute | solution.py:1207
  198.8 1.5 collective-permute-start.5
  200.4 0.7 copy-done.6
  201.2 34.0 %backward_zero.2.refs_22_ = f32[3840,128]{1,0:T(8,128)} custom-call(s32[2]{0:T(128)} %refs_0_.3, bf16[24,288,128]{2,1,0:T(8,128)(2,1)} %bitcast.48, f32[12,288,192]{2,1,0:T(8,128)} %get-tuple-element.121.refs_2_, f32[12,288,1]{2,1,0:T(8,128)} %get-tuple-element.122.refs_3_, bf16[12,288,576]{2,1,0:T(8,128)(2,1)} %get-tuple-element.123.refs_4_, ...), custom_call_target="tpu_custom_call" | custom-call | tf_op jit(solution)/shard_map/backward_zero/pallas_call | solution.py:1153
  235.3 0.7 copy-done
  236.2 35.0 %backward_zero.3.refs_1_ = f32[3840,128]{1,0:T(8,128)} custom-call(s32[2]{0:T(128)} %refs_0_.3, bf16[24,288,128]{2,1,0:T(8,128)(2,1)} %bitcast.49, f32[12,288,192]{2,1,0:T(8,128)} %get-tuple-element.106.refs_2_, f32[12,288,1]{2,1,0:T(8,128)} %get-tuple-element.107.refs_3_, bf16[12,288,576]{2,1,0:T(8,128)(2,1)} %get-tuple-element.108.refs_4_, ...), custom_call_target="tpu_custom_call" | custom-call | tf_op jit(solution)/shard_map/backward_zero/pallas_call | solution.py:1153
  271.2 60.3 %all_sum.1 = (f32[3840,128]{1,0:T(8,128)}, f32[3840,128]{1,0:T(8,128)}) custom-call(f32[3840,128]{1,0:T(8,128)} %get-tuple-element.105.refs_0_, f32[3840,128]{1,0:T(8,128)} %backward_zero.3.refs_1_), custom_call_target="tpu_custom_call" | custom-call | tf_op jit(solution)/shard_map/all_sum/pallas_call | solution.py:886
  331.5 13.5 %update.1 = (f32[192,128]{1,0:T(8,128)}, f32[20,192]{1,0:T(8,128)}, f32[2,192,576]{2,1,0:T(8,128)}, f32[2,192,192]{2,1,0:T(8,128)}, f32[2,192,768]{2,1,0:T(8,128...) custom-call(f32[3840,128]{1,0:T(8,128)} %get-tuple-element.136.mid_r, ...), custom_call_target="tpu_custom_call" | custom-call | tf_op jit(solution)/shard_map/update/pallas_call | solution.py:1005
  345.0 1.3 fusion
  (25 shorter events, 1.0 us)
Async XLA Ops:
  29.6 43.5 %collective-permute-start.2 = (bf16[12,72,192]{2,1,0:T(8,128)(2,1)}, bf16[12,72,192]{2,1,0:T(8,128)(2,1)S(1)}, u32[]{:S(2)}, u32[]{:S(2)}) collective-permute-start(bf16[12,72,192]{2,1,0:T(8,128)(2,1)} %get-tuple-element.102), channel_id=1, source_target_pairs={{0,4},{4,8},{8,12},{12,16},{16,20},{20,24},{24,28},{1,5},{5,9},{9,... | collective-permute-start | bytes 995336 | tf_op jit(solution)/shard_map/ppermute | solution.py:1207
  34.5 36.5 %copy-start.8 = (s32[2,12,12,2,12]{4,3,2,1,0:T(2,128)S(1)}, s32[2,12,12,2,12]{4,3,2,1,0:T(2,128)}, u32[]{:S(2)}) copy-start(s32[2,12,12,2,12]{4,3,2,1,0:T(2,128)} %param.34) | copy-start | bytes 82948
  34.5 38.6 %collective-permute-start.3 = (bf16[12,72,192]{2,1,0:T(8,128)(2,1)}, bf16[12,72,192]{2,1,0:T(8,128)(2,1)S(1)}, u32[]{:S(2)}, u32[]{:S(2)}) collective-permute-start(bf16[12,72,192]{2,1,0:T(8,128)(2,1)} %get-tuple-element.103), channel_id=1, source_target_pairs={{4,0},{8,4},{12,8},{16,12},{20,16},{24,20},{28,24},{5,1},{9,5},{13... | collective-permute-start | bytes 995336 | tf_op jit(solution)/shard_map/ppermute | solution.py:1207
  64.9 71.1 %collective-permute-start = (bf16[12,72,192]{2,1,0:T(8,128)(2,1)}, bf16[12,72,192]{2,1,0:T(8,128)(2,1)S(1)}, u32[]{:S(2)}, u32[]{:S(2)}) collective-permute-start(bf16[12,72,192]{2,1,0:T(8,128)(2,1)} %get-tuple-element.99), channel_id=1, source_target_pairs={{0,4},{4,8},{8,12},{12,16},{16,20},{20,24},{24,28},{1,5},{5,9},{9,... | collective-permute-start | bytes 995336 | tf_op jit(solution)/shard_map/ppermute | solution.py:1207
  69.5 66.5 %collective-permute-start.1 = (bf16[12,72,192]{2,1,0:T(8,128)(2,1)}, bf16[12,72,192]{2,1,0:T(8,128)(2,1)S(1)}, u32[]{:S(2)}, u32[]{:S(2)}) collective-permute-start(bf16[12,72,192]{2,1,0:T(8,128)(2,1)} %get-tuple-element.100), channel_id=1, source_target_pairs={{4,0},{8,4},{12,8},{16,12},{20,16},{24,20},{28,24},{5,1},{9,5},{13... | collective-permute-start | bytes 995336 | tf_op jit(solution)/shard_map/ppermute | solution.py:1207
  73.1 0.8 copy-start.4
  73.1 0.9 copy-start.5
  129.5 70.8 %collective-permute-start.6 = (bf16[12,72,192]{2,1,0:T(8,128)(2,1)}, bf16[12,72,192]{2,1,0:T(8,128)(2,1)S(1)}, u32[]{:S(2)}, u32[]{:S(2)}) collective-permute-start(bf16[12,72,192]{2,1,0:T(8,128)(2,1)} %get-tuple-element.134), channel_id=1, source_target_pairs={{0,4},{4,8},{8,12},{12,16},{16,20},{20,24},{24,28},{1,5},{5,9},{9,... | collective-permute-start | bytes 995336 | tf_op jit(solution)/shard_map/ppermute | solution.py:1207
  134.5 65.8 %collective-permute-start.7 = (bf16[12,72,192]{2,1,0:T(8,128)(2,1)}, bf16[12,72,192]{2,1,0:T(8,128)(2,1)S(1)}, u32[]{:S(2)}, u32[]{:S(2)}) collective-permute-start(bf16[12,72,192]{2,1,0:T(8,128)(2,1)} %get-tuple-element.135), channel_id=1, source_target_pairs={{4,0},{8,4},{12,8},{16,12},{20,16},{24,20},{28,24},{5,1},{9,5},{13... | collective-permute-start | bytes 995336 | tf_op jit(solution)/shard_map/ppermute | solution.py:1207
  136.0 0.8 copy-start.2
  136.0 0.9 copy-start.3
  193.3 42.0 %collective-permute-start.4 = (bf16[12,72,192]{2,1,0:T(8,128)(2,1)}, bf16[12,72,192]{2,1,0:T(8,128)(2,1)S(1)}, u32[]{:S(2)}, u32[]{:S(2)}) collective-permute-start(bf16[12,72,192]{2,1,0:T(8,128)(2,1)} %get-tuple-element.119), channel_id=1, source_target_pairs={{0,4},{4,8},{8,12},{12,16},{16,20},{20,24},{24,28},{1,5},{5,9},{9,... | collective-permute-start | bytes 995336 | tf_op jit(solution)/shard_map/ppermute | solution.py:1207
  198.8 36.5 %collective-permute-start.5 = (bf16[12,72,192]{2,1,0:T(8,128)(2,1)}, bf16[12,72,192]{2,1,0:T(8,128)(2,1)S(1)}, u32[]{:S(2)}, u32[]{:S(2)}) collective-permute-start(bf16[12,72,192]{2,1,0:T(8,128)(2,1)} %get-tuple-element.120), channel_id=1, source_target_pairs={{4,0},{8,4},{12,8},{16,12},{20,16},{24,20},{28,24},{5,1},{9,5},{13... | collective-permute-start | bytes 995336 | tf_op jit(solution)/shard_map/ppermute | solution.py:1207
  200.3 0.8 copy-start.6
  200.3 0.9 copy-start.7
  235.3 0.8 copy-start
  235.3 0.9 copy-start.1

commit v3 on v2

--- a/solution.py
+++ b/solution.py
@@ -33,8 +33,10 @@
 rate_table = (0.2, 1.0, 0.2, 0.2, 0.2, 0.2, 0.2, 1.0, 1.0)
 decay_table = (0.1, 0.1, 0.1, 0.1, 0.1, 0.1, 0.1, 0.0, 0.0)
 
-VMEM_BYTES = 56 * 1024 * 1024
-OFFSET = 1
+VMEM_BYTES = 60 * 1024 * 1024
+OFFSET = 0
+COLUMNS = 4
+XW = 256
 
 
 def dot(a, b):
@@ -66,6 +68,10 @@
     center = x - jnp.mean(x, axis=-1, keepdims=True)
     rstd = lax.rsqrt(jnp.mean(center * center, axis=-1, keepdims=True) + 1e-05)
     return center * rstd, rstd
+
+
+def with_rstd(xhat, rstd):
+    return jnp.concatenate([xhat, jnp.broadcast_to(rstd, (xhat.shape[0], XW - C))], axis=1)
 
 
 def norm_back(dy, xhat, rstd, gain):
@@ -262,38 +268,101 @@
 FLAT_ZERO = 19 * C + 64
 
 
-def forward_zero(
-    columns,
-    sample,
-    step_ref,
-    an_ref,
-    lead_ref,
-    embed_ref,
-    qkv_ref,
-    proj_ref,
-    up_ref,
-    down_ref,
-    norm_ref,
-    x0_ref,
-    r0_ref,
-    pack_ref,
-    probs_ref,
-    mix_ref,
-    x1_ref,
-    r1_ref,
-    act_ref,
-    slope_ref,
-    h1_ref,
-    top_ref,
-    bot_ref,
-    wembed,
-    wqkv,
-    wproj,
-    wup,
-    wdown,
-):
-    @pl.when(pl.program_id(0) == 0)
+class Edges:
+    def __init__(self, count, per_step, low_ref, high_ref, from_low_ref, from_high_ref, sems):
+        self.at, self.count, self.per_step = lax.axis_index("lat"), count, per_step
+        self.staged = (low_ref, high_ref)
+        self.landing = (from_low_ref, from_high_ref)
+        self.send_low, self.send_high, self.recv_low, self.recv_high, self.fill = sems
+        self.has_low, self.has_high = self.at > 0, self.at < count - 1
+
+    def greet(self):
+        barrier = pltpu.get_barrier_semaphore()
+
+        @pl.when(self.has_low)
+        def _():
+            pl.semaphore_signal(barrier, inc=1, device_id={"lat": self.at - 1}, device_id_type=pl.DeviceIdType.MESH)
+
+        @pl.when(self.has_high)
+        def _():
+            pl.semaphore_signal(barrier, inc=1, device_id={"lat": self.at + 1}, device_id_type=pl.DeviceIdType.MESH)
+
+    def met(self):
+        there = jnp.where(self.has_low, 1, 0) + jnp.where(self.has_high, 1, 0)
+        pl.semaphore_wait(pltpu.get_barrier_semaphore(), there)
+
+    def copies(self, step):
+        part = pl.ds(step * self.per_step, self.per_step)
+        down = pltpu.make_async_remote_copy(
+            src_ref=self.staged[0].at[part],
+            dst_ref=self.landing[1].at[part],
+            send_sem=self.send_low.at[step],
+            recv_sem=self.recv_high.at[step],
+            device_id={"lat": self.at - 1},
+            device_id_type=pl.DeviceIdType.MESH,
+        )
+        up = pltpu.make_async_remote_copy(
+            src_ref=self.staged[1].at[part],
+            dst_ref=self.landing[0].at[part],
+            send_sem=self.send_high.at[step],
+            recv_sem=self.recv_low.at[step],
+            device_id={"lat": self.at + 1},
+            device_id_type=pl.DeviceIdType.MESH,
+        )
+        return down, up
+
+    def send(self, step):
+        down, up = self.copies(step)
+        pl.when(self.has_low)(down.start)
+        pl.when(self.has_high)(up.start)
+
+    def finish(self, steps, zero_ref):
+        zero_ref[...] = jnp.zeros_like(zero_ref)
+        for step in range(steps):
+            down, up = self.copies(step)
+            part = pl.ds(step * self.per_step, self.per_step)
+
+            def low_there(down=down, up=up):
+                down.wait_send()
+                up.wait_recv()
+
+            def high_there(down=down, up=up):
+                up.wait_send()
+                down.wait_recv()
+
+            pl.when(self.has_low)(low_there)
+            pl.when(self.has_high)(high_there)
+
+            def fill(side, part=part):
+                copy = pltpu.make_async_copy(zero_ref, self.landing[side].at[part], self.fill)
+                copy.start()
+                copy.wait()
+
+            pl.when(jnp.logical_not(self.has_low))(partial(fill, 0))
+            pl.when(jnp.logical_not(self.has_high))(partial(fill, 1))
+
+
+def edge_scratch(count, columns):
+    steps = count // columns
+    return [low(count, HALF, C), low(count, HALF, C), low(columns, HALF, C)] + [
+        pltpu.SemaphoreType.DMA((steps,)) for _ in range(4)
+    ] + [pltpu.SemaphoreType.DMA]
+
+
+EDGE_SCRATCH = 8
+ANYWHERE = pl.BlockSpec(memory_space=pl.ANY)
+
+
+def forward_zero(columns, count, bands, *refs):
+    an_ref, hot_ref, lead_ref, embed_ref, qkv_ref, proj_ref, up_ref, down_ref, norm_ref = refs[:9]
+    x0_ref, pack_ref, probs_ref, mix_ref, x1_ref, act_ref, slope_ref, h1_ref, from_low_ref, from_high_ref = refs[9:19]
+    wembed, wqkv, wproj, wup, wdown, top_ref, bot_ref, zero_ref, *sems = refs[19:]
+    step = pl.program_id(0)
+    edges = Edges(bands, columns, top_ref, bot_ref, from_low_ref, from_high_ref, sems)
+
+    @pl.when(step == 0)
     def _():
+        edges.greet()
         wembed[...] = embed_ref[...].astype(BF)
         wqkv[...] = qkv_ref[0].astype(BF)
         wproj[...] = proj_ref[0].astype(BF)
@@ -302,14 +371,13 @@
 
     masks = head_masks()
     masks32 = [m.astype(F32) for m in masks]
-    lead_row = lead_ref[pl.ds(step_ref[sample] - 1, 1), :]
+    lead_row = jnp.sum(hot_ref[0, 0:LEADS] * lead_ref[...], axis=0, keepdims=True)
 
     def one(col):
         hidden = dot_nt(an_ref[col], wembed[...]) + lead_row
         yield 1
         xhat, rstd = norm_stats(hidden)
-        x0_ref[col] = xhat
-        r0_ref[col] = rstd
+        x0_ref[col] = with_rstd(xhat, rstd)
         normed = (xhat * norm_ref[0, 0:1] + norm_ref[0, 1:2]).astype(BF)
         yield 1
         packed = dot(normed, wqkv[...]).astype(BF)
@@ -327,8 +395,7 @@
         hidden_two = hidden + dot(mixture, wproj[...])
         yield 1
         xhat, rstd = norm_stats(hidden_two)
-        x1_ref[col] = xhat
-        r1_ref[col] = rstd
+        x1_ref[col] = with_rstd(xhat, rstd)
         normed_two = (xhat * norm_ref[1, 0:1] + norm_ref[1, 1:2]).astype(BF)
         yield 1
         yield from feed_forward(normed_two, wup, act_ref.at[col], slope_ref.at[col])
@@ -337,10 +404,20 @@
         yield 1
         xhat, _ = norm_stats(jnp.concatenate([hidden_one[0:HALF], hidden_one[COL - HALF :]], axis=0))
         normed = xhat * norm_ref[2, 0:1] + norm_ref[2, 1:2]
-        top_ref[col] = normed[0:HALF].astype(BF)
-        bot_ref[col] = normed[HALF:].astype(BF)
+        top_ref[step * columns + col] = normed[0:HALF].astype(BF)
+        bot_ref[step * columns + col] = normed[HALF:].astype(BF)
 
     drive([one(col) for col in range(columns)], OFFSET)
+
+    @pl.when(step == 0)
+    def _():
+        edges.met()
+
+    edges.send(step)
+
+    @pl.when(step == pl.num_programs(0) - 1)
+    def _():
+        edges.finish(count // columns, zero_ref)
 
 
 def feed_forward(normed_two, wup, act_ref, slope_ref):
@@ -398,56 +475,23 @@
     return jnp.concatenate([ref[0:64], ref[216:280], ref[64:72], ref[280:288], ref[72:216]], axis=0)
 
 
-def middle(columns, count, first, *refs):
-    (
-        flag_ref,
-        h1_ref,
-        up_in_ref,
-        down_in_ref,
-        target_ref,
-        mask_ref,
-        qkv_ref,
-        proj_ref,
-        up_ref,
-        down_ref,
-        decode_ref,
-        norm_ref,
-        scale_ref,
-    ) = refs[:13]
-    refs = refs[13:]
-    if not first:
-        prev_ref, refs = refs[0], refs[1:]
-    (
-        dh2_ref,
-        dn_ref,
-        x2_ref,
-        r2_ref,
-        dtop_ref,
-        dbot_ref,
-        flat_ref,
-        wqkv,
-        wproj,
-        wup,
-        wdown,
-        wdec,
-        probs_ref,
-        act_ref,
-        slope_ref,
-        du_ref,
-        gqkv_ref,
-        gproj_ref,
-        gup_ref,
-        gdown_ref,
-        gdec_ref,
-        gnorm_ref,
-        gscale_ref,
-    ) = refs[:23]
-    kept = {name: ref for (name, _, _), ref in zip(MIDDLE_KEEP, refs[23:])}
-    sums = (gqkv_ref, gproj_ref, gup_ref, gdown_ref, gdec_ref, gnorm_ref, gscale_ref)
+def middle(columns, count, bands, *refs):
+    flag_ref, h1_ref, up_in_ref, down_in_ref, target_ref, mask_ref = refs[:6]
+    qkv_ref, proj_ref, up_ref, down_ref, decode_ref, norm_ref, scale_ref = refs[6:13]
+    grad_ref, dhe_ref, dne_ref, xe_ref, part_ref, flat_ref, from_low_ref, from_high_ref = refs[13:21]
+    dtop_ref, dbot_ref, zero_ref, *sems = refs[21 : 21 + EDGE_SCRATCH]
+    refs = refs[21 + EDGE_SCRATCH :]
+    wqkv, wproj, wup, wdown, wdec, probs_ref, act_ref, slope_ref, du_ref = refs[:9]
+    sums = refs[9:16]
+    gqkv_ref, gproj_ref, gup_ref, gdown_ref, gdec_ref, gnorm_ref, gscale_ref = sums
+    kept = {name: ref for (name, _, _), ref in zip(MIDDLE_KEEP, refs[16:])}
     step = pl.program_id(0)
+    group = group_of(count // columns)
+    edges = Edges(bands, columns, dtop_ref, dbot_ref, from_low_ref, from_high_ref, sems)
 
     @pl.when(step == 0)
     def _():
+        edges.greet()
         wqkv[...] = qkv_ref[0].astype(BF)
         wproj[...] = proj_ref[0].astype(BF)
         wup[...] = up_ref[0].astype(BF)
@@ -464,7 +508,7 @@
     def one(col):
         def keep(name, value):
             rows = value.shape[0]
-            at = pl.multiple_of((step * columns + col) * rows, 16)
+            at = pl.multiple_of((lax.rem(step, group) * columns + col) * rows, 16)
             kept[name][pl.ds(at, rows), :] = value
 
         act, slope, du = act_ref.at[col], slope_ref.at[col], du_ref.at[col]
@@ -528,21 +572,15 @@
         add_norm_grads(gnorm_ref, 1, dnorm, xhat_two)
         grad = grad + norm_back(dnorm, xhat_two, rstd_two, norm_ref[3, 0:1])
         grad_low = grad.astype(BF)
-        dh2_ref[col, 0:64] = grad[0:64]
-        dh2_ref[col, 64:72] = grad[128:136]
-        dh2_ref[col, 72:216] = grad[144:288]
-        dh2_ref[col, 216:280] = grad[64:128]
-        dh2_ref[col, 280:288] = grad[136:144]
-        x2_ref[col, 0:64] = xhat_one[0:64]
-        x2_ref[col, 64:72] = xhat_one[128:136]
-        x2_ref[col, 72:216] = xhat_one[144:288]
-        x2_ref[col, 216:280] = xhat_one[64:128]
-        x2_ref[col, 280:288] = xhat_one[136:144]
-        r2_ref[col, 0:64] = rstd_one[0:64]
-        r2_ref[col, 64:72] = rstd_one[128:136]
-        r2_ref[col, 72:216] = rstd_one[144:288]
-        r2_ref[col, 216:280] = rstd_one[64:128]
-        r2_ref[col, 280:288] = rstd_one[136:144]
+        dhe_ref[col, 0:64] = grad[0:64]
+        dhe_ref[col, 64:72] = grad[128:136]
+        dhe_ref[col, 72:136] = grad[64:128]
+        dhe_ref[col, 136:144] = grad[136:144]
+        kept_edge = with_rstd(xhat_one[0:WIN], rstd_one[0:WIN])
+        xe_ref[col, 0:64] = kept_edge[0:64]
+        xe_ref[col, 64:72] = kept_edge[128:136]
+        xe_ref[col, 72:136] = kept_edge[64:128]
+        xe_ref[col, 136:144] = kept_edge[136:144]
         yield 1
         dmix = dot_nt(grad_low, wproj[...]).astype(BF)
         yield 1
@@ -565,15 +603,18 @@
         dkv = jnp.concatenate([dk, dv], axis=1)
         yield 1
         dn_kv = dot_nt(dkv, wqkv[:, C:])
-        dtop_ref[col] = dn_kv[0:HALF].astype(BF)
-        dbot_ref[col] = dn_kv[WIN : WIN + HALF].astype(BF)
+        dtop_ref[step * columns + col] = dn_kv[0:HALF].astype(BF)
+        dbot_ref[step * columns + col] = dn_kv[WIN : WIN + HALF].astype(BF)
         yield 1
         dn_q = dot_nt(dq, wqkv[:, 0:C])
-        dn_ref[col, 0:64] = dn_q[0:64] + dn_kv[72:136]
-        dn_ref[col, 64:72] = dn_q[128:136] + dn_kv[136:144]
-        dn_ref[col, 72:216] = dn_q[144:288] + dn_kv[288:432]
-        dn_ref[col, 216:280] = dn_q[64:128] + dn_kv[216:280]
-        dn_ref[col, 280:288] = dn_q[136:144] + dn_kv[280:288]
+        yield 1
+        dne_ref[col, 0:64] = dn_q[0:64] + dn_kv[72:136]
+        dne_ref[col, 64:72] = dn_q[128:136] + dn_kv[136:144]
+        dne_ref[col, 72:136] = dn_q[64:128] + dn_kv[216:280]
+        dne_ref[col, 136:144] = dn_q[136:144] + dn_kv[280:288]
+        dnorm = dn_q[WIN:] + dn_kv[2 * WIN :]
+        add_norm_grads(gnorm_ref, 0, dnorm, xhat_one[WIN:])
+        grad_ref[col] = grad[WIN:] + norm_back(dnorm, xhat_one[WIN:], rstd_one[WIN:], norm_ref[2, 0:1])
         yield 1
         gqkv_ref[:, 0:C] += dot_tn(normed_low[0:256], dq[0:256])
         yield 1
@@ -585,7 +626,13 @@
 
     drive([one(col) for col in range(columns)], OFFSET)
 
-    @pl.when(step == pl.num_programs(0) - 1)
+    @pl.when(step == 0)
+    def _():
+        edges.met()
+
+    edges.send(step)
+
+    @pl.when(lax.rem(step, group) == group - 1)
     def _():
         gup_ref[...] += dot_tn(kept["n2"][...], kept["du"][...])
         gdown_ref[...] += dot_tn(kept["dm"][...], kept["act"][...])
@@ -593,15 +640,19 @@
         gqkv_ref[:, 0:C] += dot_tn(kept["n"][...], kept["dq"][...])
         gqkv_ref[:, C:] += dot_tn(kept["nkv"][...], kept["dkv"][...])
         gdec_ref[...] += dot_tn(kept["last"][...], kept["dp"][...])
+
+    @pl.when(step == pl.num_programs(0) - 1)
+    def _():
         store_qkv_proj(flat_ref, 0, gqkv_ref, gproj_ref)
         store_wide(flat_ref, 6 * C, gup_ref, FF)
         store_wide(flat_ref, 12 * C, gdown_ref, FF)
         flat_ref[18 * C : 19 * C] = gdec_ref[...]
+        part_ref[...] = gnorm_ref[...]
+        gnorm_ref[0:2] = jnp.zeros((2, C), F32)
         store_narrow(flat_ref, 19 * C, gnorm_ref, 8)
         flat_ref[19 * C + 16 : 19 * C + 24] = gscale_ref[...]
         clear_from(flat_ref, FLAT_MIDDLE)
-        if not first:
-            flat_ref[...] += prev_ref[...]
+        edges.finish(count // columns, zero_ref)
 
 
 ZERO_KEEP = (
@@ -618,18 +669,16 @@
 )
 
 
-def backward_zero(columns, count, first, sample, *refs):
-    step_ref, an_ref, x0_ref, r0_ref, pack_ref, probs_ref, mix_ref, x1_ref, r1_ref, act_ref, slope_ref = refs[:11]
-    dh2_ref, dn_ref, x2_ref, r2_ref, ret_top_ref, ret_bot_ref = refs[11:17]
-    qkv_ref, proj_ref, up_ref, down_ref, norm_ref = refs[17:22]
-    refs = refs[22:]
-    if not first:
-        prev_ref, refs = refs[0], refs[1:]
-    flat_ref, wqkv, wproj, wup, wdown, du_ref = refs[:6]
-    sums = refs[6:13]
+def backward_zero(columns, count, *refs):
+    an_ref, hot_ref, x0_ref, pack_ref, probs_ref, mix_ref, x1_ref, act_ref, slope_ref = refs[:9]
+    grad_in_ref, dhe_ref, dne_ref, xe_ref, part_ref, from_low_ref, from_high_ref = refs[9:16]
+    qkv_ref, proj_ref, up_ref, down_ref, norm_ref = refs[16:21]
+    flat_ref, wqkv, wproj, wup, wdown, du_ref = refs[21:27]
+    sums = refs[27:34]
     gembed_ref, glead_ref, gqkv_ref, gproj_ref, gup_ref, gdown_ref, gnorm_ref = sums
-    kept = {name: ref for (name, _, _), ref in zip(ZERO_KEEP, refs[13:])}
+    kept = {name: ref for (name, _, _), ref in zip(ZERO_KEEP, refs[34:])}
     step = pl.program_id(0)
+    group = group_of(count // columns)
 
     @pl.when(step == 0)
     def _():
@@ -642,28 +691,21 @@
 
     masks = head_masks()
     masks32 = [m.astype(F32) for m in masks]
-    lead_at = pl.ds(step_ref[sample] - 1, 1)
 
     def one(col):
         def keep(name, value):
             rows = value.shape[0]
-            at = pl.multiple_of((step * columns + col) * rows, 16)
+            at = pl.multiple_of((lax.rem(step, group) * columns + col) * rows, 16)
             kept[name][pl.ds(at, rows), :] = value
 
-        dn = jnp.concatenate(
-            [
-                dn_ref[col, 0:HALF] + ret_top_ref[col].astype(F32),
-                dn_ref[col, HALF : COL - HALF],
-                dn_ref[col, COL - HALF :] + ret_bot_ref[col].astype(F32),
-            ],
-            axis=0,
-        )
-        xhat = x2_ref[col]
+        dn = dne_ref[col] + jnp.concatenate([from_low_ref[col], from_high_ref[col]], axis=0).astype(F32)
+        xhat = xe_ref[col, :, 0:C]
         add_norm_grads(gnorm_ref, 2, dn, xhat)
-        grad = dh2_ref[col] + norm_back(dn, xhat, r2_ref[col], norm_ref[2, 0:1])
+        edge = dhe_ref[col] + norm_back(dn, xhat, xe_ref[col, :, C : C + 1], norm_ref[2, 0:1])
+        grad = jnp.concatenate([edge[0:HALF], grad_in_ref[col], edge[HALF:]], axis=0)
         grad_low = grad.astype(BF)
         yield 1
-        xhat = x1_ref[col]
+        xhat = x1_ref[col, :, 0:C]
         normed_two = (xhat * norm_ref[1, 0:1] + norm_ref[1, 1:2]).astype(BF)
         yield 1
         yield from feed_backward(
@@ -672,7 +714,7 @@
         dnorm = dot_nt(du_ref[col], wup[...])
         yield 1
         add_norm_grads(gnorm_ref, 1, dnorm, xhat)
-        grad = grad + norm_back(dnorm, xhat, r1_ref[col], norm_ref[1, 0:1])
+        grad = grad + norm_back(dnorm, xhat, x1_ref[col, :, C : C + 1], norm_ref[1, 0:1])
         grad_low = grad.astype(BF)
         yield 1
         dmix = dot_nt(grad_low, wproj[...]).astype(BF)
@@ -701,15 +743,15 @@
         yield 1
         dn = dot_nt(dpacked, wqkv[...])
         yield 1
-        xhat = x0_ref[col]
+        xhat = x0_ref[col, :, 0:C]
         normed = (xhat * norm_ref[0, 0:1] + norm_ref[0, 1:2]).astype(BF)
         gqkv_ref[...] += dot_tn(normed[0:256], dpacked[0:256])
         keep("n", normed[256:])
         keep("dp", dpacked[256:])
         yield 1
         add_norm_grads(gnorm_ref, 0, dn, xhat)
-        grad = grad + norm_back(dn, xhat, r0_ref[col], norm_ref[0, 0:1])
-        glead_ref[lead_at, :] += jnp.sum(grad, axis=0, keepdims=True)
+        grad = grad + norm_back(dn, xhat, x0_ref[col, :, C : C + 1], norm_ref[0, 0:1])
+        glead_ref[...] += hot_ref[0] * jnp.sum(grad, axis=0, keepdims=True)
         grad_low = grad.astype(BF)
         yield 1
         gembed_ref[...] += dot_tn(grad_low[0:256], an_ref[col, 0:256])
@@ -718,13 +760,17 @@
 
     drive([one(col) for col in range(columns)], OFFSET)
 
-    @pl.when(step == pl.num_programs(0) - 1)
+    @pl.when(lax.rem(step, group) == group - 1)
     def _():
         gup_ref[...] += dot_tn(kept["n2"][...], kept["du"][...])
         gdown_ref[...] += dot_tn(kept["dm"][...], kept["act"][...])
         gproj_ref[...] += dot_tn(kept["mix"][...], kept["da"][...])
         gqkv_ref[...] += dot_tn(kept["n"][...], kept["dp"][...])
         gembed_ref[...] += dot_tn(kept["dh"][...], kept["an"][...])
+
+    @pl.when(step == pl.num_programs(0) - 1)
+    def _():
+        gnorm_ref[4:6] += part_ref[0:2]
         store_qkv_proj(flat_ref, 0, gqkv_ref, gproj_ref)
         store_wide(flat_ref, 6 * C, gup_ref, FF)
         store_wide(flat_ref, 12 * C, gdown_ref, FF)
@@ -732,8 +778,6 @@
         store_narrow(flat_ref, 19 * C, gnorm_ref, 8)
         store_narrow(flat_ref, 19 * C + 16, glead_ref, 24)
         clear_from(flat_ref, FLAT_ZERO)
-        if not first:
-            flat_ref[...] += prev_ref[...]
 
 
 def exchanges(sizes):
@@ -1049,32 +1093,34 @@
     return pltpu.VMEM(shape, F32)
 
 
-def kept_scratch(kept, count):
-    return [low(count * rows, width) for _, rows, width in kept]
-
-
-def run_forward(lead_step, tokens, lead_table, embed_t, qkv_w, proj_w, up_w, down_t, norm_t, sample, count, columns):
+def group_of(steps):
+    return 2 if steps % 2 == 0 else 1
+
+
+def kept_scratch(kept, count, columns):
+    held = group_of(count // columns) * columns
+    return [low(held * rows, width) for _, rows, width in kept]
+
+
+def run_forward(tokens, hot, lead_table, embed_t, qkv_w, proj_w, up_w, down_t, norm_t, bands, per_sample, columns):
+    count = tokens.shape[0]
     steps = count // columns
     outs = [
-        ((count, COL, C), F32),
-        ((count, COL, 1), F32),
+        ((count, COL, XW), F32),
         ((count, COL, 3 * C), BF),
         ((count, 2, WIN, LANES), F32),
         ((count, COL, C), BF),
-        ((count, COL, C), F32),
-        ((count, COL, 1), F32),
+        ((count, COL, XW), F32),
         ((count, COL, FF), BF),
         ((count, COL, FF), F32),
         ((count, COL, C), F32),
-        ((count, HALF, C), BF),
-        ((count, HALF, C), BF),
     ]
     return pl.pallas_call(
-        partial(forward_zero, columns, sample),
+        partial(forward_zero, columns, count, bands),
         grid=(steps,),
         in_specs=[
-            SMEM,
-            rows_of(columns, sample * steps, COL, CIN),
+            rows(columns, COL, CIN),
+            hot_spec(per_sample // columns),
             whole((LEADS, C)),
             whole((C, CIN)),
             layer((C, 3 * C), 0),
@@ -1083,35 +1129,33 @@
             layer((C, FF), 0),
             whole((5, 2, C)),
         ],
-        out_specs=[rows(columns, *shape[1:]) for shape, _ in outs],
-        out_shape=[struct(*o) for o in outs],
-        scratch_shapes=[low(C, CIN), low(C, 3 * C), low(C, C), low(C, FF), low(C, FF)],
-        compiler_params=pltpu.CompilerParams(vmem_limit_bytes=VMEM_BYTES),
+        out_specs=[rows(columns, *shape[1:]) for shape, _ in outs] + [ANYWHERE] * 2,
+        out_shape=[struct(*o) for o in outs] + [struct((count, HALF, C), BF)] * 2,
+        scratch_shapes=[low(C, CIN), low(C, 3 * C), low(C, C), low(C, FF), low(C, FF)] + edge_scratch(count, columns),
+        compiler_params=pltpu.CompilerParams(vmem_limit_bytes=VMEM_BYTES, collective_id=1, has_side_effects=True),
         name="forward_zero",
-    )(lead_step, tokens, lead_table, embed_t, qkv_w, proj_w, up_w, down_t, norm_t)
-
-
-def run_middle(flags, h1, up_in, down_in, target, cells, qkv_w, proj_w, up_w, down_t, decode_w, norm_t, scale, prev, flat_rows, sample, count, columns):
+    )(tokens, hot, lead_table, embed_t, qkv_w, proj_w, up_w, down_t, norm_t)
+
+
+def run_middle(flags, h1, up_in, down_in, target, cells, qkv_w, proj_w, up_w, down_t, decode_w, norm_t, scale, flat_rows, bands, columns):
+    count = h1.shape[0]
     steps = count // columns
     outs = [
-        ((count, COL, C), F32),
-        ((count, COL, C), F32),
-        ((count, COL, C), F32),
-        ((count, COL, 1), F32),
-        ((count, HALF, C), BF),
-        ((count, HALF, C), BF),
+        ((count, WIN, C), F32),
+        ((count, WIN, C), F32),
+        ((count, WIN, C), F32),
+        ((count, WIN, XW), F32),
     ]
-    first = prev is None
     return pl.pallas_call(
-        partial(middle, columns, count, first),
+        partial(middle, columns, count, bands),
         grid=(steps,),
         in_specs=[
             SMEM,
             rows(columns, COL, C),
             rows(columns, HALF, C),
             rows(columns, HALF, C),
-            rows_of(columns, sample * steps, COL, CIN),
-            rows_of(columns, sample * steps, 8, COL),
+            rows(columns, COL, CIN),
+            rows(columns, 8, COL),
             layer((C, 3 * C), 1),
             layer((C, C), 1),
             layer((C, FF), 1),
@@ -1119,11 +1163,14 @@
             whole((C, CIN)),
             whole((5, 2, C)),
             whole((1, CIN)),
-        ]
-        + ([] if first else [whole((flat_rows, 128))]),
-        out_specs=[rows(columns, *shape[1:]) for shape, _ in outs] + [whole((flat_rows, 128))],
-        out_shape=[struct(*o) for o in outs] + [struct((flat_rows, 128), F32)],
-        scratch_shapes=[
+        ],
+        out_specs=[rows(columns, *shape[1:]) for shape, _ in outs]
+        + [whole((8, C)), whole((flat_rows, 128)), ANYWHERE, ANYWHERE],
+        out_shape=[struct(*o) for o in outs]
+        + [struct((8, C), F32), struct((flat_rows, 128), F32)]
+        + [struct((count, HALF, C), BF)] * 2,
+        scratch_shapes=edge_scratch(count, columns)
+        + [
             low(C, 3 * C),
             low(C, C),
             low(C, FF),
@@ -1141,34 +1188,33 @@
             full(8, C),
             full(8, CIN),
         ]
-        + kept_scratch(MIDDLE_KEEP, count),
-        compiler_params=pltpu.CompilerParams(vmem_limit_bytes=VMEM_BYTES),
+        + kept_scratch(MIDDLE_KEEP, count, columns),
+        compiler_params=pltpu.CompilerParams(vmem_limit_bytes=VMEM_BYTES, collective_id=2, has_side_effects=True),
         name="middle",
-    )(flags, h1, up_in, down_in, target, cells, qkv_w, proj_w, up_w, down_t, decode_w, norm_t, scale, *([] if first else [prev]))
-
-
-def run_backward(lead_step, tokens, saved, mid_out, returned, qkv_w, proj_w, up_w, down_t, norm_t, prev, flat_rows, sample, count, columns):
+    )(flags, h1, up_in, down_in, target, cells, qkv_w, proj_w, up_w, down_t, decode_w, norm_t, scale)
+
+
+def run_backward(tokens, hot, saved, mid_out, qkv_w, proj_w, up_w, down_t, norm_t, flat_rows, per_sample, columns):
+    count = tokens.shape[0]
     steps = count // columns
-    first = prev is None
     return pl.pallas_call(
-        partial(backward_zero, columns, count, first, sample),
+        partial(backward_zero, columns, count),
         grid=(steps,),
         in_specs=[
-            SMEM,
-            rows_of(columns, sample * steps, COL, CIN),
-            rows(columns, COL, C),
-            rows(columns, COL, 1),
+            rows(columns, COL, CIN),
+            hot_spec(per_sample // columns),
+            rows(columns, COL, XW),
             rows(columns, COL, 3 * C),
             rows(columns, 2, WIN, LANES),
             rows(columns, COL, C),
-            rows(columns, COL, C),
-            rows(columns, COL, 1),
+            rows(columns, COL, XW),
             rows(columns, COL, FF),
             rows(columns, COL, FF),
-            rows(columns, COL, C),
-            rows(columns, COL, C),
-            rows(columns, COL, C),
-            rows(columns, COL, 1),
+            rows(columns, WIN, C),
+            rows(columns, WIN, C),
+            rows(columns, WIN, C),
+            rows(columns, WIN, XW),
+            whole((8, C)),
             rows(columns, HALF, C),
             rows(columns, HALF, C),
             layer((C, 3 * C), 0),
@@ -1176,8 +1222,7 @@
             layer((C, FF), 0),
             layer((C, FF), 0),
             whole((5, 2, C)),
-        ]
-        + ([] if first else [whole((flat_rows, 128))]),
+        ],
         out_specs=whole((flat_rows, 128)),
         out_shape=struct((flat_rows, 128), F32),
         scratch_shapes=[
@@ -1194,17 +1239,14 @@
             full(C, FF),
             full(8, C),
         ]
-        + kept_scratch(ZERO_KEEP, count),
+        + kept_scratch(ZERO_KEEP, count, columns),
         compiler_params=pltpu.CompilerParams(vmem_limit_bytes=VMEM_BYTES),
         name="backward_zero",
-    )(lead_step, tokens, *saved, *mid_out, *returned, qkv_w, proj_w, up_w, down_t, norm_t, *([] if first else [prev]))
-
-
-def neighbours(low, high):
-    count = lax.axis_size("lat")
-    forward = [(i, i + 1) for i in range(count - 1)]
-    backward = [(b, a) for a, b in forward]
-    return lax.ppermute(high, "lat", forward), lax.ppermute(low, "lat", backward)
+    )(tokens, hot, *saved, *mid_out, qkv_w, proj_w, up_w, down_t, norm_t)
+
+
+def hot_spec(steps):
+    return pl.BlockSpec((1, 24, 1), lambda i: (i // steps, 0, 0))
 
 
 def views(group):
@@ -1228,31 +1270,22 @@
     cells = jnp.pad(cells, ((0, 0), (0, 7), (0, 0)))
     at = lax.axis_index("lat")
     flags = jnp.stack([jnp.where(at > 0, 0.0, -1e30), jnp.where(at < sizes["lat"] - 1, 0.0, -1e30)]).astype(F32)
-    columns = 2 if blocks % 2 == 0 else 1
+    columns = next(c for c in (COLUMNS, 3, 2, 1) if blocks % c == 0)
     unit = 8 * sizes["lat"] * sizes["batch"]
     flat_rows = -(-max(FLAT_MIDDLE, FLAT_ZERO) // unit) * unit
-
-    forward = [
-        run_forward(lead_step, tokens, lead_table, embed_t, qkv_w, proj_w, up_w, down_t, norm_t, s, blocks, columns)
-        for s in range(samples)
-    ]
-    edges = [neighbours(f[10], f[11]) for f in forward]
-    mid = None
-    mids = []
-    for s in range(samples):
-        up_in, down_in = edges[s]
-        *out, mid = run_middle(
-            flags, forward[s][9], up_in, down_in, truth, cells, qkv_w, proj_w, up_w, down_t, decode_w, norm_t, scale,
-            mid, flat_rows, s, blocks, columns,
-        )
-        mids.append(out)
-    returned = [neighbours(m[4], m[5]) for m in mids]
-    zero = None
-    for s in range(samples):
-        zero = run_backward(
-            lead_step, tokens, forward[s][:9], mids[s][:4], returned[s], qkv_w, proj_w, up_w, down_t, norm_t,
-            zero, flat_rows, s, blocks, columns,
-        )
+    hot = (jnp.arange(24, dtype=jnp.int32)[None, :, None] == lead_step[:, None, None] - 1).astype(F32)
+
+    *saved, h1, from_low, from_high = run_forward(
+        tokens, hot, lead_table, embed_t, qkv_w, proj_w, up_w, down_t, norm_t, sizes["lat"], blocks, columns
+    )
+    *edge_out, part, mid, back_low, back_high = run_middle(
+        flags, h1, from_low, from_high, truth, cells, qkv_w, proj_w, up_w, down_t, decode_w, norm_t, scale,
+        flat_rows, sizes["lat"], columns,
+    )
+    zero = run_backward(
+        tokens, hot, saved, (*edge_out, part, back_low, back_high), qkv_w, proj_w, up_w, down_t, norm_t,
+        flat_rows, blocks, columns,
+    )
     if unit > 8:
         mid, zero = run_all_sum([mid, zero], sizes)
     news, moments, squares, small = run_update(mid, zero, weights, firsts, seconds)

time: 353 us -> 285 us (0.81); the launches traced: 347 us -> 285 us
  Pallas kernels: 313 us -> 278 us
  starting transfers between devices: 25.8 us -> 0 us
  local copies, waits for them, and re-layouts: 6.22 us -> 2.67 us
    pallas_call x6 -> x3, Pallas kernels: 239 us -> 204 us  [the longest x1 96.9 us: run_middle(): pl.pallas_call(partial(middle, columns, count, bands), grid=(steps,), in_...]
    ppermute x8 -> x0, starting transfers between devices: 25.8 us -> none  [the longest x4 19.8 us: neighbours(): lax.ppermute(high, 'lat', forward)]
    unnamed x18 -> x0, local copies, waits for them, and re-layouts: 3.55 us -> none
  transfers between devices with their start and end apart: 8 -> 0, of which waited for: 0 -> 0; matrix products, arithmetic and copies ran while one was open for 1% -> 0% of each run, Pallas kernels for 50% -> 0%
where the time goes in v3:
time: 285 us
  Pallas kernels  278 us (98%)
  other arithmetic  2.99 us (1%)
    pallas_call x1, Pallas kernels, run_middle(): pl.pallas_call(partial(middle, columns, count, bands), grid=(steps,), in_...  96.9 us
    pallas_call x1, Pallas kernels, run_all_sum(): pl.pallas_call(partial(all_sum, streams, len(flats)), out_shape=[struct(f...  60.3 us
    pallas_call x1, Pallas kernels, run_backward(): pl.pallas_call(partial(backward_zero, columns, count), grid=(steps,), in_...  54.1 us
    pallas_call x1, Pallas kernels, run_forward(): pl.pallas_call(partial(forward_zero, columns, count, bands), grid=(steps,...  53.5 us
    pallas_call x1, Pallas kernels, run_update(): pl.pallas_call(partial(update, steps), grid=(steps,), in_specs=[whole(mid...  13.5 us

profile of v3, /device:TPU:0, one launch (start us, length us, event | category | flops | bytes accessed | tf_op | source)
XLA Modules:
  0.0 284.7 jit_solution(8372354608115194895)
XLA Ops:
  0.7 0.6 pad_maximum_fusion.refs_0_
  1.3 0.7 broadcast_add_fusion
  1.9 0.7 fusion.refs_1_
  2.6 1.1 convert_bitcast_fusion
  3.7 0.4 copy.62
  4.1 0.1 convert_element_type.25
  4.2 0.1 copy.63
  4.4 0.7 pad.4.refs_5_
  5.0 53.5 %forward_zero.1 = (f32[24,288,256]{2,1,0:T(8,128)}, bf16[24,288,576]{2,1,0:T(8,128)(2,1)}, f32[24,2,144,896]{3,2,1,0:T(8,128)}, bf16[24,288,192]{2,1,0:T(8,128)(...) custom-call(bf16[24,288,128]{2,1,0:T(8,128)(2,1)} %bitcast.43, ...), custom_call_target="tpu_custom_call" | custom-call | tf_op jit(solution)/shard_map/forward_zero/pallas_call | solution.py:1118
  58.6 96.9 %middle.1 = (f32[24,144,192]{2,1,0:T(8,128)}, f32[24,144,192]{2,1,0:T(8,128)}, f32[24,144,192]{2,1,0:T(8,128)}, f32[24,144,256]{2,1,0:T(8,128)}, f32[8,192]{1,0:...) custom-call(f32[2]{0:T(128)} %pad_maximum_fusion.refs_0_, ...), custom_call_target="tpu_custom_call" | custom-call | tf_op jit(solution)/shard_map/middle/pallas_call | solution.py:1149
  155.5 54.1 %backward_zero.1.refs_1_ = f32[3840,128]{1,0:T(8,128)} custom-call(bf16[24,288,128]{2,1,0:T(8,128)(2,1)} %bitcast.44, f32[2,24,1]{2,1,0:T(8,128)} %fusion.refs_1_, f32[24,288,256]{2,1,0:T(8,128)} %get-tuple-element.82.refs_2_, bf16[24,288,576]{2,1,0:T(8,128)(2,1)} %get-tuple-element.83.refs_3_, f32[24,2,144,896]{3,2,1,0:T(8,128)} %get-tuple-element.84.refs_4_, ...), custom_call_target="tpu_custom_call" | custom-call | tf_op jit(solution)/shard_map/backward_zero/pallas_call | solution.py:1200
  209.6 60.3 %all_sum.1 = (f32[3840,128]{1,0:T(8,128)}, f32[3840,128]{1,0:T(8,128)}) custom-call(f32[3840,128]{1,0:T(8,128)} %get-tuple-element.81.refs_0_, f32[3840,128]{1,0:T(8,128)} %backward_zero.1.refs_1_), custom_call_target="tpu_custom_call" | custom-call | tf_op jit(solution)/shard_map/all_sum/pallas_call | solution.py:930
  269.9 13.5 %update.1 = (f32[192,128]{1,0:T(8,128)}, f32[20,192]{1,0:T(8,128)}, f32[2,192,576]{2,1,0:T(8,128)}, f32[2,192,192]{2,1,0:T(8,128)}, f32[2,192,768]{2,1,0:T(8,128...) custom-call(f32[3840,128]{1,0:T(8,128)} %get-tuple-element.96.mid_re, ...), custom_call_target="tpu_custom_call" | custom-call | tf_op jit(solution)/shard_map/update/pallas_call | solution.py:1049
  283.4 1.3 fusion.1

commit v4 on v3

--- a/solution.py
+++ b/solution.py
@@ -33,8 +33,7 @@
 rate_table = (0.2, 1.0, 0.2, 0.2, 0.2, 0.2, 0.2, 1.0, 1.0)
 decay_table = (0.1, 0.1, 0.1, 0.1, 0.1, 0.1, 0.1, 0.0, 0.0)
 
-VMEM_BYTES = 60 * 1024 * 1024
-OFFSET = 0
+VMEM_BYTES = 61 * 1024 * 1024
 COLUMNS = 4
 XW = 256
 
@@ -51,17 +50,11 @@
     return lax.dot_general(a, b, (((0,), (0,)), ((), ())), preferred_element_type=F32)
 
 
-def drive(parts, offset):
-    live = [(at * offset, part) for at, part in enumerate(parts)]
-    tick = 0
+def drive(parts):
+    live = list(parts)
     while live:
-        left = []
-        for start, part in live:
-            if tick >= start and next(part, 0) == 0:
-                continue
-            left.append((start, part))
-        live = left
-        tick += 1
+        marks = [next(part, 0) for part in live]
+        live = [part for part, mark in zip(live, marks) if mark == 1]
 
 
 def norm_stats(x):
@@ -222,9 +215,9 @@
     parts, lows, dlows = [], [], []
     for at, (a, b) in enumerate(spans):
         dprobs = ahead
+        probs = probs_ref[:, a:b]
         if at + 1 < len(spans):
             ahead = score_chunk(vals, douts, edge, at + 1)
-        probs = probs_ref[:, a:b]
         row_terms = jnp.sum(dprobs * probs, axis=0, keepdims=True)
         dscores = (probs * (dprobs - row_terms)).astype(BF)
         lows.append(probs.astype(BF))
@@ -353,8 +346,13 @@
 ANYWHERE = pl.BlockSpec(memory_space=pl.ANY)
 
 
+def lead_hot(step_ref, step, steps):
+    sample = step // (steps // step_ref.shape[0])
+    return (lax.broadcasted_iota(jnp.int32, (24, 1), 0) == step_ref[sample] - 1).astype(F32)
+
+
 def forward_zero(columns, count, bands, *refs):
-    an_ref, hot_ref, lead_ref, embed_ref, qkv_ref, proj_ref, up_ref, down_ref, norm_ref = refs[:9]
+    step_ref, an_ref, lead_ref, embed_ref, qkv_ref, proj_ref, up_ref, down_ref, norm_ref = refs[:9]
     x0_ref, pack_ref, probs_ref, mix_ref, x1_ref, act_ref, slope_ref, h1_ref, from_low_ref, from_high_ref = refs[9:19]
     wembed, wqkv, wproj, wup, wdown, top_ref, bot_ref, zero_ref, *sems = refs[19:]
     step = pl.program_id(0)
@@ -371,7 +369,7 @@
 
     masks = head_masks()
     masks32 = [m.astype(F32) for m in masks]
-    lead_row = jnp.sum(hot_ref[0, 0:LEADS] * lead_ref[...], axis=0, keepdims=True)
+    lead_row = jnp.sum(lead_hot(step_ref, step, count // columns)[0:LEADS] * lead_ref[...], axis=0, keepdims=True)
 
     def one(col):
         hidden = dot_nt(an_ref[col], wembed[...]) + lead_row
@@ -386,6 +384,7 @@
         mixtures = []
         for w in range(2):
             part = packed[WIN * w : WIN * w + WIN]
+
             yield from attention_forward(
                 part[:, 0:C], part[:, C : 2 * C], part[:, 2 * C :], masks, masks32, False, probs_ref.at[col, w], mixtures
             )
@@ -407,7 +406,7 @@
         top_ref[step * columns + col] = normed[0:HALF].astype(BF)
         bot_ref[step * columns + col] = normed[HALF:].astype(BF)
 
-    drive([one(col) for col in range(columns)], OFFSET)
+    drive([one(col) for col in range(columns)])
 
     @pl.when(step == 0)
     def _():
@@ -475,16 +474,25 @@
     return jnp.concatenate([ref[0:64], ref[216:280], ref[64:72], ref[280:288], ref[72:216]], axis=0)
 
 
+def cell_selectors():
+    token = lax.broadcasted_iota(jnp.int32, (COL, 24), 0)
+    line = lax.broadcasted_iota(jnp.int32, (COL, 24), 1)
+    of_line = (token // 24 * 2 + token % 2 == line).astype(F32).astype(BF)
+    token = lax.broadcasted_iota(jnp.int32, (COL, 12), 0)
+    place = lax.broadcasted_iota(jnp.int32, (COL, 12), 1)
+    return of_line, (token % 24 // 2 == place).astype(F32)
+
+
 def middle(columns, count, bands, *refs):
-    flag_ref, h1_ref, up_in_ref, down_in_ref, target_ref, mask_ref = refs[:6]
-    qkv_ref, proj_ref, up_ref, down_ref, decode_ref, norm_ref, scale_ref = refs[6:13]
-    grad_ref, dhe_ref, dne_ref, xe_ref, part_ref, flat_ref, from_low_ref, from_high_ref = refs[13:21]
-    dtop_ref, dbot_ref, zero_ref, *sems = refs[21 : 21 + EDGE_SCRATCH]
-    refs = refs[21 + EDGE_SCRATCH :]
-    wqkv, wproj, wup, wdown, wdec, probs_ref, act_ref, slope_ref, du_ref = refs[:9]
-    sums = refs[9:16]
+    h1_ref, up_in_ref, down_in_ref, target_ref, mask_ref = refs[:5]
+    qkv_ref, proj_ref, up_ref, down_ref, decode_ref, norm_ref, scale_ref = refs[5:12]
+    grad_ref, dhe_ref, dne_ref, xe_ref, part_ref, flat_ref, from_low_ref, from_high_ref = refs[12:20]
+    dtop_ref, dbot_ref, zero_ref, *sems = refs[20 : 20 + EDGE_SCRATCH]
+    refs = refs[20 + EDGE_SCRATCH :]
+    wqkv, wproj, wup, wdown, wdec, line_ref, place_ref, probs_ref, act_ref, slope_ref, du_ref = refs[:11]
+    sums = refs[11:18]
     gqkv_ref, gproj_ref, gup_ref, gdown_ref, gdec_ref, gnorm_ref, gscale_ref = sums
-    kept = {name: ref for (name, _, _), ref in zip(MIDDLE_KEEP, refs[16:])}
+    kept = {name: ref for (name, _, _), ref in zip(MIDDLE_KEEP, refs[18:])}
     step = pl.program_id(0)
     group = group_of(count // columns)
     edges = Edges(bands, columns, dtop_ref, dbot_ref, from_low_ref, from_high_ref, sems)
@@ -497,12 +505,13 @@
         wup[...] = up_ref[0].astype(BF)
         wdown[...] = down_ref[0].astype(BF)
         wdec[...] = decode_ref[...].astype(BF)
+        line_ref[...], place_ref[...] = cell_selectors()
         for ref in sums:
             ref[...] = jnp.zeros_like(ref)
 
     masks = head_masks()
     masks32 = [m.astype(F32) for m in masks]
-    bias = (flag_ref[0], flag_ref[1])
+    bias = (jnp.where(edges.has_low, 0.0, -1e30), jnp.where(edges.has_high, 0.0, -1e30))
     inverse = jnp.exp(-scale_ref[...])
 
     def one(col):
@@ -546,7 +555,7 @@
         normed_last = (xhat * norm_ref[4, 0:1] + norm_ref[4, 1:2]).astype(BF)
         yield 1
         predicted = dot(normed_last, wdec[...])
-        cells = dot_tn(mask_ref[col], jnp.ones((8, CIN), BF))
+        cells = dot((dot(line_ref[...], mask_ref[col]) * place_ref[...]).astype(BF), jnp.ones((12, CIN), BF))
         yield 1
         error = predicted - edge_first(target_ref[col])
         cells = edge_first(cells)
@@ -624,7 +633,7 @@
         keep("nkv", n_kv[256:])
         keep("dkv", dkv[256:])
 
-    drive([one(col) for col in range(columns)], OFFSET)
+    drive([one(col) for col in range(columns)])
 
     @pl.when(step == 0)
     def _():
@@ -655,6 +664,195 @@
         edges.finish(count // columns, zero_ref)
 
 
+def exchanges(sizes):
+    out = []
+    for axis in ("batch", "lat"):
+        size = sizes[axis]
+        if size % 2 == 0:
+            out.append((axis, 1, 2))
+            if size > 2:
+                out.append((axis, 2, size // 2))
+        elif size > 1:
+            out.append((axis, 1, size))
+    return out
+
+
+ORDERS = ((1, 2, 3), (2, 1, 3), (3, 1, 2))
+SHARES = (2, 2, 1)
+
+
+def streams_of(sizes, rows):
+    base = exchanges(sizes)
+    unit = 8 * sizes["lat"] * sizes["batch"]
+    orders = [base]
+    if len(base) == 4:
+        orders = [[base[0], base[i], base[j], base[k]] for i, j, k in ORDERS]
+    units = rows // unit
+    at = 0
+    out = []
+    for n, order in enumerate(orders):
+        share = units - at if n == len(orders) - 1 else min(units - at, -(-units * SHARES[n] // sum(SHARES)))
+        if share:
+            out.append((at * unit, share * unit, order))
+        at += share
+    return out
+
+
+def stream_buffers(streams):
+    scratch = []
+    for _, length, order in streams:
+        held, landed = [], []
+        for _, _, count in order:
+            length //= count
+            held.append(full(length, 128))
+            landed.append(full(count - 1, length, 128))
+        scratch += held + landed + held[:-1]
+    return scratch
+
+
+def stream_sems(streams):
+    out = []
+    for _, _, order in streams:
+        out += [pltpu.SemaphoreType.DMA((count,)) for _ in range(4) for _, _, count in order] + [pltpu.SemaphoreType.DMA]
+    return out
+
+
+def span(place, rows):
+    return pl.ds(pl.multiple_of(place * rows, 8), rows)
+
+
+class Peers:
+    def __init__(self, streams):
+        self.places, self.others = {}, {}
+        for _, _, order in streams:
+            for stage in order:
+                if stage in self.places:
+                    continue
+                axis, stride, count = stage
+                index = lax.axis_index(axis)
+                place = lax.rem(index // stride, count)
+                self.places[stage] = place
+                self.others[stage] = []
+                for hop in range(1, count):
+                    other = lax.rem(place + hop, count)
+                    self.others[stage].append((other, {axis: index + (other - place) * stride}))
+
+    def greet(self):
+        barrier = pltpu.get_barrier_semaphore()
+        for others in self.others.values():
+            for _, device in others:
+                pl.semaphore_signal(barrier, inc=1, device_id=device, device_id_type=pl.DeviceIdType.MESH)
+
+    def met(self):
+        number = sum(len(others) for others in self.others.values())
+        if number:
+            pl.semaphore_wait(pltpu.get_barrier_semaphore(), number)
+
+    def stream(self, which, source_ref, target_ref, buffers, sems):
+        start, length, order = which
+        levels = len(order)
+
+        def take(scratch, count):
+            head = scratch[:count]
+            del scratch[:count]
+            return head
+
+        held, landed, gathered = (take(buffers, count) for count in (levels, levels, max(levels - 1, 0)))
+        send, recv, send_back, recv_back = (take(sems, levels) for _ in range(4))
+        (own_sem,) = take(sems, 1)
+        sources = [source_ref.at[pl.ds(start, length)]] + held
+        targets = [target_ref.at[pl.ds(start, length)]] + gathered + held[-1:]
+
+        def remote(source, target, send_sem, recv_sem, device):
+            return pltpu.make_async_remote_copy(
+                src_ref=source,
+                dst_ref=target,
+                send_sem=send_sem,
+                recv_sem=recv_sem,
+                device_id=device,
+                device_id_type=pl.DeviceIdType.MESH,
+            )
+
+        def out(s, outgoing):
+            rows, place = held[s].shape[0], self.places[order[s]]
+            return [
+                remote(
+                    sources[s].at[span(other, rows)],
+                    landed[s].at[order[s][2] - 2 - hop if outgoing else hop],
+                    send[s].at[other],
+                    recv[s].at[place if outgoing else other],
+                    device,
+                )
+                for hop, (other, device) in enumerate(self.others[order[s]])
+            ]
+
+        def back(s, outgoing):
+            rows, place = held[s].shape[0], self.places[order[s]]
+            return [
+                remote(
+                    targets[s + 1],
+                    targets[s].at[span(place if outgoing else other, rows)],
+                    send_back[s].at[other],
+                    recv_back[s].at[place if outgoing else other],
+                    device,
+                )
+                for other, device in self.others[order[s]]
+            ]
+
+        def start_out(s):
+            for copy in out(s, True):
+                copy.start()
+
+        def end_out(s):
+            for copy in out(s, False):
+                copy.wait()
+            rows = held[s].shape[0]
+            total = sources[s][span(self.places[order[s]], rows), :]
+            for hop in range(order[s][2] - 1):
+                total = total + landed[s][hop]
+            held[s][...] = total
+
+        def start_back(s):
+            for copy in back(s, True):
+                copy.start()
+            place = span(self.places[order[s]], held[s].shape[0])
+            if s:
+                targets[s][place, :] = targets[s + 1][...]
+            else:
+                pltpu.make_async_copy(targets[1], targets[0].at[place], own_sem).start()
+
+        def end_back(s):
+            for copy in back(s, False):
+                copy.wait()
+            if not s:
+                place = span(self.places[order[0]], held[0].shape[0])
+                pltpu.make_async_copy(targets[1], targets[0].at[place], own_sem).wait()
+
+        if not levels:
+
+            def alone():
+                copy = pltpu.make_async_copy(source_ref, target_ref, own_sem)
+                copy.start()
+                copy.wait()
+
+            return [alone]
+        moves = [(start_out, end_out, s) for s in range(levels)]
+        moves += [(start_back, end_back, s) for s in reversed(range(levels))]
+
+        def tick(at):
+            def run():
+                if at:
+                    _, end, s = moves[at - 1]
+                    end(s)
+                if at < len(moves):
+                    begin, _, s = moves[at]
+                    begin(s)
+
+            return run
+
+        return [tick(at) for at in range(len(moves) + 1)]
+
+
 ZERO_KEEP = (
     ("act", TAIL, FF),
     ("du", TAIL, FF),
@@ -669,26 +867,42 @@
 )
 
 
-def backward_zero(columns, count, *refs):
-    an_ref, hot_ref, x0_ref, pack_ref, probs_ref, mix_ref, x1_ref, act_ref, slope_ref = refs[:9]
+def backward_zero(columns, count, streams, *refs):
+    step_ref, an_ref, x0_ref, pack_ref, probs_ref, mix_ref, x1_ref, act_ref, slope_ref = refs[:9]
     grad_in_ref, dhe_ref, dne_ref, xe_ref, part_ref, from_low_ref, from_high_ref = refs[9:16]
-    qkv_ref, proj_ref, up_ref, down_ref, norm_ref = refs[16:21]
-    flat_ref, wqkv, wproj, wup, wdown, du_ref = refs[21:27]
-    sums = refs[27:34]
+    qkv_ref, proj_ref, up_ref, down_ref, norm_ref, mid_ref, mid_out_ref, zero_out_ref = refs[16:24]
+    flat_ref, wqkv, wproj, wup, wdown, du_ref = refs[24:30]
+    sums = refs[30:37]
     gembed_ref, glead_ref, gqkv_ref, gproj_ref, gup_ref, gdown_ref, gnorm_ref = sums
-    kept = {name: ref for (name, _, _), ref in zip(ZERO_KEEP, refs[34:])}
+    kept = {name: ref for (name, _, _), ref in zip(ZERO_KEEP, refs[37:])}
     step = pl.program_id(0)
-    group = group_of(count // columns)
+    steps = count // columns
+    group = group_of(steps)
+    comm = list(refs[37 + len(ZERO_KEEP) :])
+    kinds = (stream_buffers(streams), stream_sems(streams))
+    early_comm, late_comm = [], []
+    for kind in kinds:
+        for group_comm in (early_comm, late_comm):
+            group_comm.append(comm[: len(kind)])
+            del comm[: len(kind)]
+    peers = Peers(streams)
+    early = [peers.stream(each, mid_ref, mid_out_ref, *early_comm) for each in streams]
+    late = [peers.stream(each, flat_ref, zero_out_ref, *late_comm) for each in streams]
+    ticks = max(len(each) for each in early)
+    between = min(steps - 1, ticks - 1)
 
     @pl.when(step == 0)
     def _():
+        peers.greet()
         wqkv[...] = qkv_ref[0].astype(BF)
         wproj[...] = proj_ref[0].astype(BF)
         wup[...] = up_ref[0].astype(BF)
         wdown[...] = down_ref[0].astype(BF)
         for ref in sums:
             ref[...] = jnp.zeros_like(ref)
-
+        peers.met()
+
+    hot = lead_hot(step_ref, step, steps)
     masks = head_masks()
     masks32 = [m.astype(F32) for m in masks]
 
@@ -751,14 +965,23 @@
         yield 1
         add_norm_grads(gnorm_ref, 0, dn, xhat)
         grad = grad + norm_back(dn, xhat, x0_ref[col, :, C : C + 1], norm_ref[0, 0:1])
-        glead_ref[...] += hot_ref[0] * jnp.sum(grad, axis=0, keepdims=True)
+        glead_ref[...] += hot * jnp.sum(grad, axis=0, keepdims=True)
         grad_low = grad.astype(BF)
         yield 1
         gembed_ref[...] += dot_tn(grad_low[0:256], an_ref[col, 0:256])
         keep("an", an_ref[col, 256:COL])
         keep("dh", grad_low[256:])
 
-    drive([one(col) for col in range(columns)], OFFSET)
+    parts = [one(col) for col in range(columns)]
+    drive(parts)
+
+    for at in range(between):
+
+        def now(at=at):
+            for each in early:
+                each[at]()
+
+        pl.when(step == at)(now)
 
     @pl.when(lax.rem(step, group) == group - 1)
     def _():
@@ -778,166 +1001,12 @@
         store_narrow(flat_ref, 19 * C, gnorm_ref, 8)
         store_narrow(flat_ref, 19 * C + 16, glead_ref, 24)
         clear_from(flat_ref, FLAT_ZERO)
-
-
-def exchanges(sizes):
-    out = []
-    for axis in ("batch", "lat"):
-        size = sizes[axis]
-        if size % 2 == 0:
-            out.append((axis, 1, 2))
-            if size > 2:
-                out.append((axis, 2, size // 2))
-        elif size > 1:
-            out.append((axis, 1, size))
-    return out
-
-
-def streams_of(sizes, arrays, rows):
-    base = exchanges(sizes)
-    unit = 8 * sizes["lat"] * sizes["batch"]
-    orders = [base]
-    if len(base) == 4:
-        orders = [[base[0], base[i], base[j], base[k]] for i, j, k in ORDERS]
-    out = []
-    for array in range(arrays):
-        units = rows // unit
-        at = 0
-        for n, order in enumerate(orders):
-            left = len(orders) - n
-            share = units - at if left == 1 else min(units - at, -(-units * SHARES[n] // sum(SHARES)))
-            if share:
-                out.append((array, at * unit, share * unit, order))
-            at += share
-    return out
-
-
-ORDERS = ((1, 2, 3), (2, 1, 3), (3, 1, 2))
-SHARES = (2, 2, 1)
-
-
-def all_sum(streams, arrays, *refs):
-    sources, outs, scratch = refs[:arrays], refs[arrays : 2 * arrays], list(refs[2 * arrays :])
-
-    def take(count):
-        head = scratch[:count]
-        del scratch[:count]
-        return head
-
-    met = []
-    for _, _, _, order in streams:
-        for stage in order:
-            if stage not in met:
-                met.append(stage)
-    places, peers = {}, {}
-    for axis, stride, count in met:
-        index = lax.axis_index(axis)
-        place = lax.rem(index // stride, count)
-        others = []
-        for hop in range(1, count):
-            other = lax.rem(place + hop, count)
-            others.append((other, {axis: index + (other - place) * stride}))
-        places[axis, stride, count] = place
-        peers[axis, stride, count] = others
-
-    barrier = pltpu.get_barrier_semaphore()
-    for others in peers.values():
-        for _, device in others:
-            pl.semaphore_signal(barrier, inc=1, device_id=device, device_id_type=pl.DeviceIdType.MESH)
-    pl.semaphore_wait(barrier, sum(len(others) for others in peers.values()))
-
-    def span(place, rows):
-        return pl.ds(pl.multiple_of(place * rows, 8), rows)
-
-    def stream(array, start, length, order):
-        levels = len(order)
-        held, landed, gathered = take(levels), take(levels), take(levels - 1)
-        send, recv, send_back, recv_back = take(levels), take(levels), take(levels), take(levels)
-        whole_in = sources[array].at[pl.ds(start, length)]
-        whole_out = outs[array].at[pl.ds(start, length)]
-
-        def out_copies(s, outgoing):
-            rows = held[s].shape[0]
-            source = whole_in if s == 0 else held[s - 1]
-            place = places[order[s]]
-            return [
-                pltpu.make_async_remote_copy(
-                    src_ref=source.at[span(other, rows)],
-                    dst_ref=landed[s].at[place if outgoing else other],
-                    send_sem=send[s].at[other],
-                    recv_sem=recv[s].at[place if outgoing else other],
-                    device_id=device,
-                    device_id_type=pl.DeviceIdType.MESH,
-                )
-                for other, device in peers[order[s]]
-            ]
-
-        def back_copies(s, outgoing):
-            rows = held[s].shape[0]
-            own = held[s] if s == levels - 1 else gathered[s]
-            target = whole_out if s == 0 else gathered[s - 1]
-            place = places[order[s]]
-            return [
-                pltpu.make_async_remote_copy(
-                    src_ref=own,
-                    dst_ref=target.at[span(place if outgoing else other, rows)],
-                    send_sem=send_back[s].at[other],
-                    recv_sem=recv_back[s].at[place if outgoing else other],
-                    device_id=device,
-                    device_id_type=pl.DeviceIdType.MESH,
-                )
-                for other, device in peers[order[s]]
-            ]
-
-        for s in range(levels):
-            rows = held[s].shape[0]
-            source = whole_in if s == 0 else held[s - 1]
-            for copy in out_copies(s, True):
-                copy.start()
-            yield 1
-            for copy in out_copies(s, False):
-                copy.wait()
-            total = source[span(places[order[s]], rows), :]
-            for other, _ in peers[order[s]]:
-                total = total + landed[s][other]
-            held[s][...] = total
-        for s in reversed(range(levels)):
-            rows = held[s].shape[0]
-            own = held[s] if s == levels - 1 else gathered[s]
-            target = whole_out if s == 0 else gathered[s - 1]
-            for copy in back_copies(s, True):
-                copy.start()
-            target[span(places[order[s]], rows), :] = own[...]
-            yield 1
-            for copy in back_copies(s, False):
-                copy.wait()
-
-    drive([stream(*each) for each in streams], 0)
-
-
-def run_all_sum(flats, sizes):
-    rows = flats[0].shape[0]
-    streams = streams_of(sizes, len(flats), rows)
-    scratch = []
-    for _, _, length, order in streams:
-        held, landed, sems = [], [], []
-        for _, _, count in order:
-            length //= count
-            held.append(pltpu.VMEM((length, 128), F32))
-            landed.append(pltpu.VMEM((count, length, 128), F32))
-            sems.append(pltpu.SemaphoreType.DMA((count,)))
-        scratch += held + landed + held[:-1] + sems * 4
-    return pl.pallas_call(
-        partial(all_sum, streams, len(flats)),
-        out_shape=[struct(flat.shape, F32) for flat in flats],
-        in_specs=[pl.BlockSpec(memory_space=pltpu.VMEM)] * len(flats),
-        out_specs=[pl.BlockSpec(memory_space=pltpu.VMEM)] * len(flats),
-        scratch_shapes=scratch,
-        compiler_params=pltpu.CompilerParams(
-            collective_id=0, has_side_effects=True, vmem_limit_bytes=VMEM_BYTES
-        ),
-        name="all_sum",
-    )(*flats)
+        for at in range(max(ticks, ticks - between)):
+            for each in late:
+                each[at]()
+            if between + at < ticks:
+                for each in early:
+                    each[between + at]()
 
 
 def update(steps, mid_ref, zero_ref, *refs):
@@ -1059,14 +1128,14 @@
     return out[0:9], out[9:18], out[18:27], out[27]
 
 
-def whole(shape):
+def whole(shape, once=False):
     zeros = (0,) * len(shape)
-    return pl.BlockSpec(shape, lambda i: zeros)
+    return pl.BlockSpec(shape, lambda i: zeros, pipeline_mode=pl.Buffered(1) if once else None)
 
 
 def layer(shape, index):
     at = (index,) + (0,) * len(shape)
-    return pl.BlockSpec((1,) + shape, lambda i: at)
+    return pl.BlockSpec((1,) + shape, lambda i: at, pipeline_mode=pl.Buffered(1))
 
 
 def rows_of(columns, offset, *shape):
@@ -1102,7 +1171,7 @@
     return [low(held * rows, width) for _, rows, width in kept]
 
 
-def run_forward(tokens, hot, lead_table, embed_t, qkv_w, proj_w, up_w, down_t, norm_t, bands, per_sample, columns):
+def run_forward(lead_step, tokens, lead_table, embed_t, qkv_w, proj_w, up_w, down_t, norm_t, bands, columns):
     count = tokens.shape[0]
     steps = count // columns
     outs = [
@@ -1119,8 +1188,8 @@
         partial(forward_zero, columns, count, bands),
         grid=(steps,),
         in_specs=[
+            SMEM,
             rows(columns, COL, CIN),
-            hot_spec(per_sample // columns),
             whole((LEADS, C)),
             whole((C, CIN)),
             layer((C, 3 * C), 0),
@@ -1134,10 +1203,10 @@
         scratch_shapes=[low(C, CIN), low(C, 3 * C), low(C, C), low(C, FF), low(C, FF)] + edge_scratch(count, columns),
         compiler_params=pltpu.CompilerParams(vmem_limit_bytes=VMEM_BYTES, collective_id=1, has_side_effects=True),
         name="forward_zero",
-    )(tokens, hot, lead_table, embed_t, qkv_w, proj_w, up_w, down_t, norm_t)
-
-
-def run_middle(flags, h1, up_in, down_in, target, cells, qkv_w, proj_w, up_w, down_t, decode_w, norm_t, scale, flat_rows, bands, columns):
+    )(lead_step, tokens, lead_table, embed_t, qkv_w, proj_w, up_w, down_t, norm_t)
+
+
+def run_middle(h1, up_in, down_in, target, mask, qkv_w, proj_w, up_w, down_t, decode_w, norm_t, scale, flat_rows, bands, columns):
     count = h1.shape[0]
     steps = count // columns
     outs = [
@@ -1150,12 +1219,11 @@
         partial(middle, columns, count, bands),
         grid=(steps,),
         in_specs=[
-            SMEM,
             rows(columns, COL, C),
             rows(columns, HALF, C),
             rows(columns, HALF, C),
             rows(columns, COL, CIN),
-            rows(columns, 8, COL),
+            rows(columns, 24, 12),
             layer((C, 3 * C), 1),
             layer((C, C), 1),
             layer((C, FF), 1),
@@ -1176,6 +1244,8 @@
             low(C, FF),
             low(C, FF),
             low(C, CIN),
+            low(COL, 24),
+            full(COL, 12),
             full(columns, 2, WIN, LANES),
             low(columns, COL, FF),
             full(columns, COL, FF),
@@ -1191,18 +1261,19 @@
         + kept_scratch(MIDDLE_KEEP, count, columns),
         compiler_params=pltpu.CompilerParams(vmem_limit_bytes=VMEM_BYTES, collective_id=2, has_side_effects=True),
         name="middle",
-    )(flags, h1, up_in, down_in, target, cells, qkv_w, proj_w, up_w, down_t, decode_w, norm_t, scale)
-
-
-def run_backward(tokens, hot, saved, mid_out, qkv_w, proj_w, up_w, down_t, norm_t, flat_rows, per_sample, columns):
+    )(h1, up_in, down_in, target, mask, qkv_w, proj_w, up_w, down_t, decode_w, norm_t, scale)
+
+
+def run_backward(lead_step, tokens, saved, mid_out, mid, qkv_w, proj_w, up_w, down_t, norm_t, sizes, columns):
     count = tokens.shape[0]
     steps = count // columns
+    streams = streams_of(sizes, mid.shape[0])
     return pl.pallas_call(
-        partial(backward_zero, columns, count),
+        partial(backward_zero, columns, count, streams),
         grid=(steps,),
         in_specs=[
+            SMEM,
             rows(columns, COL, CIN),
-            hot_spec(per_sample // columns),
             rows(columns, COL, XW),
             rows(columns, COL, 3 * C),
             rows(columns, 2, WIN, LANES),
@@ -1222,10 +1293,12 @@
             layer((C, FF), 0),
             layer((C, FF), 0),
             whole((5, 2, C)),
+            whole(mid.shape, True),
         ],
-        out_specs=whole((flat_rows, 128)),
-        out_shape=struct((flat_rows, 128), F32),
+        out_specs=[ANYWHERE] * 2,
+        out_shape=[struct(mid.shape, F32)] * 2,
         scratch_shapes=[
+            full(*mid.shape),
             low(C, 3 * C),
             low(C, C),
             low(C, FF),
@@ -1239,14 +1312,12 @@
             full(C, FF),
             full(8, C),
         ]
-        + kept_scratch(ZERO_KEEP, count, columns),
-        compiler_params=pltpu.CompilerParams(vmem_limit_bytes=VMEM_BYTES),
+        + kept_scratch(ZERO_KEEP, count, columns)
+        + stream_buffers(streams) * 2
+        + stream_sems(streams) * 2,
+        compiler_params=pltpu.CompilerParams(vmem_limit_bytes=VMEM_BYTES, collective_id=3, has_side_effects=True),
         name="backward_zero",
-    )(tokens, hot, *saved, *mid_out, qkv_w, proj_w, up_w, down_t, norm_t)
-
-
-def hot_spec(steps):
-    return pl.BlockSpec((1, 24, 1), lambda i: (i // steps, 0, 0))
+    )(lead_step, tokens, *saved, *mid_out, qkv_w, proj_w, up_w, down_t, norm_t, mid)
 
 
 def views(group):
@@ -1266,28 +1337,22 @@
     sizes = {axis: lax.axis_size(axis) for axis in ("lat", "batch")}
     tokens = analysis.transpose(0, 1, 2, 4, 3, 5).reshape(samples * blocks, COL, CIN)
     truth = target.transpose(0, 1, 2, 4, 3, 5).reshape(samples * blocks, COL, CIN)
-    cells = loss_mask.transpose(0, 1, 2, 4, 3).reshape(samples * blocks, 1, COL).astype(BF)
-    cells = jnp.pad(cells, ((0, 0), (0, 7), (0, 0)))
-    at = lax.axis_index("lat")
-    flags = jnp.stack([jnp.where(at > 0, 0.0, -1e30), jnp.where(at < sizes["lat"] - 1, 0.0, -1e30)]).astype(F32)
+    lines = loss_mask.reshape(samples * blocks, 24, 12).astype(BF)
     columns = next(c for c in (COLUMNS, 3, 2, 1) if blocks % c == 0)
     unit = 8 * sizes["lat"] * sizes["batch"]
     flat_rows = -(-max(FLAT_MIDDLE, FLAT_ZERO) // unit) * unit
-    hot = (jnp.arange(24, dtype=jnp.int32)[None, :, None] == lead_step[:, None, None] - 1).astype(F32)
 
     *saved, h1, from_low, from_high = run_forward(
-        tokens, hot, lead_table, embed_t, qkv_w, proj_w, up_w, down_t, norm_t, sizes["lat"], blocks, columns
+        lead_step, tokens, lead_table, embed_t, qkv_w, proj_w, up_w, down_t, norm_t, sizes["lat"], columns
     )
     *edge_out, part, mid, back_low, back_high = run_middle(
-        flags, h1, from_low, from_high, truth, cells, qkv_w, proj_w, up_w, down_t, decode_w, norm_t, scale,
+        h1, from_low, from_high, truth, lines, qkv_w, proj_w, up_w, down_t, decode_w, norm_t, scale,
         flat_rows, sizes["lat"], columns,
     )
-    zero = run_backward(
-        tokens, hot, saved, (*edge_out, part, back_low, back_high), qkv_w, proj_w, up_w, down_t, norm_t,
-        flat_rows, blocks, columns,
+    mid, zero = run_backward(
+        lead_step, tokens, saved, (*edge_out, part, back_low, back_high), mid, qkv_w, proj_w, up_w, down_t, norm_t,
+        sizes, columns,
     )
-    if unit > 8:
-        mid, zero = run_all_sum([mid, zero], sizes)
     news, moments, squares, small = run_update(mid, zero, weights, firsts, seconds)
     return (*unviews(news), *unviews(moments), *unviews(squares), small[0, 0], small[1, 0], small[2, 0])
 

time: 285 us -> 270 us (0.947)
  Pallas kernels: 278 us -> 266 us
    pallas_call x2 -> x1, Pallas kernels: 114 us -> 98.5 us  [run_backward(): pl.pallas_call(partial(backward_zero, columns, count, streams), grid=(ste...]
    pallas_call x1, Pallas kernels: 96.9 us -> 100 us  [run_middle(): pl.pallas_call(partial(middle, columns, count, bands), grid=(steps,), in_...]
where the time goes in v4:
time: 270 us; the launch traced here: 269 us
  Pallas kernels  266 us (99%)
    pallas_call x1, Pallas kernels, run_middle(): pl.pallas_call(partial(middle, columns, count, bands), grid=(steps,), in_...  100 us
    pallas_call x1, Pallas kernels, run_backward(): pl.pallas_call(partial(backward_zero, columns, count, streams), grid=(ste...  98.5 us
    pallas_call x1, Pallas kernels, run_forward(): pl.pallas_call(partial(forward_zero, columns, count, bands), grid=(steps,...  53.4 us
    pallas_call x1, Pallas kernels, run_update(): pl.pallas_call(partial(update, steps), grid=(steps,), in_specs=[whole(mid...  13.5 us

profile of v4, /device:TPU:0, one launch (start us, length us, event | category | flops | bytes accessed | tf_op | source)
XLA Modules:
  0.0 269.3 jit_solution(9014652473539819896)
XLA Ops:
  0.7 1.7 convert_element_type.5
  2.4 53.4 %forward_zero.1 = (f32[24,288,256]{2,1,0:T(8,128)}, bf16[24,288,576]{2,1,0:T(8,128)(2,1)}, f32[24,2,144,896]{3,2,1,0:T(8,128)}, bf16[24,288,192]{2,1,0:T(8,128)(...) custom-call(s32[2]{0:T(128)} %refs_0_.3, ...), custom_call_target="tpu_custom_call" | custom-call | tf_op jit(solution)/shard_map/forward_zero/pallas_call | solution.py:1187
  55.8 100.1 %middle.1 = (f32[24,144,192]{2,1,0:T(8,128)}, f32[24,144,192]{2,1,0:T(8,128)}, f32[24,144,192]{2,1,0:T(8,128)}, f32[24,144,256]{2,1,0:T(8,128)}, f32[8,192]{1,0:...) custom-call(f32[24,288,192]{2,1,0:T(8,128)} %get-tuple-element.85.refs_0_, ...), custom_call_target="tpu_custom_call" | custom-call | tf_op jit(solution)/shard_map/middle/pallas_call | solution.py:1218
  155.9 98.5 %backward_zero.1 = (f32[3840,128]{1,0:T(8,128)}, f32[3840,128]{1,0:T(8,128)}) custom-call(s32[2]{0:T(128)} %refs_0_.3, bf16[24,288,128]{2,1,0:T(8,128)(2,1)} %bitcast.39, f32[24,288,256]{2,1,0:T(8,128)} %get-tuple-element.78.refs_2_, bf16[24,288,576]{2,1,0:T(8,128)(2,1)} %get-tuple-element.79.refs_3_, f32[24,2,144,896]{3,2,1,0:T(8,128)} %get-tuple-element.80.refs_4_, ...), custom_call_target="tpu_custom_call" | custom-call | tf_op jit(solution)/shard_map/backward_zero/pallas_call | solution.py:1271
  254.4 13.5 %update.1 = (f32[192,128]{1,0:T(8,128)}, f32[20,192]{1,0:T(8,128)}, f32[2,192,576]{2,1,0:T(8,128)}, f32[2,192,192]{2,1,0:T(8,128)}, f32[2,192,768]{2,1,0:T(8,128...) custom-call(f32[3840,128]{1,0:T(8,128)} %get-tuple-element.96.mid_re, ...), custom_call_target="tpu_custom_call" | custom-call | tf_op jit(solution)/shard_map/update/pallas_call | solution.py:1118
  268.0 1.3 fusion
